TPU v7x, 32 devices: a whole 2x2x4 slice. The times are simulated.
32 devices in a mesh: grp: 2 (over x), tp: 8 (over z, y), section: 2 (over core).
Axes of the slice: x: 2, y: 2, z: 4, core: 2. Of those that a mesh axis runs over, the one named last changes fastest.
Arguments:
- hidden_in: bfloat16 [128, 4096], P(('grp', 'section')), parts along dimension 0, may hold values from -6 to 6
- temporal_gain: float32 [4096], replicated, may hold values from 0.5 to 1.5
- temporal_qkv: bfloat16 [3, 4096, 4096], P(None, None, 'tp'), may hold values from -0.09375 to 0.09375
- temporal_out_weight: bfloat16 [4096, 4096], P('tp'), may hold values from -0.125 to 0.125
- cache_keys: bfloat16 [128, 64, 4096], P(('grp', 'section'), None, 'tp'), parts along dimension 0, may hold values from -240 to 240
- cache_values: bfloat16 [128, 64, 4096], P(('grp', 'section'), None, 'tp'), parts along dimension 0, may hold values from -6 to 6
- lengths: int32 [128], P(('grp', 'section')), parts along dimension 0, may hold values from 1 to 64, as said below
- depth_in: bfloat16 [8, 4096, 1024], P('section', 'tp'), may hold values from -0.09375 to 0.09375
- depth_embed: bfloat16 [8, 2048, 1024], P('section', 'tp'), may hold values from -6 to 6
- depth_gain: float32 [1024], replicated, may hold values from 0.5 to 1.5
- depth_qkv: bfloat16 [8, 3, 1024, 1024], P('section', None, None, 'tp'), may hold values from -0.1875 to 0.1875
- depth_out_weight: bfloat16 [8, 1024, 1024], P('section', 'tp'), may hold values from -0.1875 to 0.1875
- head_gain: float32 [1024], replicated, may hold values from 0.5 to 1.5
- head_weight: bfloat16 [8, 1024, 2048], P('section', 'tp'), may hold values from -0.25 to 0.25
- tokens: int32 [128, 8], P('grp', 'section'), parts along dimension 0, may hold values from 0 to 2047
Outputs:
- temporal_out: bfloat16 [128, 4096], P(('grp', 'section'), 'tp'), parts along dimension 0
- logits: float32 [128, 8, 2048], P('grp', 'section', 'tp'), parts along dimension 0
There are 2 independent parts, one for each index of `grp`. A program takes and returns all parts, laid end to end along the dimension named above; an argument that names none is the same for every part. Nothing has to cross between parts.
Inputs may be any that keep to these rules, and one draw needn't show every extreme that they name: Cached positions 0 to lengths - 1 of a stream are live and the new token stands at position lengths; some stream of every group holds 64 live positions.
All inputs are finite; a program needn't handle non-finite values.
Results may differ from a plain program's by a relative error of at most 0.009.
Values may be sent and summed in bfloat16 or wider, within the bound.
No kernel may reach another device: no remote copies, remote signals or barrier semaphores. Data moves between devices by JAX's collectives and lax.ppermute only.
A program may use at most 64 MiB of HBM per device.

v0:
```python
import math

import jax
import jax.numpy as jnp
from jax import lax
from jax.sharding import PartitionSpec as P

HEAD_DIM = 128
DEPTH_HDIM = 64


EPSILON = 1e-05


def passed_along(block, axis, distance):
    devices = range(lax.axis_size(axis))
    route = [(i - distance, i) for i in devices if i - distance in devices]
    return lax.ppermute(block, axis, route)


def from_partner(shard, axis, distance):
    return lax.ppermute(shard, axis, [(i, i ^ 1 << distance) for i in range(lax.axis_size(axis))])


def rms_norm(values, scale):
    wide = values.astype(jnp.float32)
    return wide * lax.rsqrt(jnp.mean(wide * wide, axis=-1, keepdims=True) + EPSILON) * scale


def rotate(vectors, positions):
    halfdim = vectors.shape[-1] // 2
    spacing = jnp.arange(halfdim, dtype=jnp.float32) / halfdim
    inverse = jnp.exp(-math.log(10000.0) * spacing)
    angles = positions.astype(jnp.float32)[:, None, None] * inverse[None, None, :]
    cosine = jnp.cos(angles)
    sine = jnp.sin(angles)
    first = vectors[..., :halfdim]
    second = vectors[..., halfdim:]
    return jnp.concatenate(
        [first * cosine - second * sine, first * sine + second * cosine], axis=-1
    )


def per_device(
    hidden_in,
    temporal_gain,
    temporal_qkv,
    temporal_out_weight,
    cache_keys,
    cache_values,
    lengths,
    depth_in,
    depth_embed,
    depth_gain,
    depth_qkv,
    depth_out_weight,
    head_gain,
    head_weight,
    tokens,
):
    local_streams = hidden_in.shape[0]
    local_cols = temporal_qkv.shape[2]
    local_heads = local_cols // HEAD_DIM
    cache_len = cache_keys.shape[1]
    normed = rms_norm(hidden_in, temporal_gain).astype(jnp.bfloat16)
    projected = jnp.einsum("sd,tdf->tsf", normed, temporal_qkv, preferred_element_type=jnp.float32)
    layout = (local_streams, local_heads, HEAD_DIM)
    queries = rotate(projected[0].reshape(layout), lengths).astype(jnp.bfloat16)
    keys_new = rotate(projected[1].reshape(layout), lengths).astype(jnp.bfloat16)
    values_new = projected[2].reshape(layout).astype(jnp.bfloat16)
    cached_keys = cache_keys.reshape(local_streams, cache_len, local_heads, HEAD_DIM)
    cached_values = cache_values.reshape(local_streams, cache_len, local_heads, HEAD_DIM)
    factor = 1.0 / math.sqrt(HEAD_DIM)
    scores = (
        jnp.einsum("shd,sphd->shp", queries, cached_keys, preferred_element_type=jnp.float32)
        * factor
    )
    own_score = (
        jnp.sum(queries.astype(jnp.float32) * keys_new.astype(jnp.float32), axis=-1) * factor
    )
    valid = jnp.arange(cache_len, dtype=jnp.int32)[None, None, :] < lengths[:, None, None]
    scores = jnp.where(valid, scores, -jnp.inf)
    highest = jnp.maximum(jnp.max(scores, axis=-1), own_score)
    expo = jnp.exp(scores - highest[..., None])
    own_expo = jnp.exp(own_score - highest)
    totals = jnp.sum(expo, axis=-1) + own_expo
    weights = (expo / totals[..., None]).astype(jnp.bfloat16)
    own_weight = (own_expo / totals).astype(jnp.bfloat16)
    mixed = jnp.einsum("shp,sphd->shd", weights, cached_values, preferred_element_type=jnp.float32)
    mixed = mixed + own_weight.astype(jnp.float32)[..., None] * values_new.astype(jnp.float32)
    mixed = mixed.astype(jnp.bfloat16).reshape(local_streams, local_cols)
    partial_rows = jnp.dot(mixed, temporal_out_weight, preferred_element_type=jnp.float32)
    summed = lax.psum_scatter(partial_rows, "tp", scatter_dimension=1, tiled=True)
    slice_width = summed.shape[1]
    tp_place = lax.axis_index("tp")
    resid_in = lax.dynamic_slice_in_dim(hidden_in, tp_place * slice_width, slice_width, 1)
    temporal = (resid_in.astype(jnp.float32) + summed).astype(jnp.bfloat16)
    all_rows = lax.all_gather(temporal, "section", axis=0, tiled=True)
    streams = all_rows.shape[0]
    codes = depth_in.shape[0]
    entry_part = jnp.einsum("sd,cde->sce", all_rows, depth_in, preferred_element_type=jnp.float32)
    vocab_local = depth_embed.shape[1]
    first_id = tp_place * vocab_local
    onehot = (
        tokens[:, :, None] == first_id + jnp.arange(vocab_local, dtype=jnp.int32)[None, None, :]
    ).astype(jnp.bfloat16)
    embedded = jnp.einsum("scv,cve->sce", onehot, depth_embed, preferred_element_type=jnp.float32)
    entry_terms = entry_part + embedded
    hidden_rows = head_weight.shape[1]
    hidden_start = tp_place * hidden_rows
    entry = lax.psum(entry_terms, "tp")
    depth_normed = rms_norm(entry, depth_gain).astype(jnp.bfloat16)
    dproj = jnp.einsum(
        "sce,ctef->tscf", depth_normed, depth_qkv, preferred_element_type=jnp.float32
    ).astype(jnp.bfloat16)
    prior_keys, prior_values = passed_along((dproj[1], dproj[2]), "section", 1)
    depth_cols = dproj.shape[3]
    head_part = min(depth_cols, DEPTH_HDIM)
    local_parts = depth_cols // head_part
    sharers = DEPTH_HDIM // head_part
    all_keys = jnp.concatenate([prior_keys, dproj[1]], axis=1).reshape(
        streams, 2 * codes, local_parts, head_part
    )
    all_values = jnp.concatenate([prior_values, dproj[2]], axis=1).reshape(
        streams, 2 * codes, local_parts, head_part
    )
    depth_queries = dproj[0].reshape(streams, codes, local_parts, head_part)
    depth_scores = jnp.einsum(
        "sqhd,skhd->shqk", depth_queries, all_keys, preferred_element_type=jnp.float32
    )
    for level in range(sharers.bit_length() - 1):
        depth_scores = depth_scores + from_partner(depth_scores, "tp", level)
    depth_scores = depth_scores * (1.0 / math.sqrt(DEPTH_HDIM))
    section_place = lax.axis_index("section")
    query_pos = jnp.arange(codes, dtype=jnp.int32)[:, None]
    key_pos = jnp.arange(2 * codes, dtype=jnp.int32)[None, :]
    allowed = jnp.where(key_pos < codes, section_place > 0, key_pos - codes <= query_pos)
    depth_scores = jnp.where(allowed[None, None], depth_scores, -jnp.inf)
    depth_top = jnp.max(depth_scores, axis=-1, keepdims=True)
    depth_expo = jnp.exp(depth_scores - depth_top)
    depth_weights = (depth_expo / jnp.sum(depth_expo, axis=-1, keepdims=True)).astype(jnp.bfloat16)
    depth_mixed = jnp.einsum(
        "shqk,skhd->sqhd", depth_weights, all_values, preferred_element_type=jnp.float32
    ).astype(jnp.bfloat16)
    depth_mixed = depth_mixed.reshape(streams, codes, depth_cols)
    depth_terms = jnp.einsum(
        "scf,cfe->sce", depth_mixed, depth_out_weight, preferred_element_type=jnp.float32
    )
    resid = entry + lax.psum(depth_terms, "tp")
    head_normed = rms_norm(resid, head_gain).astype(jnp.bfloat16)
    own_hidden = lax.dynamic_slice_in_dim(head_normed, hidden_start, hidden_rows, 2)
    partial_logits = jnp.einsum(
        "sce,cev->scv", own_hidden, head_weight, preferred_element_type=jnp.float32
    )
    logits = lax.psum_scatter(partial_logits, "tp", scatter_dimension=2, tiled=True)
    return (temporal, logits)


def solution(mesh):
    return jax.shard_map(
        per_device,
        mesh=mesh,
        in_specs=(
            P(("grp", "section"), None),
            P(),
            P(None, None, "tp"),
            P("tp", None),
            P(("grp", "section"), None, "tp"),
            P(("grp", "section"), None, "tp"),
            P(("grp", "section")),
            P("section", "tp", None),
            P("section", "tp", None),
            P(),
            P("section", None, None, "tp"),
            P("section", "tp", None),
            P(),
            P("section", "tp", None),
            P("grp", "section"),
        ),
        out_specs=(P(("grp", "section"), "tp"), P("grp", "section", "tp")),
        check_vma=False,
    )
```

profile of v0, /device:TPU:0, one launch (start us, length us, event | category | flops | bytes accessed | tf_op | source)
XLA Modules:
  0.0 357.3 jit_solution(17455452350365381096)
XLA Ops:
  8.9 1.1 fusion.13
  10.0 7.0 %convolution_bitcast_fusion.3 = f32[3,32,512]{2,1,0:T(8,128)S(1)} fusion(bf16[3,4096,512]{2,1,0:T(8,128)(2,1)} %param.17, bf16[32,4096]{1,0:T(8,128)(2,1)} %param.15, f32[4096]{0:T(1024)} %param.16, f32[32]{0:T(128)S(1)} %add_rsqrt_fusion.2), kind=kOutput, calls=%fused_computation.17 | convolution fusion | flops 403177472 | bytes 13058176 | tf_op jit(solution)/shard_map/sd,tdf->tsf/dot_general | solution.py:66
  17.8 2.8 fusion.4
  21.1 2.2 fusion.1
  23.5 3.8 %fusion.48 = f32[32,4096]{1,0:T(8,128)} fusion(bf16[512,4096]{1,0:T(8,128)(2,1)} %param.18, bf16[4,8,4,128]{3,2,1,0:T(4,128)(2,1)S(1)} %bitcast.91), kind=kOutput, calls=%fused_computation.70 | convolution fusion | flops 134217728 | bytes 4751360 | tf_op jit(solution)/shard_map/dot_general | solution.py:92
  27.4 65.1 %reduce-scatter.3.cloned.1.call-done = f32[32,512]{1,0:T(8,128)} async-done(((f32[32,4096]{1,0:T(8,128)}), f32[32,512]{1,0:T(8,128)}) %reduce-scatter.3.cloned.1.call-update) | async-done | bytes 65552 | tf_op jit(solution)/shard_map/reduce_scatter | solution.py:93
  94.0 1.8 all_gather.3
  95.8 3.2 fusion.40
  99.0 1.6 fusion.7
  100.7 77.2 %all-reduce.3.cloned.1.call-done = f32[64,4,1024]{2,0,1:T(8,128)} async-done(((f32[64,4,1024]{2,0,1:T(8,128)}), f32[64,4,1024]{2,0,1:T(8,128)}) %all-reduce.3.cloned.1.call-update) | async-done | bytes 1048592 | tf_op jit(solution)/shard_map/psum | solution.py:111
  177.9 1.5 multiply_reduce_fusion.1
  180.9 1.9 collective-permute-start.1
  182.8 1.9 collective-permute-start
  186.6 0.9 concatenate.29
  188.4 0.9 concatenate.26
  190.2 1.5 fusion.88
  191.7 3.6 %fusion.12 = bf16[64,4,2,64]{3,1,2,0:T(4,128)(2,1)} fusion(bf16[64,4,2,64]{3,1,2,0:T(4,128)(2,1)} %copy.41, bf16[64,4,2,64]{3,1,2,0:T(4,128)(2,1)} %copy.40, f32[64,2,4]{2,1,0:T(2,128)S(1)} %fusion.88, bf16[64,4,2,64]{3,1,2,0:T(4,128)(2,1)S(1)} %copy-done.4, bf16[64,4,2,64]{3,1,2,0:T(4,128)(2,1)} %copy.42, bf16[64,4,2,64]{3,2,0,1:T(2,128)(2,1)S(1)} %reshape_squeeze.12, ...), kind=kOutput, calls=%fused_computation.19 | convolution fusion | flops 1626631 | bytes 395296 | tf_op jit(solution)/shard_map/shqk,skhd->sqhd/dot_general | solution.py:142
  195.3 1.0 copy.45
  196.5 2.5 convolution_bitcast_fusion.1
  199.8 77.1 %all-reduce.5.cloned.1.call-done = f32[64,4,1024]{2,0,1:T(8,128)} async-done(((f32[64,4,1024]{2,0,1:T(8,128)}), f32[64,4,1024]{2,0,1:T(8,128)}) %all-reduce.5.cloned.1.call-update) | async-done | bytes 1048592 | tf_op jit(solution)/shard_map/psum | solution.py:149
  276.9 1.9 multiply_reduce_fusion
  279.1 1.8 convolution_bitcast_fusion
  281.0 68.0 %reduce-scatter.5.cloned.1.call-done = f32[64,4,256]{2,0,1:T(8,128)} async-done(((f32[64,4,2048]{2,0,1:T(8,128)}), f32[64,4,256]{2,0,1:T(8,128)}) %reduce-scatter.5.cloned.1.call-update) | async-done | bytes 262160 | tf_op jit(solution)/shard_map/reduce_scatter | solution.py:155
  348.9 1.8 copy.46
  (65 shorter events, 11.0 us)
Async XLA Ops:
  7.2 172.3 %copy-start = (bf16[4,3,1024,128]{3,2,1,0:T(8,128)(2,1)S(1)}, bf16[4,3,1024,128]{3,2,1,0:T(8,128)(2,1)}, u32[]{:S(2)}) copy-start(bf16[4,3,1024,128]{3,2,1,0:T(8,128)(2,1)} %param.25) | copy-start | bytes 9437188
  7.2 85.3 %reduce-scatter.3.cloned.1.call-start = ((), (), s32[]{:S(2)}) async-start(), calls=%async_computation.2 | async-start | bytes 589824 | tf_op jit(solution)/shard_map/reduce_scatter | solution.py:93
  27.3 150.7 %all-reduce.3.cloned.1.call-start = ((), (), s32[]{:S(2)}) async-start(), calls=%async_computation.3 | async-start | bytes 2097152 | tf_op jit(solution)/shard_map/psum | solution.py:111
  93.3 0.6 copy-start.5
  95.8 3.2 copy-start.2
  95.8 3.2 copy-start.7
  100.6 78.8 %copy-start.6 = (f32[1024]{0:T(1024)S(1)}, f32[1024]{0:T(1024)}, u32[]{:S(2)}) copy-start(f32[1024]{0:T(1024)} %param.24) | copy-start | bytes 12292
  100.6 176.2 %all-reduce.5.cloned.1.call-start = ((), (), s32[]{:S(2)}) async-start(), calls=%async_computation.4 | async-start | bytes 2097152 | tf_op jit(solution)/shard_map/psum | solution.py:149
  177.9 1.5 copy-start.1
  180.9 5.8 %collective-permute-start.1 = (bf16[64,4,128]{2,0,1:T(8,128)(2,1)}, bf16[64,4,128]{2,0,1:T(8,128)(2,1)}, u32[]{:S(2)}, u32[]{:S(2)}) collective-permute-start(bf16[64,4,128]{2,0,1:T(8,128)(2,1)} %get-tuple-element.14), channel_id=1, source_target_pairs={{0,1},{2,3},{4,5},{6,7},{8,9},{10,11},{12,13},{14,15},{16,17},{18,... | collective-permute-start | bytes 196616 | tf_op jit(solution)/shard_map/ppermute | solution.py:18
  182.8 5.7 %collective-permute-start = (bf16[64,4,128]{2,0,1:T(8,128)(2,1)}, bf16[64,4,128]{2,0,1:T(8,128)(2,1)}, u32[]{:S(2)}, u32[]{:S(2)}) collective-permute-start(bf16[64,4,128]{2,0,1:T(8,128)(2,1)} %get-tuple-element.13), channel_id=1, source_target_pairs={{0,1},{2,3},{4,5},{6,7},{8,9},{10,11},{12,13},{14,15},{16,17},{18,... | collective-permute-start | bytes 196616 | tf_op jit(solution)/shard_map/ppermute | solution.py:18
  185.8 5.9 %copy-start.4 = (bf16[64,4,2,64]{3,1,2,0:T(4,128)(2,1)S(1)}, bf16[64,4,2,64]{3,1,2,0:T(4,128)(2,1)}, u32[]{:S(2)}) copy-start(bf16[64,4,2,64]{3,1,2,0:T(4,128)(2,1)} %copy.43) | copy-start | bytes 196612
  199.0 149.9 %reduce-scatter.5.cloned.1.call-start = ((), (), s32[]{:S(2)}) async-start(), calls=%async_computation.5 | async-start | bytes 2359296 | tf_op jit(solution)/shard_map/reduce_scatter | solution.py:155
  276.9 2.2 copy-start.3
Sparse Core Ops, SparseCore 0:
  27.4 65.0 reduce-scatter.2
  100.8 77.1 all-reduce.2
  199.1 77.7 all-reduce.4
  281.1 67.7 reduce-scatter.4
where the time goes:
time: 358 us; the launch traced here: 357 us
  waiting for transfers between devices  287 us (80%)
  matrix products  30.7 us (9%)
  between operations  14 us (4%)
  local copies, waits for them, and re-layouts  11.1 us (3%)
  other arithmetic  8.11 us (2%)
  starting transfers between devices  3.96 us (1%)
    psum x1, waiting for transfers between devices, per_device(): entry = lax.psum(entry_terms, 'tp')  77.2 us
    psum x1, waiting for transfers between devices, per_device(): resid = entry + lax.psum(depth_terms, 'tp')  77.1 us
    reduce_scatter x1, waiting for transfers between devices, per_device(): lax.psum_scatter(partial_logits, 'tp', scatter_dimension=2, tiled=True)  68 us
    reduce_scatter x1, waiting for transfers between devices, per_device(): lax.psum_scatter(partial_rows, 'tp', scatter_dimension=1, tiled=True)  65.1 us
  transfers between devices with their start and end apart: 6, of which 4 were waited for; matrix products, arithmetic and copies ran while one was open for 1% of the time, Pallas kernels for 0%

commit v1 on v0

--- a/solution.py
+++ b/solution.py
@@ -39,6 +39,16 @@
     return jnp.concatenate(
         [first * cosine - second * sine, first * sine + second * cosine], axis=-1
     )
+
+
+def scattered_sum(parts):
+    moved = lax.all_to_all(parts.astype(jnp.bfloat16), "tp", 0, 0)
+    return jnp.sum(moved.astype(jnp.float32), axis=0)
+
+
+def gathered(block):
+    size = lax.axis_size("tp")
+    return lax.all_to_all(jnp.broadcast_to(block[None], (size,) + block.shape), "tp", 0, 0)
 
 
 def per_device(
@@ -58,6 +68,7 @@
     head_weight,
     tokens,
 ):
+    tp = lax.axis_size("tp")
     local_streams = hidden_in.shape[0]
     local_cols = temporal_qkv.shape[2]
     local_heads = local_cols // HEAD_DIM
@@ -90,43 +101,51 @@
     mixed = mixed + own_weight.astype(jnp.float32)[..., None] * values_new.astype(jnp.float32)
     mixed = mixed.astype(jnp.bfloat16).reshape(local_streams, local_cols)
     partial_rows = jnp.dot(mixed, temporal_out_weight, preferred_element_type=jnp.float32)
-    summed = lax.psum_scatter(partial_rows, "tp", scatter_dimension=1, tiled=True)
-    slice_width = summed.shape[1]
+    slice_width = partial_rows.shape[1] // tp
+    by_slice = partial_rows.reshape(local_streams, tp, slice_width).transpose(1, 0, 2)
+    summed = scattered_sum(by_slice)
     tp_place = lax.axis_index("tp")
     resid_in = lax.dynamic_slice_in_dim(hidden_in, tp_place * slice_width, slice_width, 1)
     temporal = (resid_in.astype(jnp.float32) + summed).astype(jnp.bfloat16)
     all_rows = lax.all_gather(temporal, "section", axis=0, tiled=True)
     streams = all_rows.shape[0]
     codes = depth_in.shape[0]
-    entry_part = jnp.einsum("sd,cde->sce", all_rows, depth_in, preferred_element_type=jnp.float32)
+    width = depth_in.shape[2]
     vocab_local = depth_embed.shape[1]
     first_id = tp_place * vocab_local
     onehot = (
         tokens[:, :, None] == first_id + jnp.arange(vocab_local, dtype=jnp.int32)[None, None, :]
     ).astype(jnp.bfloat16)
-    embedded = jnp.einsum("scv,cve->sce", onehot, depth_embed, preferred_element_type=jnp.float32)
-    entry_terms = entry_part + embedded
+    embedded = jnp.einsum("scv,cve->cse", onehot, depth_embed, preferred_element_type=jnp.float32)
+    entry_terms = embedded + jnp.einsum(
+        "sd,cde->cse", all_rows, depth_in, preferred_element_type=jnp.float32
+    )
     hidden_rows = head_weight.shape[1]
     hidden_start = tp_place * hidden_rows
-    entry = lax.psum(entry_terms, "tp")
-    depth_normed = rms_norm(entry, depth_gain).astype(jnp.bfloat16)
+    entry = scattered_sum(entry_terms.reshape(codes, streams, tp, hidden_rows).transpose(2, 0, 1, 3))
+    own_gain = lax.dynamic_slice_in_dim(depth_gain, hidden_start, hidden_rows, 0)
+    scaled = (entry * own_gain).astype(jnp.bfloat16)
+    rows = gathered(scaled)
+    plain = rows.astype(jnp.float32) / depth_gain.reshape(tp, 1, 1, hidden_rows)
+    inv_rms = lax.rsqrt(jnp.sum(plain * plain, axis=(0, 3)) / width + EPSILON)
     dproj = jnp.einsum(
-        "sce,ctef->tscf", depth_normed, depth_qkv, preferred_element_type=jnp.float32
-    ).astype(jnp.bfloat16)
-    prior_keys, prior_values = passed_along((dproj[1], dproj[2]), "section", 1)
+        "tcse,cntef->ncsf",
+        rows,
+        depth_qkv.reshape(codes, 3, tp, hidden_rows, -1),
+        preferred_element_type=jnp.float32,
+    )
+    dproj = (dproj * inv_rms[None, :, :, None]).astype(jnp.bfloat16)
+    prior = passed_along(dproj[1:], "section", 1)
     depth_cols = dproj.shape[3]
     head_part = min(depth_cols, DEPTH_HDIM)
     local_parts = depth_cols // head_part
     sharers = DEPTH_HDIM // head_part
-    all_keys = jnp.concatenate([prior_keys, dproj[1]], axis=1).reshape(
-        streams, 2 * codes, local_parts, head_part
-    )
-    all_values = jnp.concatenate([prior_values, dproj[2]], axis=1).reshape(
-        streams, 2 * codes, local_parts, head_part
-    )
-    depth_queries = dproj[0].reshape(streams, codes, local_parts, head_part)
-    depth_scores = jnp.einsum(
-        "sqhd,skhd->shqk", depth_queries, all_keys, preferred_element_type=jnp.float32
+    both = jnp.concatenate([prior, dproj[1:]], axis=1)
+    all_keys = both[0].reshape(2 * codes, streams, local_parts, head_part)
+    all_values = both[1].reshape(2 * codes, streams, local_parts, head_part)
+    depth_queries = dproj[0].reshape(codes, streams, local_parts, head_part)
+    depth_scores = jnp.sum(
+        depth_queries[:, None].astype(jnp.float32) * all_keys[None].astype(jnp.float32), axis=-1
     )
     for level in range(sharers.bit_length() - 1):
         depth_scores = depth_scores + from_partner(depth_scores, "tp", level)
@@ -135,25 +154,41 @@
     query_pos = jnp.arange(codes, dtype=jnp.int32)[:, None]
     key_pos = jnp.arange(2 * codes, dtype=jnp.int32)[None, :]
     allowed = jnp.where(key_pos < codes, section_place > 0, key_pos - codes <= query_pos)
-    depth_scores = jnp.where(allowed[None, None], depth_scores, -jnp.inf)
-    depth_top = jnp.max(depth_scores, axis=-1, keepdims=True)
+    depth_scores = jnp.where(allowed[:, :, None, None], depth_scores, -jnp.inf)
+    depth_top = jnp.max(depth_scores, axis=1, keepdims=True)
     depth_expo = jnp.exp(depth_scores - depth_top)
-    depth_weights = (depth_expo / jnp.sum(depth_expo, axis=-1, keepdims=True)).astype(jnp.bfloat16)
-    depth_mixed = jnp.einsum(
-        "shqk,skhd->sqhd", depth_weights, all_values, preferred_element_type=jnp.float32
+    depth_weights = (depth_expo / jnp.sum(depth_expo, axis=1, keepdims=True)).astype(jnp.bfloat16)
+    depth_mixed = jnp.sum(
+        depth_weights[..., None].astype(jnp.float32) * all_values[None].astype(jnp.float32), axis=1
     ).astype(jnp.bfloat16)
-    depth_mixed = depth_mixed.reshape(streams, codes, depth_cols)
+    depth_mixed = depth_mixed.reshape(codes, streams, depth_cols)
     depth_terms = jnp.einsum(
-        "scf,cfe->sce", depth_mixed, depth_out_weight, preferred_element_type=jnp.float32
-    )
-    resid = entry + lax.psum(depth_terms, "tp")
-    head_normed = rms_norm(resid, head_gain).astype(jnp.bfloat16)
-    own_hidden = lax.dynamic_slice_in_dim(head_normed, hidden_start, hidden_rows, 2)
+        "csf,cfe->cse", depth_mixed, depth_out_weight, preferred_element_type=jnp.float32
+    )
+    added = scattered_sum(depth_terms.reshape(codes, streams, tp, hidden_rows).transpose(2, 0, 1, 3))
+    resid = entry + added
+    own_head_gain = lax.dynamic_slice_in_dim(head_gain, hidden_start, hidden_rows, 0)
+    own_hidden = (resid * own_head_gain).astype(jnp.bfloat16)
+    squares = jnp.sum(resid * resid, axis=2)
+    high = squares.astype(jnp.bfloat16)
+    low = (squares - high.astype(jnp.float32)).astype(jnp.bfloat16)
     partial_logits = jnp.einsum(
-        "sce,cev->scv", own_hidden, head_weight, preferred_element_type=jnp.float32
-    )
-    logits = lax.psum_scatter(partial_logits, "tp", scatter_dimension=2, tiled=True)
-    return (temporal, logits)
+        "cse,cev->csv", own_hidden, head_weight, preferred_element_type=jnp.float32
+    )
+    vocab_slice = partial_logits.shape[2] // tp
+    outgoing = partial_logits.reshape(codes, streams, tp, vocab_slice).transpose(2, 0, 1, 3)
+    outgoing = outgoing.astype(jnp.bfloat16).reshape(tp, codes * streams, vocab_slice)
+    extra = jnp.stack([high.reshape(-1), low.reshape(-1)])
+    extra = jnp.pad(extra, ((0, 14), (0, 0))).reshape(-1, vocab_slice)
+    packed = jnp.concatenate(
+        [outgoing, jnp.broadcast_to(extra[None], (tp,) + extra.shape)], axis=1
+    )
+    moved = lax.all_to_all(packed, "tp", 0, 0).astype(jnp.float32)
+    rows_total = jnp.sum(moved, axis=0)
+    stats = rows_total[codes * streams :].reshape(16, codes, streams)
+    head_inv = lax.rsqrt((stats[0] + stats[1]) / width + EPSILON)
+    logits = rows_total[: codes * streams].reshape(codes, streams, vocab_slice) * head_inv[..., None]
+    return (temporal, logits.transpose(1, 0, 2))
 
 
 def solution(mesh):

time: 358 us -> 170 us (0.47)
  waiting for transfers between devices: 287 us -> 47.8 us
  blocking collectives: 1.84 us -> 32.5 us
  starting transfers between devices: 3.96 us -> 21.6 us
  between operations: 14 us -> 0.99 us
  local copies, waits for them, and re-layouts: 11.1 us -> 21.8 us
  other arithmetic: 8.11 us -> 16.4 us
    psum x2 -> x0, waiting for transfers between devices: 154 us -> none  [the longest x1 77.2 us: per_device(): entry = lax.psum(entry_terms, 'tp')]
    reduce_scatter x2 -> x0, waiting for transfers between devices: 133 us -> none  [the longest x1 68 us: per_device(): lax.psum_scatter(partial_logits, 'tp', scatter_dimension=2, tiled=True)]
    all_to_all x0 -> x4, waiting for transfers between devices: none -> 47.7 us  [the longest x3 33.5 us: scattered_sum(): moved = lax.all_to_all(parts.astype(jnp.bfloat16), 'tp', 0, 0)]
    all_to_all x0 -> x1, blocking collectives: none -> 30.6 us  [per_device(): moved = lax.all_to_all(packed, 'tp', 0, 0).astype(jnp.float32)]
    all_to_all x0 -> x4, starting transfers between devices: none -> 19.7 us  [the longest x3 15.6 us: scattered_sum(): moved = lax.all_to_all(parts.astype(jnp.bfloat16), 'tp', 0, 0)]
    convert_element_type x1 -> x12, local copies, waits for them, and re-layouts: 1.01 us -> 10.6 us  [the longest x2 3.14 us: per_device(): all_keys[None].astype(jnp.float32)]
    reduce_sum x0 -> x9, other arithmetic: none -> 7.03 us  [the longest x3 2.29 us: scattered_sum(): return jnp.sum(moved.astype(jnp.float32), axis=0)]
    dot_general x0 -> x1, local copies, waits for them, and re-layouts: none -> 6.47 us  [per_device(): jnp.dot(mixed, temporal_out_weight, preferred_element_type=jnp.float32)]
  transfers between devices with their start and end apart: 6 -> 5, of which waited for: 4 -> 4; matrix products, arithmetic and copies ran while one was open for 1% -> 4% of each run, Pallas kernels for 0% -> 0%
where the time goes in v1:
time: 170 us; the launch traced here: 169 us
  waiting for transfers between devices  47.8 us (28%)
  blocking collectives  32.5 us (19%)
  matrix products  27.9 us (16%)
  local copies, waits for them, and re-layouts  21.8 us (13%)
  starting transfers between devices  21.6 us (13%)
  other arithmetic  16.4 us (10%)
    all_to_all x3, waiting for transfers between devices, scattered_sum(): moved = lax.all_to_all(parts.astype(jnp.bfloat16), 'tp', 0, 0)  33.5 us
    all_to_all x1, blocking collectives, per_device(): moved = lax.all_to_all(packed, 'tp', 0, 0).astype(jnp.float32)  30.6 us
    all_to_all x3, starting transfers between devices, scattered_sum(): moved = lax.all_to_all(parts.astype(jnp.bfloat16), 'tp', 0, 0)  15.6 us
    all_to_all x1, waiting for transfers between devices, gathered(): lax.all_to_all(jnp.broadcast_to(block[None], (size,) + block.shape), 'tp'...  14.3 us
    dot_general x1, matrix products, per_device(): jnp.einsum('sd,tdf->tsf', normed, temporal_qkv, preferred_element_type=jn...  7.01 us
    dot_general x1, local copies, waits for them, and re-layouts, per_device(): jnp.dot(mixed, temporal_out_weight, preferred_element_type=jnp.float32)  6.47 us
    dot_general x1, matrix products, per_device(): jnp.dot(mixed, temporal_out_weight, preferred_element_type=jnp.float32)  4.23 us
    all_to_all x1, starting transfers between devices, gathered(): lax.all_to_all(jnp.broadcast_to(block[None], (size,) + block.shape), 'tp'...  4.14 us
  transfers between devices with their start and end apart: 5, of which 4 were waited for; matrix products, arithmetic and copies ran while one was open for 4% of the time, Pallas kernels for 0%

profile of v1, /device:TPU:0, one launch (start us, length us, event | category | flops | bytes accessed | tf_op | source)
XLA Modules:
  0.0 169.0 jit_solution(8608200967481113115)
XLA Ops:
  3.4 7.0 %convolution_bitcast_fusion.2 = f32[3,32,512]{2,1,0:T(8,128)S(1)} fusion(bf16[3,4096,512]{2,1,0:T(8,128)(2,1)} %param.17, bf16[32,4096]{1,0:T(8,128)(2,1)} %param.15, f32[4096]{0:T(1024)} %param.16, f32[32]{0:T(128)S(1)} %add_rsqrt_fusion.1), kind=kOutput, calls=%fused_computation.21 | convolution fusion | flops 403177472 | bytes 13058176 | tf_op jit(solution)/shard_map/sd,tdf->tsf/dot_general | solution.py:77
  11.2 2.8 %fusion.3 = f32[32,4,1,64]{3,2,1,0:T(1,128)S(1)} fusion(bf16[32,4,128,1]{2,1,0,3:T(4,128)(2,1)S(1)} %fusion.49, bf16[32,64,512]{2,1,0:T(8,128)(2,1)} %param.19), kind=kOutput, calls=%fused_computation.5 | convolution fusion | flops 2097152 | bytes 2162688 | tf_op jit(solution)/shard_map/shd,sphd->shp/dot_general | solution.py:86
  14.6 2.2 %fusion = f32[32,4,1,128]{3,2,1,0:T(1,128)S(1)} fusion(bf16[32,4,64,1]{2,0,1,3:T(8,128)(2,1)S(1)} %fusion.38, bf16[32,64,512]{2,1,0:T(8,128)(2,1)} %param.20), kind=kOutput, calls=%fused_computation.2 | convolution fusion | flops 2097152 | bytes 2179072 | tf_op jit(solution)/shard_map/shp,sphd->shd/dot_general | solution.py:100
  16.9 6.5 %copy.73 = bf16[4096,512]{1,0:T(8,128)(2,1)} copy(bf16[4096,512]{0,1:T(8,128)(2,1)} %bitcast.120) | data formatting | bytes 8388608 | tf_op jit(solution)/shard_map/dot_general | solution.py:103
  23.4 4.2 %fusion.12 = bf16[8,32,512]{2,1,0:T(8,128)(2,1)} fusion(bf16[32,512,1]{1,0,2:T(8,128)(2,1)S(1)} %reshape.317, bf16[8,512,512]{2,1,0:T(8,128)(2,1)} %bitcast.119), kind=kOutput, calls=%fused_computation.20 | convolution fusion | flops 134348800 | bytes 4489216 | tf_op jit(solution)/shard_map/dot_general | solution.py:103
  27.6 7.3 %all-to-all-start = ((bf16[8,32,512]{2,1,0:T(8,128)(2,1)}), bf16[8,32,512]{2,1,0:T(8,128)(2,1)S(1)}, u32[]{:S(2)}, u32[]{:S(2)}) async-start(bf16[8,32,512]{2,1,0:T(8,128)(2,1)} %fusion.12), calls=%async_computation | async-start | bytes 524288 | tf_op jit(solution)/shard_map/all_to_all | solution.py:45
  35.0 3.1 %fusion.22 = f32[4,64,1024]{2,1,0:T(8,128)} fusion(bf16[4,256,1024]{2,1,0:T(8,128)(2,1)} %param.23, s32[256]{0:T(256)S(1)} %iota_add_fusion, s32[64,4]{0,1:T(4,128)S(1)} %copy-done.3), kind=kOutput, calls=%fused_computation.43 | convolution fusion | flops 134283264 | bytes 3147776 | tf_op jit(solution)/shard_map/scv,cve->cse/dot_general | solution.py:119
  38.1 5.8 %all-to-all-done = bf16[8,32,512]{2,1,0:T(8,128)(2,1)S(1)} async-done(((bf16[8,32,512]{2,1,0:T(8,128)(2,1)}), bf16[8,32,512]{2,1,0:T(8,128)(2,1)S(1)}, u32[]{:S(2)}, u32[]{:S(2)}) %all-to-all-start) | async-done | bytes 262176 | tf_op jit(solution)/shard_map/all_to_all | solution.py:45
  45.3 1.8 %all_gather.3 = bf16[64,512]{1,0:T(8,128)(2,1)S(1)} all-gather(bf16[32,512]{1,0:T(8,128)(2,1)S(1)} %add_convert_fusion), channel_id=1, replica_groups=mesh['grp'=2,'tp'=8,'section'=2] {'section'}, dimensions={0}, use_global_device_ids=true | all-gather | bytes 98304 | tf_op jit(solution)/shard_map/all_gather | solution.py:110
  47.1 3.4 %fusion.9 = bf16[4,8,8,8,128]{4,3,2,1,0:T(8,128)(2,1)S(1)} fusion(f32[4,64,1024]{2,1,0:T(8,128)} %fusion.22, bf16[4,512,1024]{2,1,0:T(8,128)(2,1)} %param.22, bf16[64,512]{1,0:T(8,128)(2,1)S(1)} %all_gather.3), kind=kOutput, calls=%fused_computation.15 | convolution fusion | flops 268959744 | bytes 5832704 | tf_op jit(solution)/shard_map/sd,cde->cse/dot_general | solution.py:120
  51.5 4.1 %all-to-all-start.1 = ((bf16[8,4,64,128]{3,2,1,0:T(8,128)(2,1)}), bf16[8,4,64,128]{3,2,1,0:T(8,128)(2,1)}, u32[]{:S(2)}, u32[]{:S(2)}) async-start(bf16[8,4,64,128]{3,2,1,0:T(8,128)(2,1)} %bitcast.124), calls=%async_computation.1 | async-start | bytes 1048576 | tf_op jit(solution)/shard_map/all_to_all | solution.py:45
  55.7 15.0 %all-to-all-done.1 = bf16[8,4,64,128]{3,2,1,0:T(8,128)(2,1)} async-done(((bf16[8,4,64,128]{3,2,1,0:T(8,128)(2,1)}), bf16[8,4,64,128]{3,2,1,0:T(8,128)(2,1)}, u32[]{:S(2)}, u32[]{:S(2)}) %all-to-all-start.1) | async-done | bytes 524320 | tf_op jit(solution)/shard_map/all_to_all | solution.py:45
  72.8 4.1 %all-to-all-start.2 = ((bf16[8,4,64,128]{3,2,1,0:T(8,128)(2,1)}), bf16[8,4,64,128]{3,2,1,0:T(8,128)(2,1)}, u32[]{:S(2)}, u32[]{:S(2)}) async-start(bf16[8,4,64,128]{3,2,1,0:T(8,128)(2,1)} %broadcast_in_dim.41), calls=%async_computation.2 | async-start | bytes 1048576 | tf_op jit(solution)/shard_map/all_to_all | solution.py:51
  77.0 14.3 %all-to-all-done.2 = bf16[8,4,64,128]{3,2,1,0:T(8,128)(2,1)} async-done(((bf16[8,4,64,128]{3,2,1,0:T(8,128)(2,1)}), bf16[8,4,64,128]{3,2,1,0:T(8,128)(2,1)}, u32[]{:S(2)}, u32[]{:S(2)}) %all-to-all-start.2) | async-done | bytes 524320 | tf_op jit(solution)/shard_map/all_to_all | solution.py:51
  92.5 1.7 %fusion.13 = bf16[3,4,64,128]{3,2,0,1:T(8,128)(2,1)S(1)} fusion(bf16[4,3,8,128,128]{4,3,2,1,0:T(8,128)(2,1)S(1)} %bitcast.118, f32[4,64]{1,0:T(4,128)S(1)} %add_rsqrt_fusion, bf16[8,4,64,128]{3,2,1,0:T(8,128)(2,1)} %all-to-all-done.2), kind=kOutput, calls=%fused_computation.22 | convolution fusion | flops 201523200 | bytes 3867648 | tf_op jit(solution)/shard_map/tcse,cntef->ncsf/dot_general | solution.py:131
  94.9 1.9 %collective-permute-start = (bf16[2,4,64,128]{3,2,0,1:T(8,128)(2,1)}, bf16[2,4,64,128]{3,2,0,1:T(8,128)(2,1)}, u32[]{:S(2)}, u32[]{:S(2)}) collective-permute-start(bf16[2,4,64,128]{3,2,0,1:T(8,128)(2,1)} %slice.71), channel_id=1, source_target_pairs={{0,1},{2,3},{4,5},{6,7},{8,9},{10,11},{12,13},{14,15},{16,17},{18,... | collective-permute-start | bytes 393224 | tf_op jit(solution)/shard_map/ppermute | solution.py:18
  99.3 1.7 fusion.25
  101.0 2.1 %reshape.310 = f32[8,64,2,64]{3,2,1,0:T(2,128)} reshape(f32[1,8,64,128]{3,2,0,1:T(8,128)} %get-tuple-element.12) | data formatting | bytes 524288 | tf_op jit(solution)/shard_map/convert_element_type | solution.py:148
  104.1 1.6 multiply_reduce_fusion.1
  110.7 1.5 fusion.8
  113.2 4.1 %all-to-all-start.3 = ((bf16[8,4,64,128]{3,2,1,0:T(8,128)(2,1)}), bf16[8,4,64,128]{3,2,1,0:T(8,128)(2,1)}, u32[]{:S(2)}, u32[]{:S(2)}) async-start(bf16[8,4,64,128]{3,2,1,0:T(8,128)(2,1)} %bitcast.125), calls=%async_computation.3 | async-start | bytes 1048576 | tf_op jit(solution)/shard_map/all_to_all | solution.py:45
  118.1 12.7 %all-to-all-done.3 = bf16[8,4,64,128]{3,2,1,0:T(8,128)(2,1)} async-done(((bf16[8,4,64,128]{3,2,1,0:T(8,128)(2,1)}), bf16[8,4,64,128]{3,2,1,0:T(8,128)(2,1)}, u32[]{:S(2)}, u32[]{:S(2)}) %all-to-all-start.3) | async-done | bytes 524320 | tf_op jit(solution)/shard_map/all_to_all | solution.py:45
  132.0 2.0 %convolution_convert_fusion = bf16[4,64,2048]{2,1,0:T(8,128)(2,1)S(1)} fusion(bf16[4,128,2048]{2,1,0:T(8,128)(2,1)} %param.28, f32[128]{0:T(128)S(1)} %dynamic_slice.11, f32[4,64,128]{2,1,0:T(8,128)S(1)} %convert_reduce_fusion.2, f32[4,64,128]{2,1,0:T(8,128)S(1)} %convert_reduce_fusion.1), kind=kOutput, calls=%fused_computation | convolution fusion | flops 134840320 | bytes 3408384 | tf_op jit(solution)/shard_map/cse,cev->csv/dot_general | solution.py:175
  137.1 30.6 %all_to_all.25 = bf16[8,272,256]{2,1,0:T(8,128)(2,1)S(1)} all-to-all(bf16[8,272,256]{2,1,0:T(8,128)(2,1)S(1)} %pad_maximum_fusion), channel_id=1, replica_groups=mesh['grp'=2,'tp'=8,'section'=2] {'tp'}, dimensions={0} | all-to-all | bytes 2228224 | tf_op jit(solution)/shard_map/all_to_all | solution.py:186
  (76 shorter events, 26.4 us)
Async XLA Ops:
  0.6 91.9 %copy-start = (bf16[4,3,1024,128]{3,2,1,0:T(8,128)(2,1)S(1)}, bf16[4,3,1024,128]{3,2,1,0:T(8,128)(2,1)}, u32[]{:S(2)}) copy-start(bf16[4,3,1024,128]{3,2,1,0:T(8,128)(2,1)} %param.25) | copy-start | bytes 9437188
  23.4 11.5 %copy-start.3 = (s32[64,4]{0,1:T(4,128)S(1)}, s32[64,4]{0,1:T(4,128)}, u32[]{:S(2)}) copy-start(s32[64,4]{0,1:T(4,128)} %param.29) | copy-start | bytes 3076
  27.6 16.2 %all-to-all-start = ((bf16[8,32,512]{2,1,0:T(8,128)(2,1)}), bf16[8,32,512]{2,1,0:T(8,128)(2,1)S(1)}, u32[]{:S(2)}, u32[]{:S(2)}) async-start(bf16[8,32,512]{2,1,0:T(8,128)(2,1)} %fusion.12), calls=%async_computation | async-start | bytes 524288 | tf_op jit(solution)/shard_map/all_to_all | solution.py:45
  44.7 0.6 copy-start.1
  50.5 5.1 %copy-start.2 = (f32[1024]{0:T(1024)S(1)}, f32[1024]{0:T(1024)}, u32[]{:S(2)}) copy-start(f32[1024]{0:T(1024)} %param.24) | copy-start | bytes 12292
  51.5 19.2 %all-to-all-start.1 = ((bf16[8,4,64,128]{3,2,1,0:T(8,128)(2,1)}), bf16[8,4,64,128]{3,2,1,0:T(8,128)(2,1)}, u32[]{:S(2)}, u32[]{:S(2)}) async-start(bf16[8,4,64,128]{3,2,1,0:T(8,128)(2,1)} %bitcast.124), calls=%async_computation.1 | async-start | bytes 1048576 | tf_op jit(solution)/shard_map/all_to_all | solution.py:45
  72.8 18.4 %all-to-all-start.2 = ((bf16[8,4,64,128]{3,2,1,0:T(8,128)(2,1)}), bf16[8,4,64,128]{3,2,1,0:T(8,128)(2,1)}, u32[]{:S(2)}, u32[]{:S(2)}) async-start(bf16[8,4,64,128]{3,2,1,0:T(8,128)(2,1)} %broadcast_in_dim.41), calls=%async_computation.2 | async-start | bytes 1048576 | tf_op jit(solution)/shard_map/all_to_all | solution.py:51
  94.9 4.4 %collective-permute-start = (bf16[2,4,64,128]{3,2,0,1:T(8,128)(2,1)}, bf16[2,4,64,128]{3,2,0,1:T(8,128)(2,1)}, u32[]{:S(2)}, u32[]{:S(2)}) collective-permute-start(bf16[2,4,64,128]{3,2,0,1:T(8,128)(2,1)} %slice.71), channel_id=1, source_target_pairs={{0,1},{2,3},{4,5},{6,7},{8,9},{10,11},{12,13},{14,15},{16,17},{18,... | collective-permute-start | bytes 393224 | tf_op jit(solution)/shard_map/ppermute | solution.py:18
  113.2 17.6 %all-to-all-start.3 = ((bf16[8,4,64,128]{3,2,1,0:T(8,128)(2,1)}), bf16[8,4,64,128]{3,2,1,0:T(8,128)(2,1)}, u32[]{:S(2)}, u32[]{:S(2)}) async-start(bf16[8,4,64,128]{3,2,1,0:T(8,128)(2,1)} %bitcast.125), calls=%async_computation.3 | async-start | bytes 1048576 | tf_op jit(solution)/shard_map/all_to_all | solution.py:45

commit v2 on v1

--- a/solution.py
+++ b/solution.py
@@ -1,8 +1,11 @@
+import functools
 import math
 
 import jax
 import jax.numpy as jnp
 from jax import lax
+from jax.experimental import pallas as pl
+from jax.experimental.pallas import tpu as pltpu
 from jax.sharding import PartitionSpec as P
 
 HEAD_DIM = 128
@@ -51,7 +54,7 @@
     return lax.all_to_all(jnp.broadcast_to(block[None], (size,) + block.shape), "tp", 0, 0)
 
 
-def per_device(
+def general_device(
     hidden_in,
     temporal_gain,
     temporal_qkv,
@@ -191,6 +194,569 @@
     return (temporal, logits.transpose(1, 0, 2))
 
 
+HBM = pl.BlockSpec(memory_space=pltpu.HBM)
+VMEM = pl.BlockSpec(memory_space=pltpu.VMEM)
+SMEM = pl.BlockSpec(memory_space=pltpu.SMEM)
+
+
+def params(mebibytes):
+    return pltpu.CompilerParams(vmem_limit_bytes=mebibytes * 1024 * 1024)
+
+
+def in_hbm(array):
+    return pltpu.with_memory_space_constraint(array, pltpu.HBM)
+
+
+def shape(dims, dtype):
+    return jax.ShapeDtypeStruct(dims, dtype)
+
+
+def product(left, right):
+    return jnp.dot(left, right, preferred_element_type=jnp.float32)
+
+
+def product_t(left, right):
+    return lax.dot_general(left, right, (((1,), (1,)), ((), ())), preferred_element_type=jnp.float32)
+
+
+def column_of(row):
+    size = row.shape[1]
+    first = lax.broadcasted_iota(jnp.int32, (size, size), 0)
+    second = lax.broadcasted_iota(jnp.int32, (size, size), 1)
+    return jnp.sum(jnp.where(first == second, row, 0.0), axis=1, keepdims=True)
+
+
+def temporal_kernel(
+    hidden_hbm, gain_hbm, lengths_ref, qkv_hbm, out_hbm, keys_hbm, values_hbm, parts_ref,
+    hidden_buf, gain_buf, qkv_buf, out_buf, keys_buf, values_buf, small_sems, qkv_sems, out_sems, cache_sems,
+):
+    streams, depth = hidden_buf.shape
+    cols = qkv_buf.shape[2]
+    heads = cols // HEAD_DIM
+    cache_len = keys_buf.shape[1]
+    steps = qkv_sems.shape[1]
+    chunk = depth // steps
+    places = parts_ref.shape[0]
+    width = parts_ref.shape[2]
+    small = [
+        pltpu.make_async_copy(hidden_hbm, hidden_buf, small_sems.at[0]),
+        pltpu.make_async_copy(gain_hbm, gain_buf, small_sems.at[1]),
+    ]
+    weight = [
+        [
+            pltpu.make_async_copy(
+                qkv_hbm.at[n, pl.ds(i * chunk, chunk)],
+                qkv_buf.at[n, pl.ds(i * chunk, chunk)],
+                qkv_sems.at[n, i],
+            )
+            for i in range(steps)
+        ]
+        for n in range(3)
+    ]
+    caches = [
+        pltpu.make_async_copy(keys_hbm, keys_buf, cache_sems.at[0]),
+        pltpu.make_async_copy(values_hbm, values_buf, cache_sems.at[1]),
+    ]
+    outs = [
+        pltpu.make_async_copy(
+            out_hbm.at[:, pl.ds(t * width, width)], out_buf.at[:, pl.ds(t * width, width)], out_sems.at[t]
+        )
+        for t in range(places)
+    ]
+    for copy in small + weight[0] + weight[1] + caches[:1] + weight[2] + caches[1:] + outs:
+        copy.start()
+
+    for copy in small:
+        copy.wait()
+    wide = hidden_buf[...].astype(jnp.float32)
+    inv = lax.rsqrt(jnp.mean(wide * wide, axis=1, keepdims=True) + EPSILON)
+    normed = (wide * inv * gain_buf[...]).astype(jnp.bfloat16)
+
+    def projected(n):
+        total = None
+        for i in range(steps):
+            weight[n][i].wait()
+            part = product(normed[:, i * chunk : (i + 1) * chunk], qkv_buf[n, pl.ds(i * chunk, chunk), :])
+            total = part if total is None else total + part
+        return total
+
+    lengths_row = lengths_ref[...].astype(jnp.float32)
+    lengths_col = column_of(lengths_row)
+    half = HEAD_DIM // 2
+    lane = lax.broadcasted_iota(jnp.int32, (streams, HEAD_DIM), 1)
+    spacing = (lane & (half - 1)).astype(jnp.float32) / half
+    angles = lengths_col * jnp.exp(-math.log(10000.0) * spacing)
+    cosine = jnp.cos(angles)
+    sine = jnp.where(lane < half, -1.0, 1.0) * jnp.sin(angles)
+
+    def rotated(block):
+        pieces = []
+        for h in range(heads):
+            piece = block[:, h * HEAD_DIM : (h + 1) * HEAD_DIM]
+            pieces.append(piece * cosine + pltpu.roll(piece, half, 1) * sine)
+        return jnp.concatenate(pieces, axis=1)
+
+    queries = rotated(projected(0))
+    keys_new = rotated(projected(1)).astype(jnp.bfloat16)
+    head_lane = lax.broadcasted_iota(jnp.int32, (streams, cols), 1) // HEAD_DIM
+    spread = jnp.concatenate(
+        [jnp.where(head_lane == h, queries, 0.0) for h in range(heads)], axis=0
+    ).astype(jnp.bfloat16)
+    pairs = heads * streams
+    factor = 1.0 / math.sqrt(HEAD_DIM)
+    pair = lax.broadcasted_iota(jnp.int32, (1, pairs), 1)
+    pair_stream = pair % streams
+    own = product_t(keys_new, spread) * factor
+    stream_row = lax.broadcasted_iota(jnp.int32, (streams, pairs), 0)
+    own_score = jnp.sum(jnp.where(stream_row == pair_stream, own, 0.0), axis=0, keepdims=True)
+    tiled = jnp.sum(jnp.where(stream_row == pair_stream, lengths_col, 0.0), axis=0, keepdims=True)
+    first_row = pair_stream * cache_len
+    last_row = first_row + tiled.astype(jnp.int32)
+    caches[0].wait()
+    rows = streams * cache_len
+    scores = product_t(keys_buf[...].reshape(rows, cols), spread) * factor
+    row = lax.broadcasted_iota(jnp.int32, (rows, pairs), 0)
+    scores = jnp.where((row >= first_row) & (row < last_row), scores, -jnp.inf)
+    highest = jnp.maximum(jnp.max(scores, axis=0, keepdims=True), own_score)
+    expo = jnp.exp(scores - highest)
+    own_expo = jnp.exp(own_score - highest)
+    inverse = 1.0 / (jnp.sum(expo, axis=0, keepdims=True) + own_expo)
+    weights = (expo * inverse).astype(jnp.bfloat16)
+    own_weight = (own_expo * inverse).astype(jnp.bfloat16).astype(jnp.float32)
+    values_new = projected(2).astype(jnp.bfloat16).astype(jnp.float32)
+    caches[1].wait()
+    mixed_all = lax.dot_general(
+        weights,
+        values_buf[...].reshape(rows, cols),
+        (((0,), (0,)), ((), ())),
+        preferred_element_type=jnp.float32,
+    )
+    pair_lane = lax.broadcasted_iota(jnp.int32, (streams, pairs), 1)
+    pair_row = lax.broadcasted_iota(jnp.int32, (streams, pairs), 0)
+    mixed = []
+    for h in range(heads):
+        own_col = jnp.sum(
+            jnp.where(pair_lane == pair_row + h * streams, own_weight, 0.0), axis=1, keepdims=True
+        )
+        lanes = slice(h * HEAD_DIM, (h + 1) * HEAD_DIM)
+        mixed.append(
+            mixed_all[h * streams : (h + 1) * streams, lanes] + own_col * values_new[:, lanes]
+        )
+    mixed = jnp.concatenate(mixed, axis=1).astype(jnp.bfloat16)
+    for t in range(places):
+        outs[t].wait()
+        parts_ref[t] = product(mixed, out_buf[:, pl.ds(t * width, width)]).astype(jnp.bfloat16)
+
+
+def temporal_parts(hidden_in, gain, lengths, qkv, out_weight, keys, values, places):
+    streams, depth = hidden_in.shape
+    cols = qkv.shape[2]
+    steps = 4
+    bf16 = jnp.bfloat16
+    return pl.pallas_call(
+        temporal_kernel,
+        in_specs=[HBM, HBM, VMEM, HBM, HBM, HBM, HBM],
+        out_specs=VMEM,
+        out_shape=shape((places, streams, out_weight.shape[1] // places), bf16),
+        scratch_shapes=[
+            pltpu.VMEM(hidden_in.shape, bf16),
+            pltpu.VMEM((1, depth), jnp.float32),
+            pltpu.VMEM(qkv.shape, bf16),
+            pltpu.VMEM(out_weight.shape, bf16),
+            pltpu.VMEM(keys.shape, bf16),
+            pltpu.VMEM(values.shape, bf16),
+            pltpu.SemaphoreType.DMA((2,)),
+            pltpu.SemaphoreType.DMA((3, steps)),
+            pltpu.SemaphoreType.DMA((places,)),
+            pltpu.SemaphoreType.DMA((2,)),
+        ],
+        compiler_params=params(30),
+        name="temporal",
+    )(
+        in_hbm(hidden_in),
+        in_hbm(gain.reshape(1, depth)),
+        lengths.reshape(1, streams),
+        in_hbm(qkv),
+        in_hbm(out_weight),
+        in_hbm(keys),
+        in_hbm(values),
+    )
+
+
+def entry_kernel(rows_ref, tokens_ref, weight_hbm, embed_hbm, parts_ref, weight_buf, embed_buf, sems):
+    codes, depth, width = weight_buf.shape
+    vocab = embed_buf.shape[1]
+    places = parts_ref.shape[0]
+    part = width // places
+    streams = rows_ref.shape[0]
+    weight = [pltpu.make_async_copy(weight_hbm.at[c], weight_buf.at[c], sems.at[0, c]) for c in range(codes)]
+    embed = [pltpu.make_async_copy(embed_hbm.at[c], embed_buf.at[c], sems.at[1, c]) for c in range(codes)]
+    for c in range(codes):
+        embed[c].start()
+        weight[c].start()
+    vocab_lane = lax.broadcasted_iota(jnp.int32, (streams, vocab), 1)
+    for c in range(codes):
+        hit = tokens_ref[:, c : c + 1] == vocab_lane
+        onehot = jnp.where(hit, 1.0, 0.0).astype(jnp.bfloat16)
+        embed[c].wait()
+        total = product(onehot, embed_buf[c])
+        weight[c].wait()
+        total = (total + product(rows_ref[...], weight_buf[c])).astype(jnp.bfloat16)
+        for t in range(places):
+            parts_ref[t, c] = total[:, t * part : (t + 1) * part]
+
+
+def entry_parts(rows, local_tokens, weight, embed, places):
+    codes, depth, width = weight.shape
+    streams = rows.shape[0]
+    return pl.pallas_call(
+        entry_kernel,
+        in_specs=[VMEM, VMEM, HBM, HBM],
+        out_specs=VMEM,
+        out_shape=shape((places, codes, streams, width // places), jnp.bfloat16),
+        scratch_shapes=[
+            pltpu.VMEM(weight.shape, jnp.bfloat16),
+            pltpu.VMEM(embed.shape, jnp.bfloat16),
+            pltpu.SemaphoreType.DMA((2, codes)),
+        ],
+        compiler_params=params(24),
+        name="entry",
+    )(rows, local_tokens, weight, embed)
+
+
+def qkv_kernel(rows_ref, gain_ref, weight_hbm, queries_ref, pair_ref, weight_buf, sems):
+    codes, _, width, cols = weight_buf.shape
+    places = rows_ref.shape[0]
+    copies = [pltpu.make_async_copy(weight_hbm.at[c], weight_buf.at[c], sems.at[c]) for c in range(codes)]
+    for copy in copies:
+        copy.start()
+    inverse_gain = 1.0 / gain_ref[...]
+    for c in range(codes):
+        row = jnp.concatenate([rows_ref[t, c] for t in range(places)], axis=1)
+        plain = row.astype(jnp.float32) * inverse_gain
+        inv = lax.rsqrt(jnp.sum(plain * plain, axis=1, keepdims=True) / width + EPSILON)
+        copies[c].wait()
+        for n in range(3):
+            value = (product(row, weight_buf[c, n]) * inv).astype(jnp.bfloat16)
+            if n == 0:
+                queries_ref[c] = value
+            else:
+                pair_ref[n - 1, c] = value
+
+
+def depth_projections(rows, gain, weight):
+    codes, _, width, cols = weight.shape
+    streams = rows.shape[2]
+    bf16 = jnp.bfloat16
+    return pl.pallas_call(
+        qkv_kernel,
+        in_specs=[VMEM, VMEM, HBM],
+        out_specs=[VMEM, VMEM],
+        out_shape=[shape((codes, streams, cols), bf16), shape((2, codes, streams, cols), bf16)],
+        scratch_shapes=[pltpu.VMEM(weight.shape, bf16), pltpu.SemaphoreType.DMA((codes,))],
+        compiler_params=params(16),
+        name="depth_qkv",
+    )(rows, gain.reshape(1, width), weight)
+
+
+def mix_kernel(place_ref, queries_ref, own_ref, prior_ref, weight_hbm, kept_ref, *rest):
+    sends, (total_buf, weight_buf, sems) = rest[:-3], rest[-3:]
+    codes, streams, cols = queries_ref.shape
+    span = kept_ref.shape[2]
+    copy = pltpu.make_async_copy(weight_hbm, weight_buf, sems)
+    copy.start()
+    has_prior = place_ref[1] > 0
+    first = lax.broadcasted_iota(jnp.int32, (2 * cols, cols), 0) % cols
+    second = lax.broadcasted_iota(jnp.int32, (2 * cols, cols), 1)
+    same = jnp.where(first // DEPTH_HDIM == second // DEPTH_HDIM, 1.0, 0.0).astype(jnp.bfloat16)
+    keys = [prior_ref[0, j].astype(jnp.float32) for j in range(codes)]
+    keys += [own_ref[0, j].astype(jnp.float32) for j in range(codes)]
+    values = [prior_ref[1, j].astype(jnp.float32) for j in range(codes)]
+    values += [own_ref[1, j].astype(jnp.float32) for j in range(codes)]
+    factor = 1.0 / math.sqrt(DEPTH_HDIM)
+    mixed = []
+    for q in range(codes):
+        query = queries_ref[q].astype(jnp.float32)
+        reach = codes + q + 1
+        pieces = []
+        for j in range(reach):
+            exact = query * keys[j]
+            high = exact.astype(jnp.bfloat16)
+            low = (exact - high.astype(jnp.float32)).astype(jnp.bfloat16)
+            pieces.append(jnp.concatenate([high, low], axis=1))
+        scores = product(jnp.concatenate(pieces, axis=0), same) * factor
+        score = [scores[j * streams : (j + 1) * streams] for j in range(reach)]
+        score = [jnp.where(has_prior, s, -jnp.inf) if j < codes else s for j, s in enumerate(score)]
+        top = score[0]
+        for s in score[1:]:
+            top = jnp.maximum(top, s)
+        expo = [jnp.exp(s - top) for s in score]
+        inverse = 1.0 / sum(expo)
+        total = jnp.zeros_like(query)
+        for j in range(reach):
+            total = total + (expo[j] * inverse).astype(jnp.bfloat16).astype(jnp.float32) * values[j]
+        mixed.append(total.astype(jnp.bfloat16))
+    copy.wait()
+    for q in range(codes):
+        total_buf[q] = product(mixed[q], weight_buf[q])
+    place = place_ref[0] // 2
+    for k in range(len(sends) + 1):
+        start = pl.multiple_of((place ^ k) * span, span)
+        block = total_buf[:, :, pl.ds(start, span)]
+        if k == 0:
+            kept_ref[...] = block
+        else:
+            sends[k - 1][...] = block.astype(jnp.bfloat16)
+
+
+def mixed_parts(place, queries, own, prior, weight, far):
+    codes, streams, cols = queries.shape
+    width = weight.shape[2]
+    block = (codes, streams, width // (far + 1))
+    return pl.pallas_call(
+        mix_kernel,
+        in_specs=[SMEM, VMEM, VMEM, VMEM, HBM],
+        out_specs=[VMEM] * (far + 1),
+        out_shape=[shape(block, jnp.float32)] + [shape(block, jnp.bfloat16)] * far,
+        scratch_shapes=[
+            pltpu.VMEM((codes, streams, width), jnp.float32),
+            pltpu.VMEM(weight.shape, jnp.bfloat16),
+            pltpu.SemaphoreType.DMA(()),
+        ],
+        compiler_params=params(16),
+        name="depth_mix",
+    )(place, queries, own, prior, weight)
+
+
+def pair_sum_kernel(place_ref, entry_ref, kept_ref, *rest):
+    arrived, (total_ref, sent_ref) = rest[:-2], rest[-2:]
+    total = kept_ref[...]
+    for block in arrived:
+        total = total + block[...].astype(jnp.float32)
+    entry = entry_ref[...]
+    none = jnp.zeros_like(entry)
+    odd = place_ref[0] % 2 == 1
+    total = total + jnp.concatenate([jnp.where(odd, none, entry), jnp.where(odd, entry, none)], axis=2)
+    total_ref[...] = total
+    sent_ref[...] = total.astype(jnp.bfloat16)
+
+
+def pair_sums(place, entry, kept, arrived):
+    return pl.pallas_call(
+        pair_sum_kernel,
+        in_specs=[SMEM] + [VMEM] * (2 + len(arrived)),
+        out_specs=[VMEM, VMEM],
+        out_shape=[shape(kept.shape, jnp.float32), shape(kept.shape, jnp.bfloat16)],
+        compiler_params=params(16),
+        name="pair_sum",
+    )(place, entry, kept, *arrived)
+
+
+def swap_kernel(place_ref, weight_hbm, *rest):
+    halves, sems = rest[:-1], rest[-1]
+    count, codes, _, part = halves[0].shape
+    other = 1 - place_ref[0] % 2
+    copies = [
+        pltpu.make_async_copy(
+            weight_hbm.at[pl.ds(n * codes, codes), :, pl.ds(pl.multiple_of((2 * k + other) * part, part), part)],
+            half.at[k],
+            sems.at[n, k],
+        )
+        for n, half in enumerate(halves)
+        for k in range(count)
+    ]
+    for copy in copies:
+        copy.start()
+    for copy in copies:
+        copy.wait()
+
+
+def partner_columns(place, weight, places):
+    codes, depth, vocab = weight.shape
+    half = shape((places // 2, codes // 2, depth, vocab // places), jnp.bfloat16)
+    return pl.pallas_call(
+        swap_kernel,
+        in_specs=[SMEM, HBM],
+        out_specs=[VMEM, VMEM],
+        out_shape=[half, half],
+        scratch_shapes=[pltpu.SemaphoreType.DMA((2, places // 2))],
+        name="partner_columns",
+    )(place, in_hbm(weight))
+
+
+STAT_ROWS = 16
+
+
+def head_kernel(place_ref, gain_ref, total_ref, arrived_ref, own_hbm, early_ref, late_ref, kept_ref, stat_ref, *rest):
+    sends, (weight_buf, sems) = rest[:-2], rest[-2:]
+    codes, streams, span = total_ref.shape
+    count, _, depth, part = weight_buf.shape
+    odd = place_ref[0] % 2
+    place = place_ref[0] // 2
+    copies = [
+        pltpu.make_async_copy(
+            own_hbm.at[:, :, pl.ds(pl.multiple_of((2 * (place ^ k) + odd) * part, part), part)],
+            weight_buf.at[k],
+            sems.at[k],
+        )
+        for k in range(count)
+    ]
+    for copy in copies:
+        copy.start()
+    resid = total_ref[...] + arrived_ref[...].astype(jnp.float32)
+    flat = resid.reshape(codes * streams, span)
+    squares = flat * flat
+    stat = product_t(jnp.ones((STAT_ROWS // 2, span), jnp.float32), squares)[:1]
+    stat_ref[...] = stat
+    high = stat.astype(jnp.bfloat16).astype(jnp.float32)
+    stat_row = lax.broadcasted_iota(jnp.int32, (STAT_ROWS, codes * streams), 0)
+    stat_block = jnp.where(stat_row == 0, high, jnp.where(stat_row == 1, stat - high, 0.0))
+    stat_block = stat_block.astype(jnp.bfloat16)
+    scaled = resid * gain_ref[...]
+    low_half, high_half = scaled[:, :, :depth], scaled[:, :, depth:]
+    ordered = jnp.concatenate(
+        [jnp.where(odd == 1, high_half, low_half), jnp.where(odd == 1, low_half, high_half)], axis=2
+    ).astype(jnp.bfloat16)
+    rows = codes * streams
+    for k in range(count):
+        copies[k].wait()
+        blocks = []
+        for c in range(codes):
+            partner = early_ref[place ^ k, c] if c < codes // 2 else late_ref[place ^ k, c - codes // 2]
+            blocks.append(product(ordered[c], jnp.concatenate([weight_buf[k, c], partner], axis=0)))
+        block = jnp.concatenate(blocks, axis=0)
+        if k == 0:
+            kept_ref[...] = block
+        else:
+            sends[k - 1][pl.ds(0, rows), :] = block.astype(jnp.bfloat16)
+            sends[k - 1][pl.ds(rows, STAT_ROWS), :] = stat_block
+
+
+def head_parts(place, gain, total, arrived, weight, early, late):
+    codes, streams, span = total.shape
+    count, _, depth, part = early.shape
+    rows = codes * streams
+    return pl.pallas_call(
+        head_kernel,
+        in_specs=[SMEM, VMEM, VMEM, VMEM, HBM, VMEM, VMEM],
+        out_specs=[VMEM] * (count + 1),
+        out_shape=[shape((rows, part), jnp.float32), shape((1, rows), jnp.float32)]
+        + [shape((rows + STAT_ROWS, part), jnp.bfloat16)] * (count - 1),
+        scratch_shapes=[
+            pltpu.VMEM((count, codes, depth, part), jnp.bfloat16),
+            pltpu.SemaphoreType.DMA((count,)),
+        ],
+        compiler_params=params(16),
+        name="head",
+    )(place, gain, total, arrived, in_hbm(weight), early, late)
+
+
+def logits_kernel(width, kept_ref, stat_ref, *rest):
+    arrived, out_ref = rest[:-1], rest[-1]
+    streams, codes, part = out_ref.shape
+    rows = codes * streams
+    total = kept_ref[...]
+    stat = stat_ref[...]
+    for block in arrived:
+        wide = block[...].astype(jnp.float32)
+        total = total + wide[:rows]
+        stat = stat + wide[rows : rows + 1] + wide[rows + 1 : rows + 2]
+    total = total * column_of(lax.rsqrt(stat / width + EPSILON))
+    for c in range(codes):
+        out_ref[:, c, :] = total[c * streams : (c + 1) * streams]
+
+
+def finished_logits(kept, stat, arrived, codes, width):
+    rows, part = kept.shape
+    return pl.pallas_call(
+        functools.partial(logits_kernel, width),
+        in_specs=[VMEM] * (2 + len(arrived)),
+        out_specs=VMEM,
+        out_shape=shape((rows // codes, codes, part), jnp.float32),
+        compiler_params=params(16),
+        name="logits",
+    )(kept, stat, *arrived)
+
+
+def paired_device(
+    hidden_in,
+    temporal_gain,
+    temporal_qkv,
+    temporal_out_weight,
+    cache_keys,
+    cache_values,
+    lengths,
+    depth_in,
+    depth_embed,
+    depth_gain,
+    depth_qkv,
+    depth_out_weight,
+    head_gain,
+    head_weight,
+    tokens,
+):
+    tp = lax.axis_size("tp")
+    tp_place = lax.axis_index("tp")
+    place = jnp.stack([tp_place, lax.axis_index("section")])
+    far = tp // 2 - 1
+
+    def to_pairs(blocks):
+        return [
+            lax.ppermute(block, "tp", [(i, i ^ 2 * (k + 1)) for i in range(tp)])
+            for k, block in enumerate(blocks)
+        ]
+
+    def to_neighbour(block):
+        return lax.ppermute(block, "tp", [(i, i ^ 1) for i in range(tp)])
+
+    early_half, late_half = partner_columns(place, head_weight, tp)
+    early = to_neighbour(early_half)
+    parts = temporal_parts(
+        hidden_in, temporal_gain, lengths, temporal_qkv, temporal_out_weight, cache_keys, cache_values, tp
+    )
+    slice_width = parts.shape[2]
+    parts, early = lax.optimization_barrier((parts, early))
+    summed = scattered_sum(parts)
+    resid_in = lax.dynamic_slice_in_dim(hidden_in, tp_place * slice_width, slice_width, 1)
+    temporal = (resid_in.astype(jnp.float32) + summed).astype(jnp.bfloat16)
+    all_rows = lax.all_gather(temporal, "section", axis=0, tiled=True)
+    codes = depth_in.shape[0]
+    width = depth_in.shape[2]
+    hidden_rows = head_weight.shape[1]
+    local_tokens = tokens - tp_place * depth_embed.shape[1]
+    entry = scattered_sum(entry_parts(all_rows, local_tokens, depth_in, depth_embed, tp))
+    own_gain = lax.dynamic_slice_in_dim(depth_gain, tp_place * hidden_rows, hidden_rows, 0)
+    rows = gathered((entry * own_gain).astype(jnp.bfloat16))
+    queries, own_pair = depth_projections(rows, depth_gain, depth_qkv)
+    prior_pair = passed_along(own_pair, "section", 1)
+    kept, *blocks = mixed_parts(place, queries, own_pair, prior_pair, depth_out_weight, far)
+    late_half, kept = lax.optimization_barrier((late_half, kept))
+    late = to_neighbour(late_half)
+    total, sent = pair_sums(place, entry, kept, to_pairs(blocks))
+    pair_gain = lax.dynamic_slice_in_dim(head_gain, tp_place // 2 * 2 * hidden_rows, 2 * hidden_rows, 0)
+    kept, stat, *blocks = head_parts(
+        place, pair_gain.reshape(1, 1, -1), total, to_neighbour(sent), head_weight, early, late
+    )
+    logits = finished_logits(kept, stat, to_pairs(blocks), codes, width)
+    return (temporal, logits)
+
+
+def per_device(*arrays):
+    hidden_in, temporal_qkv, depth_qkv, head_weight = arrays[0], arrays[2], arrays[10], arrays[13]
+    tp = lax.axis_size("tp")
+    pairs = hidden_in.shape[0] * (temporal_qkv.shape[2] // HEAD_DIM)
+    whole_tiles = (
+        pairs % 128 == 0
+        and temporal_qkv.shape[2] % HEAD_DIM == 0
+        and head_weight.shape[1] % 128 == 0
+        and head_weight.shape[2] // tp % 128 == 0
+        and depth_qkv.shape[3] % 128 == 0
+        and tp >= 4
+        and tp & (tp - 1) == 0
+    )
+    return (paired_device if whole_tiles else general_device)(*arrays)
+
+
 def solution(mesh):
     return jax.shard_map(
         per_device,

time: 170 us -> 128 us (0.75)
  matrix products: 27.9 us -> 0 us
  Pallas kernels: 0 us -> 26.7 us
  local copies, waits for them, and re-layouts: 21.8 us -> 6.54 us
  other arithmetic: 16.4 us -> 2.66 us
  blocking collectives: 32.5 us -> 20 us
  starting transfers between devices: 21.6 us -> 26 us
  waiting for transfers between devices: 47.8 us -> 44.8 us
    dot_general x9 -> x0, matrix products: 27.9 us -> none  [the longest x1 7.01 us: per_device(): jnp.einsum('sd,tdf->tsf', normed, temporal_qkv, preferred_element_type=jn...]
    pallas_call x0 -> x8, Pallas kernels: none -> 26.7 us  [the longest x1 14.5 us: temporal_parts(): pl.pallas_call(temporal_kernel, in_specs=[HBM, HBM, VMEM, HBM, HBM, HBM,...]
    ppermute x0 -> x9, waiting for transfers between devices: none -> 20.3 us  [the longest x6 17.5 us: to_pairs(): lax.ppermute(block, 'tp', [(i, i ^ 2 * (k + 1)) for i in range(tp)])]
    ppermute x0 -> x9, starting transfers between devices: none -> 15.5 us  [the longest x6 9.38 us: to_pairs(): lax.ppermute(block, 'tp', [(i, i ^ 2 * (k + 1)) for i in range(tp)])]
    all_to_all x1 -> x0, waiting for transfers between devices: 14.3 us -> none  [gathered(): lax.all_to_all(jnp.broadcast_to(block[None], (size,) + block.shape), 'tp'...]
    all_to_all x1, blocking collectives: 30.6 us -> 18.1 us  [gathered(): lax.all_to_all(jnp.broadcast_to(block[None], (size,) + block.shape), 'tp'...]
    convert_element_type x14 -> x0, local copies, waits for them, and re-layouts: 10.7 us -> none  [the longest x2 3.14 us: per_device(): all_keys[None].astype(jnp.float32)]
    all_to_all x3 -> x2, waiting for transfers between devices: 33.5 us -> 23.5 us  [scattered_sum(): moved = lax.all_to_all(parts.astype(jnp.bfloat16), 'tp', 0, 0)]
  transfers between devices with their start and end apart: 5 -> 12, of which waited for: 4 -> 8; matrix products, arithmetic and copies ran while one was open for 4% -> 1% of each run, Pallas kernels for 0% -> 12%
where the time goes in v2:
time: 128 us; the launch traced here: 127 us
  waiting for transfers between devices  44.8 us (35%)
  Pallas kernels  26.7 us (21%)
  starting transfers between devices  26 us (20%)
  blocking collectives  20 us (16%)
  local copies, waits for them, and re-layouts  6.54 us (5%)
  other arithmetic  2.66 us (2%)
    all_to_all x2, waiting for transfers between devices, scattered_sum(): moved = lax.all_to_all(parts.astype(jnp.bfloat16), 'tp', 0, 0)  23.5 us
    all_to_all x1, blocking collectives, gathered(): lax.all_to_all(jnp.broadcast_to(block[None], (size,) + block.shape), 'tp'...  18.1 us
    ppermute x6, waiting for transfers between devices, to_pairs(): lax.ppermute(block, 'tp', [(i, i ^ 2 * (k + 1)) for i in range(tp)])  17.5 us
    pallas_call x1, Pallas kernels, temporal_parts(): pl.pallas_call(temporal_kernel, in_specs=[HBM, HBM, VMEM, HBM, HBM, HBM,...  14.5 us
    ppermute x6, starting transfers between devices, to_pairs(): lax.ppermute(block, 'tp', [(i, i ^ 2 * (k + 1)) for i in range(tp)])  9.38 us
    all_to_all x2, starting transfers between devices, scattered_sum(): moved = lax.all_to_all(parts.astype(jnp.bfloat16), 'tp', 0, 0)  9.29 us
    ppermute x3, starting transfers between devices, to_neighbour(): return lax.ppermute(block, 'tp', [(i, i ^ 1) for i in range(tp)])  6.08 us
    unnamed x25, local copies, waits for them, and re-layouts  5.59 us
  transfers between devices with their start and end apart: 12, of which 8 were waited for; matrix products, arithmetic and copies ran while one was open for 1% of the time, Pallas kernels for 12%

profile of v2, /device:TPU:0, one launch (start us, length us, event | category | flops | bytes accessed | tf_op | source)
XLA Modules:
  0.0 127.5 jit_solution(12431137946362422259)
XLA Ops:
  1.2 3.0 %partner_columns.1 = (bf16[4,2,128,256]{3,2,1,0:T(8,128)(2,1)}, bf16[4,2,128,256]{3,2,1,0:T(8,128)(2,1)}) custom-call(s32[2]{0:T(128)} %pad_add_fusion.place_ref, bf16[4,128,2048]{2,1,0:T(8,128)(2,1)} %own_hbm.1), custom_call_target="tpu_custom_call" | custom-call | tf_op jit(solution)/shard_map/partner_columns/pallas_call | solution.py:577
  4.3 3.0 %collective-permute-start = (bf16[4,2,128,256]{3,2,1,0:T(8,128)(2,1)}, bf16[4,2,128,256]{3,2,1,0:T(8,128)(2,1)S(1)}, u32[]{:S(2)}, u32[]{:S(2)}) collective-permute-start(bf16[4,2,128,256]{3,2,1,0:T(8,128)(2,1)} %get-tuple-element.21), channel_id=1, source_target_pairs={{0,2},{2,0},{4,6},{6,4},{8,10},{10,8},{12,14},{14,12},{1,3},{3,1},... | collective-permute-start | bytes 1572872 | tf_op jit(solution)/shard_map/ppermute | solution.py:710
  8.0 14.5 %temporal.1 = bf16[8,32,512]{2,1,0:T(8,128)(2,1)} custom-call(bf16[32,4096]{1,0:T(8,128)(2,1)} %hidden_hbm.1, f32[1,4096]{1,0:T(1,128)} %bitcast.9, s32[1,32]{1,0:T(1,128)S(1)} %bitcast.8, bf16[3,4096,512]{2,1,0:T(8,128)(2,1)} %qkv_hbm.1, bf16[512,4096]{1,0:T(8,128)(2,1)} %out_hbm.1, bf16[32,64,512]{2,1,0:T(8,128)(2,1)} %keys_hbm.1, ...), custom_call_target="tpu_custom_call" | custom-call | tf_op jit(solution)/shard_map/temporal/pallas_call | solution.py:356
  23.3 4.9 %all-to-all-start = ((bf16[8,32,512]{2,1,0:T(8,128)(2,1)}), bf16[8,32,512]{2,1,0:T(8,128)(2,1)S(1)}, u32[]{:S(2)}, u32[]{:S(2)}) async-start(bf16[8,32,512]{2,1,0:T(8,128)(2,1)} %temporal.1), calls=%async_computation | async-start | bytes 524288 | tf_op jit(solution)/shard_map/all_to_all | solution.py:48
  28.3 8.5 %all-to-all-done = bf16[8,32,512]{2,1,0:T(8,128)(2,1)S(1)} async-done(((bf16[8,32,512]{2,1,0:T(8,128)(2,1)}), bf16[8,32,512]{2,1,0:T(8,128)(2,1)S(1)}, u32[]{:S(2)}, u32[]{:S(2)}) %all-to-all-start) | async-done | bytes 262176 | tf_op jit(solution)/shard_map/all_to_all | solution.py:48
  37.6 1.9 %all_gather.3.rows_ref = bf16[64,512]{1,0:T(8,128)(2,1)S(1)} all-gather(bf16[32,512]{1,0:T(8,128)(2,1)S(1)} %add_convert_fusion), channel_id=1, replica_groups=mesh['grp'=2,'tp'=8,'section'=2] {'section'}, dimensions={0}, use_global_device_ids=true | all-gather | bytes 98304 | tf_op jit(solution)/shard_map/all_gather | solution.py:722
  39.5 2.2 %copy-done = bf16[4,512,1024]{2,1,0:T(8,128)(2,1)S(1)} copy-done((bf16[4,512,1024]{2,1,0:T(8,128)(2,1)S(1)}, bf16[4,512,1024]{2,1,0:T(8,128)(2,1)}, u32[]{:S(2)}) %copy-start) | copy-done | bytes 4194328
  41.7 2.3 %entry.1 = bf16[8,4,64,128]{3,2,1,0:T(8,128)(2,1)S(1)} custom-call(bf16[64,512]{1,0:T(8,128)(2,1)S(1)} %all_gather.3.rows_ref, s32[64,4]{1,0:T(8,128)S(1)} %broadcast_subtract_fusion.tokens_ref, bf16[4,512,1024]{2,1,0:T(8,128)(2,1)S(1)} %copy-done, bf16[4,256,1024]{2,1,0:T(8,128)(2,1)S(1)} %copy-done.2), custom_call_target="tpu_custom_call" | custom-call | tf_op jit(solution)/shard_map/entry/pallas_call | solution.py:412
  44.8 4.4 %all-to-all-start.1 = ((bf16[8,4,64,128]{3,2,1,0:T(8,128)(2,1)}), bf16[8,4,64,128]{3,2,1,0:T(8,128)(2,1)}, u32[]{:S(2)}, u32[]{:S(2)}) async-start(bf16[8,4,64,128]{3,2,1,0:T(8,128)(2,1)} %copy-done.3), calls=%async_computation.1 | async-start | bytes 1048576 | tf_op jit(solution)/shard_map/all_to_all | solution.py:48
  49.3 15.0 %all-to-all-done.1 = bf16[8,4,64,128]{3,2,1,0:T(8,128)(2,1)} async-done(((bf16[8,4,64,128]{3,2,1,0:T(8,128)(2,1)}), bf16[8,4,64,128]{3,2,1,0:T(8,128)(2,1)}, u32[]{:S(2)}, u32[]{:S(2)}) %all-to-all-start.1) | async-done | bytes 524320 | tf_op jit(solution)/shard_map/all_to_all | solution.py:48
  65.6 18.1 %all_to_all.15.rows_ref = bf16[8,4,64,128]{3,2,1,0:T(8,128)(2,1)S(1)} all-to-all(bf16[8,4,64,128]{3,2,1,0:T(8,128)(2,1)S(1)} %broadcast_in_dim.2), channel_id=1, replica_groups=mesh['grp'=2,'tp'=8,'section'=2] {'tp'}, dimensions={0} | all-to-all | bytes 1048576 | tf_op jit(solution)/shard_map/all_to_all | solution.py:54
  87.4 1.5 %depth_mix.1 = (f32[4,64,256]{2,1,0:T(8,128)S(1)}, bf16[4,64,256]{2,1,0:T(8,128)(2,1)S(1)}, bf16[4,64,256]{2,1,0:T(8,128)(2,1)S(1)}, bf16[4,64,256]{2,1,0:T(8,128)(2,1)S(1)}) custom-call(s32[2]{0:T(128)S(1)} %copy-done.7, bf16[4,64,128]{2,1,0:T(8,128)(2,1)S(1)} %get-tuple-element.24.queries_ref, bf16[2,4,64,128]{3,2,1,0:T(8,128)(2,1)S(1)} %get-tuple-element.25.own_ref, ...), custom_call_target="tpu_custom_call" | custom-call | tf_op jit(solution)/shard_map/depth_mix/pallas_call | solution.py:516
  89.0 1.5 %collective-permute-start.6 = (bf16[4,2,128,256]{3,2,1,0:T(8,128)(2,1)}, bf16[4,2,128,256]{3,2,1,0:T(8,128)(2,1)S(1)}, u32[]{:S(2)}, u32[]{:S(2)}) collective-permute-start(bf16[4,2,128,256]{3,2,1,0:T(8,128)(2,1)} %get-tuple-element.34), channel_id=1, source_target_pairs={{0,2},{2,0},{4,6},{6,4},{8,10},{10,8},{12,14},{14,12},{1,3},{3,1},... | collective-permute-start | bytes 1572872 | tf_op jit(solution)/shard_map/ppermute | solution.py:710
  90.5 2.1 %collective-permute-start.3 = (bf16[4,64,256]{2,1,0:T(8,128)(2,1)S(1)}, bf16[4,64,256]{2,1,0:T(8,128)(2,1)S(1)}, u32[]{:S(2)}, u32[]{:S(2)}) collective-permute-start(bf16[4,64,256]{2,1,0:T(8,128)(2,1)S(1)} %get-tuple-element.29), channel_id=1, source_target_pairs={{0,8},{2,10},{4,12},{6,14},{8,0},{10,2},{12,4},{14,6},{1,9},{3,11}... | collective-permute-start | bytes 393224 | tf_op jit(solution)/shard_map/ppermute | solution.py:705
  92.6 2.3 %collective-permute-start.4 = (bf16[4,64,256]{2,1,0:T(8,128)(2,1)S(1)}, bf16[4,64,256]{2,1,0:T(8,128)(2,1)S(1)}, u32[]{:S(2)}, u32[]{:S(2)}) collective-permute-start(bf16[4,64,256]{2,1,0:T(8,128)(2,1)S(1)} %get-tuple-element.30), channel_id=1, source_target_pairs={{0,12},{2,14},{4,8},{6,10},{8,4},{10,6},{12,0},{14,2},{1,13},{3,15... | collective-permute-start | bytes 393224 | tf_op jit(solution)/shard_map/ppermute | solution.py:705
  94.9 2.9 %collective-permute-done.2.rest_0_ = bf16[4,64,256]{2,1,0:T(8,128)(2,1)S(1)} collective-permute-done((bf16[4,64,256]{2,1,0:T(8,128)(2,1)S(1)}, bf16[4,64,256]{2,1,0:T(8,128)(2,1)S(1)}, u32[]{:S(2)}, u32[]{:S(2)}) %collective-permute-start.2) | collective-permute-done | bytes 131104 | tf_op jit(solution)/shard_map/ppermute | solution.py:705
  97.8 5.7 %collective-permute-done.3.rest_1_ = bf16[4,64,256]{2,1,0:T(8,128)(2,1)S(1)} collective-permute-done((bf16[4,64,256]{2,1,0:T(8,128)(2,1)S(1)}, bf16[4,64,256]{2,1,0:T(8,128)(2,1)S(1)}, u32[]{:S(2)}, u32[]{:S(2)}) %collective-permute-start.3) | collective-permute-done | bytes 131104 | tf_op jit(solution)/shard_map/ppermute | solution.py:705
  104.1 1.5 %collective-permute-start.5 = (bf16[4,64,256]{2,1,0:T(8,128)(2,1)S(1)}, bf16[4,64,256]{2,1,0:T(8,128)(2,1)S(1)}, u32[]{:S(2)}, u32[]{:S(2)}) collective-permute-start(bf16[4,64,256]{2,1,0:T(8,128)(2,1)S(1)} %get-tuple-element.32), channel_id=1, source_target_pairs={{0,2},{2,0},{4,6},{6,4},{8,10},{10,8},{12,14},{14,12},{1,3},{3,1},... | collective-permute-start | bytes 393224 | tf_op jit(solution)/shard_map/ppermute | solution.py:710
  106.3 2.8 %collective-permute-done.5.arrived_ref = bf16[4,64,256]{2,1,0:T(8,128)(2,1)S(1)} collective-permute-done((bf16[4,64,256]{2,1,0:T(8,128)(2,1)S(1)}, bf16[4,64,256]{2,1,0:T(8,128)(2,1)S(1)}, u32[]{:S(2)}, u32[]{:S(2)}) %collective-permute-start.5) | collective-permute-done | bytes 131104 | tf_op jit(solution)/shard_map/ppermute | solution.py:710
  110.2 2.5 %head.1 = (f32[256,256]{1,0:T(8,128)S(1)}, f32[1,256]{1,0:T(1,128)S(1)}, bf16[272,256]{1,0:T(8,128)(2,1)S(1)}, bf16[272,256]{1,0:T(8,128)(2,1)S(1)}, bf16[272,256]{1,0:T(8,128)(2,1)S(1)}) custom-call(s32[2]{0:T(128)S(1)} %copy-done.7, f32[1,1,256]{2,1,0:T(1,128)S(1)} %bitcast.6, f32[4,64,256]{2,1,0:T(8,128)S(1)} %get-tuple-element.31.total_ref, ...), custom_call_target="tpu_custom_call" | custom-call | tf_op jit(solution)/shard_map/head/pallas_call | solution.py:639
  112.6 2.6 %collective-permute-start.7 = (bf16[272,256]{1,0:T(8,128)(2,1)S(1)}, bf16[272,256]{1,0:T(8,128)(2,1)S(1)}, u32[]{:S(2)}, u32[]{:S(2)}) collective-permute-start(bf16[272,256]{1,0:T(8,128)(2,1)S(1)} %get-tuple-element.37), channel_id=1, source_target_pairs={{0,4},{2,6},{4,0},{6,2},{8,12},{10,14},{12,8},{14,10},{1,5},{3,7},... | collective-permute-start | bytes 417800 | tf_op jit(solution)/shard_map/ppermute | solution.py:705
  115.3 2.3 %collective-permute-start.9 = (bf16[272,256]{1,0:T(8,128)(2,1)S(1)}, bf16[272,256]{1,0:T(8,128)(2,1)S(1)}, u32[]{:S(2)}, u32[]{:S(2)}) collective-permute-start(bf16[272,256]{1,0:T(8,128)(2,1)S(1)} %get-tuple-element.39), channel_id=1, source_target_pairs={{0,12},{2,14},{4,8},{6,10},{8,4},{10,6},{12,0},{14,2},{1,13},{3,15... | collective-permute-start | bytes 417800 | tf_op jit(solution)/shard_map/ppermute | solution.py:705
  117.6 1.7 %collective-permute-done.7.rest_0_ = bf16[272,256]{1,0:T(8,128)(2,1)S(1)} collective-permute-done((bf16[272,256]{1,0:T(8,128)(2,1)S(1)}, bf16[272,256]{1,0:T(8,128)(2,1)S(1)}, u32[]{:S(2)}, u32[]{:S(2)}) %collective-permute-start.7) | collective-permute-done | bytes 139296 | tf_op jit(solution)/shard_map/ppermute | solution.py:705
  119.3 7.3 %collective-permute-done.8.rest_1_ = bf16[272,256]{1,0:T(8,128)(2,1)S(1)} collective-permute-done((bf16[272,256]{1,0:T(8,128)(2,1)S(1)}, bf16[272,256]{1,0:T(8,128)(2,1)S(1)}, u32[]{:S(2)}, u32[]{:S(2)}) %collective-permute-start.8) | collective-permute-done | bytes 139296 | tf_op jit(solution)/shard_map/ppermute | solution.py:705
  (44 shorter events, 12.4 us)
Async XLA Ops:
  4.3 18.2 %collective-permute-start = (bf16[4,2,128,256]{3,2,1,0:T(8,128)(2,1)}, bf16[4,2,128,256]{3,2,1,0:T(8,128)(2,1)S(1)}, u32[]{:S(2)}, u32[]{:S(2)}) collective-permute-start(bf16[4,2,128,256]{3,2,1,0:T(8,128)(2,1)} %get-tuple-element.21), channel_id=1, source_target_pairs={{0,2},{2,0},{4,6},{6,4},{8,10},{10,8},{12,14},{14,12},{1,3},{3,1},... | collective-permute-start | bytes 1572872 | tf_op jit(solution)/shard_map/ppermute | solution.py:710
  7.3 0.7 copy-start.9
  8.0 20.2 %copy-start.11 = (s32[64,4]{0,1:T(4,128)S(1)}, s32[64,4]{0,1:T(4,128)}, u32[]{:S(2)}) copy-start(s32[64,4]{0,1:T(4,128)} %param.29) | copy-start | bytes 3076
  8.0 31.5 %copy-start.2 = (bf16[4,256,1024]{2,1,0:T(8,128)(2,1)S(1)}, bf16[4,256,1024]{2,1,0:T(8,128)(2,1)}, u32[]{:S(2)}) copy-start(bf16[4,256,1024]{2,1,0:T(8,128)(2,1)} %embed_hbm.1) | copy-start | bytes 6291460
  22.5 0.8 copy-start.5
  23.3 13.5 %all-to-all-start = ((bf16[8,32,512]{2,1,0:T(8,128)(2,1)}), bf16[8,32,512]{2,1,0:T(8,128)(2,1)S(1)}, u32[]{:S(2)}, u32[]{:S(2)}) async-start(bf16[8,32,512]{2,1,0:T(8,128)(2,1)} %temporal.1), calls=%async_computation | async-start | bytes 524288 | tf_op jit(solution)/shard_map/all_to_all | solution.py:48
  37.6 6.3 %copy-start.10 = (bf16[32,512]{1,0:T(8,128)(2,1)}, bf16[32,512]{1,0:T(8,128)(2,1)S(1)}, u32[]{:S(2)}) copy-start(bf16[32,512]{1,0:T(8,128)(2,1)S(1)} %add_convert_fusion) | copy-start | bytes 98308
  39.5 2.2 %copy-start = (bf16[4,512,1024]{2,1,0:T(8,128)(2,1)S(1)}, bf16[4,512,1024]{2,1,0:T(8,128)(2,1)}, u32[]{:S(2)}) copy-start(bf16[4,512,1024]{2,1,0:T(8,128)(2,1)} %weight_hbm.5) | copy-start | bytes 12582916
  41.7 7.5 %copy-start.8 = (f32[1024]{0:T(1024)S(1)}, f32[1024]{0:T(1024)}, u32[]{:S(2)}) copy-start(f32[1024]{0:T(1024)} %param.24) | copy-start | bytes 12292
  44.0 0.8 copy-start.3
  44.8 39.0 %copy-start.1 = (bf16[4,3,1024,128]{3,2,1,0:T(8,128)(2,1)S(1)}, bf16[4,3,1024,128]{3,2,1,0:T(8,128)(2,1)}, u32[]{:S(2)}) copy-start(bf16[4,3,1024,128]{3,2,1,0:T(8,128)(2,1)} %weight_hbm.6) | copy-start | bytes 9437188
  44.8 19.5 %all-to-all-start.1 = ((bf16[8,4,64,128]{3,2,1,0:T(8,128)(2,1)}), bf16[8,4,64,128]{3,2,1,0:T(8,128)(2,1)}, u32[]{:S(2)}, u32[]{:S(2)}) async-start(bf16[8,4,64,128]{3,2,1,0:T(8,128)(2,1)} %copy-done.3), calls=%async_computation.1 | async-start | bytes 1048576 | tf_op jit(solution)/shard_map/all_to_all | solution.py:48
  49.2 38.3 %copy-start.7 = (s32[2]{0:T(128)S(1)}, s32[2]{0:T(128)}, u32[]{:S(2)}) copy-start(s32[2]{0:T(128)} %pad_add_fusion.place_ref) | copy-start | bytes 28
  64.3 23.2 %copy-start.4 = (bf16[4,128,1024]{2,1,0:T(8,128)(2,1)S(1)}, bf16[4,128,1024]{2,1,0:T(8,128)(2,1)}, u32[]{:S(2)}) copy-start(bf16[4,128,1024]{2,1,0:T(8,128)(2,1)} %weight_hbm.7) | copy-start | bytes 3145732
  85.2 2.3 %collective-permute-start.1 = (bf16[2,4,64,128]{3,2,1,0:T(8,128)(2,1)S(1)}, bf16[2,4,64,128]{3,2,1,0:T(8,128)(2,1)S(1)}, u32[]{:S(2)}, u32[]{:S(2)}) collective-permute-start(bf16[2,4,64,128]{3,2,1,0:T(8,128)(2,1)S(1)} %get-tuple-element.25.own_ref), channel_id=1, source_target_pairs={{0,1},{2,3},{4,5},{6,7},{8,9},{10,11},{12,13},{14,15},{16,17},{18,... | collective-permute-start | bytes 393224 | tf_op jit(solution)/shard_map/ppermute | solution.py:21
  89.0 20.1 %collective-permute-start.6 = (bf16[4,2,128,256]{3,2,1,0:T(8,128)(2,1)}, bf16[4,2,128,256]{3,2,1,0:T(8,128)(2,1)S(1)}, u32[]{:S(2)}, u32[]{:S(2)}) collective-permute-start(bf16[4,2,128,256]{3,2,1,0:T(8,128)(2,1)} %get-tuple-element.34), channel_id=1, source_target_pairs={{0,2},{2,0},{4,6},{6,4},{8,10},{10,8},{12,14},{14,12},{1,3},{3,1},... | collective-permute-start | bytes 1572872 | tf_op jit(solution)/shard_map/ppermute | solution.py:710
  90.5 7.3 %collective-permute-start.2 = (bf16[4,64,256]{2,1,0:T(8,128)(2,1)S(1)}, bf16[4,64,256]{2,1,0:T(8,128)(2,1)S(1)}, u32[]{:S(2)}, u32[]{:S(2)}) collective-permute-start(bf16[4,64,256]{2,1,0:T(8,128)(2,1)S(1)} %get-tuple-element.28), channel_id=1, source_target_pairs={{0,4},{2,6},{4,0},{6,2},{8,12},{10,14},{12,8},{14,10},{1,5},{3,7},... | collective-permute-start | bytes 393224 | tf_op jit(solution)/shard_map/ppermute | solution.py:705
  90.5 12.9 %collective-permute-start.3 = (bf16[4,64,256]{2,1,0:T(8,128)(2,1)S(1)}, bf16[4,64,256]{2,1,0:T(8,128)(2,1)S(1)}, u32[]{:S(2)}, u32[]{:S(2)}) collective-permute-start(bf16[4,64,256]{2,1,0:T(8,128)(2,1)S(1)} %get-tuple-element.29), channel_id=1, source_target_pairs={{0,8},{2,10},{4,12},{6,14},{8,0},{10,2},{12,4},{14,6},{1,9},{3,11}... | collective-permute-start | bytes 393224 | tf_op jit(solution)/shard_map/ppermute | solution.py:705
  92.6 10.8 %collective-permute-start.4 = (bf16[4,64,256]{2,1,0:T(8,128)(2,1)S(1)}, bf16[4,64,256]{2,1,0:T(8,128)(2,1)S(1)}, u32[]{:S(2)}, u32[]{:S(2)}) collective-permute-start(bf16[4,64,256]{2,1,0:T(8,128)(2,1)S(1)} %get-tuple-element.30), channel_id=1, source_target_pairs={{0,12},{2,14},{4,8},{6,10},{8,4},{10,6},{12,0},{14,2},{1,13},{3,15... | collective-permute-start | bytes 393224 | tf_op jit(solution)/shard_map/ppermute | solution.py:705
  104.1 5.0 %collective-permute-start.5 = (bf16[4,64,256]{2,1,0:T(8,128)(2,1)S(1)}, bf16[4,64,256]{2,1,0:T(8,128)(2,1)S(1)}, u32[]{:S(2)}, u32[]{:S(2)}) collective-permute-start(bf16[4,64,256]{2,1,0:T(8,128)(2,1)S(1)} %get-tuple-element.32), channel_id=1, source_target_pairs={{0,2},{2,0},{4,6},{6,4},{8,10},{10,8},{12,14},{14,12},{1,3},{3,1},... | collective-permute-start | bytes 393224 | tf_op jit(solution)/shard_map/ppermute | solution.py:710
  109.1 1.0 copy-start.6
  112.6 6.7 %collective-permute-start.7 = (bf16[272,256]{1,0:T(8,128)(2,1)S(1)}, bf16[272,256]{1,0:T(8,128)(2,1)S(1)}, u32[]{:S(2)}, u32[]{:S(2)}) collective-permute-start(bf16[272,256]{1,0:T(8,128)(2,1)S(1)} %get-tuple-element.37), channel_id=1, source_target_pairs={{0,4},{2,6},{4,0},{6,2},{8,12},{10,14},{12,8},{14,10},{1,5},{3,7},... | collective-permute-start | bytes 417800 | tf_op jit(solution)/shard_map/ppermute | solution.py:705
  115.2 11.4 %collective-permute-start.8 = (bf16[272,256]{1,0:T(8,128)(2,1)S(1)}, bf16[272,256]{1,0:T(8,128)(2,1)S(1)}, u32[]{:S(2)}, u32[]{:S(2)}) collective-permute-start(bf16[272,256]{1,0:T(8,128)(2,1)S(1)} %get-tuple-element.38), channel_id=1, source_target_pairs={{0,8},{2,10},{4,12},{6,14},{8,0},{10,2},{12,4},{14,6},{1,9},{3,11}... | collective-permute-start | bytes 417800 | tf_op jit(solution)/shard_map/ppermute | solution.py:705
  115.3 11.2 %collective-permute-start.9 = (bf16[272,256]{1,0:T(8,128)(2,1)S(1)}, bf16[272,256]{1,0:T(8,128)(2,1)S(1)}, u32[]{:S(2)}, u32[]{:S(2)}) collective-permute-start(bf16[272,256]{1,0:T(8,128)(2,1)S(1)} %get-tuple-element.39), channel_id=1, source_target_pairs={{0,12},{2,14},{4,8},{6,10},{8,4},{10,6},{12,0},{14,2},{1,13},{3,15... | collective-permute-start | bytes 417800 | tf_op jit(solution)/shard_map/ppermute | solution.py:705

commit v3 on v2

--- a/solution.py
+++ b/solution.py
@@ -211,6 +211,10 @@
     return jax.ShapeDtypeStruct(dims, dtype)
 
 
+def vmem(dims, dtype):
+    return pltpu.VMEM(dims, dtype)
+
+
 def product(left, right):
     return jnp.dot(left, right, preferred_element_type=jnp.float32)
 
@@ -226,45 +230,59 @@
     return jnp.sum(jnp.where(first == second, row, 0.0), axis=1, keepdims=True)
 
 
+IN_FLIGHT = 6
+
+
+class Stream:
+    def __init__(self, copies):
+        self.copies = copies
+        self.done = 0
+        for copy in copies[:IN_FLIGHT]:
+            copy.start()
+
+    def arrived(self, upto):
+        while self.done <= upto:
+            self.copies[self.done].wait()
+            if self.done + IN_FLIGHT < len(self.copies):
+                self.copies[self.done + IN_FLIGHT].start()
+            self.done += 1
+
+
 def temporal_kernel(
-    hidden_hbm, gain_hbm, lengths_ref, qkv_hbm, out_hbm, keys_hbm, values_hbm, parts_ref,
-    hidden_buf, gain_buf, qkv_buf, out_buf, keys_buf, values_buf, small_sems, qkv_sems, out_sems, cache_sems,
+    place_ref, hidden_hbm, gain_hbm, lengths_hbm, qkv_hbm, out_hbm, keys_hbm, values_hbm, kept_ref, sent_ref,
+    hidden_buf, gain_buf, lengths_buf, qkv_buf, out_buf, keys_buf, values_buf, small_sems, sems,
 ):
     streams, depth = hidden_buf.shape
     cols = qkv_buf.shape[2]
     heads = cols // HEAD_DIM
     cache_len = keys_buf.shape[1]
-    steps = qkv_sems.shape[1]
+    steps, halves = QKV_STEPS, CACHE_STEPS
     chunk = depth // steps
-    places = parts_ref.shape[0]
-    width = parts_ref.shape[2]
+    batch = streams // halves
+    count, _, width = kept_ref.shape
+    odd = place_ref[0] % 2
+    place = place_ref[0] // 2
     small = [
         pltpu.make_async_copy(hidden_hbm, hidden_buf, small_sems.at[0]),
         pltpu.make_async_copy(gain_hbm, gain_buf, small_sems.at[1]),
+        pltpu.make_async_copy(lengths_hbm, lengths_buf, small_sems.at[2]),
     ]
-    weight = [
-        [
-            pltpu.make_async_copy(
-                qkv_hbm.at[n, pl.ds(i * chunk, chunk)],
-                qkv_buf.at[n, pl.ds(i * chunk, chunk)],
-                qkv_sems.at[n, i],
-            )
-            for i in range(steps)
-        ]
-        for n in range(3)
+    for copy in small:
+        copy.start()
+    pairs = []
+    for n in (0, 1):
+        pairs += [(qkv_hbm.at[n, pl.ds(i * chunk, chunk)], qkv_buf.at[n, pl.ds(i * chunk, chunk)]) for i in range(steps)]
+    pairs += [(keys_hbm.at[pl.ds(i * batch, batch)], keys_buf.at[pl.ds(i * batch, batch)]) for i in range(halves)]
+    pairs += [(qkv_hbm.at[2, pl.ds(i * chunk, chunk)], qkv_buf.at[2, pl.ds(i * chunk, chunk)]) for i in range(steps)]
+    pairs += [(values_hbm.at[pl.ds(i * batch, batch)], values_buf.at[pl.ds(i * batch, batch)]) for i in range(halves)]
+    pairs += [
+        (out_hbm.at[:, pl.ds(pl.multiple_of((place ^ k) * 2 * width, 2 * width), 2 * width)], out_buf.at[k])
+        for k in range(count)
     ]
-    caches = [
-        pltpu.make_async_copy(keys_hbm, keys_buf, cache_sems.at[0]),
-        pltpu.make_async_copy(values_hbm, values_buf, cache_sems.at[1]),
-    ]
-    outs = [
-        pltpu.make_async_copy(
-            out_hbm.at[:, pl.ds(t * width, width)], out_buf.at[:, pl.ds(t * width, width)], out_sems.at[t]
-        )
-        for t in range(places)
-    ]
-    for copy in small + weight[0] + weight[1] + caches[:1] + weight[2] + caches[1:] + outs:
-        copy.start()
+    stream = Stream([pltpu.make_async_copy(src, dst, sems.at[i]) for i, (src, dst) in enumerate(pairs)])
+    first_of = (0, steps, 2 * steps + halves)
+    keys_end = 2 * steps + halves - 1
+    values_end = 3 * steps + 2 * halves - 1
 
     for copy in small:
         copy.wait()
@@ -275,12 +293,12 @@
     def projected(n):
         total = None
         for i in range(steps):
-            weight[n][i].wait()
+            stream.arrived(first_of[n] + i)
             part = product(normed[:, i * chunk : (i + 1) * chunk], qkv_buf[n, pl.ds(i * chunk, chunk), :])
             total = part if total is None else total + part
         return total
 
-    lengths_row = lengths_ref[...].astype(jnp.float32)
+    lengths_row = lengths_buf[...].astype(jnp.float32)
     lengths_col = column_of(lengths_row)
     half = HEAD_DIM // 2
     lane = lax.broadcasted_iota(jnp.int32, (streams, HEAD_DIM), 1)
@@ -312,7 +330,7 @@
     tiled = jnp.sum(jnp.where(stream_row == pair_stream, lengths_col, 0.0), axis=0, keepdims=True)
     first_row = pair_stream * cache_len
     last_row = first_row + tiled.astype(jnp.int32)
-    caches[0].wait()
+    stream.arrived(keys_end)
     rows = streams * cache_len
     scores = product_t(keys_buf[...].reshape(rows, cols), spread) * factor
     row = lax.broadcasted_iota(jnp.int32, (rows, pairs), 0)
@@ -324,7 +342,7 @@
     weights = (expo * inverse).astype(jnp.bfloat16)
     own_weight = (own_expo * inverse).astype(jnp.bfloat16).astype(jnp.float32)
     values_new = projected(2).astype(jnp.bfloat16).astype(jnp.float32)
-    caches[1].wait()
+    stream.arrived(values_end)
     mixed_all = lax.dot_general(
         weights,
         values_buf[...].reshape(rows, cols),
@@ -343,39 +361,46 @@
             mixed_all[h * streams : (h + 1) * streams, lanes] + own_col * values_new[:, lanes]
         )
     mixed = jnp.concatenate(mixed, axis=1).astype(jnp.bfloat16)
-    for t in range(places):
-        outs[t].wait()
-        parts_ref[t] = product(mixed, out_buf[:, pl.ds(t * width, width)]).astype(jnp.bfloat16)
-
-
-def temporal_parts(hidden_in, gain, lengths, qkv, out_weight, keys, values, places):
+    for k in range(count):
+        stream.arrived(values_end + 1 + k)
+        block = product(mixed, out_buf[k])
+        even_side, odd_side = block[:, :width], block[:, width:]
+        kept_ref[k] = jnp.where(odd == 1, odd_side, even_side)
+        sent_ref[k] = jnp.where(odd == 1, even_side, odd_side).astype(jnp.bfloat16)
+
+
+QKV_STEPS = 4
+CACHE_STEPS = 2
+
+
+def temporal_parts(place, hidden_in, gain, lengths, qkv, out_weight, keys, values, places):
     streams, depth = hidden_in.shape
-    cols = qkv.shape[2]
-    steps = 4
     bf16 = jnp.bfloat16
+    count, width = places // 2, out_weight.shape[1] // places
+    block = (count, streams, width)
     return pl.pallas_call(
         temporal_kernel,
-        in_specs=[HBM, HBM, VMEM, HBM, HBM, HBM, HBM],
-        out_specs=VMEM,
-        out_shape=shape((places, streams, out_weight.shape[1] // places), bf16),
+        in_specs=[SMEM] + [HBM] * 7,
+        out_specs=[VMEM, VMEM],
+        out_shape=[vmem(block, jnp.float32), vmem(block, bf16)],
         scratch_shapes=[
             pltpu.VMEM(hidden_in.shape, bf16),
             pltpu.VMEM((1, depth), jnp.float32),
+            pltpu.VMEM((1, streams), jnp.int32),
             pltpu.VMEM(qkv.shape, bf16),
-            pltpu.VMEM(out_weight.shape, bf16),
+            pltpu.VMEM((count, out_weight.shape[0], 2 * width), bf16),
             pltpu.VMEM(keys.shape, bf16),
             pltpu.VMEM(values.shape, bf16),
-            pltpu.SemaphoreType.DMA((2,)),
-            pltpu.SemaphoreType.DMA((3, steps)),
-            pltpu.SemaphoreType.DMA((places,)),
-            pltpu.SemaphoreType.DMA((2,)),
+            pltpu.SemaphoreType.DMA((3,)),
+            pltpu.SemaphoreType.DMA((3 * QKV_STEPS + 2 * CACHE_STEPS + count,)),
         ],
         compiler_params=params(30),
         name="temporal",
     )(
+        place,
         in_hbm(hidden_in),
         in_hbm(gain.reshape(1, depth)),
-        lengths.reshape(1, streams),
+        in_hbm(lengths.reshape(1, streams)),
         in_hbm(qkv),
         in_hbm(out_weight),
         in_hbm(keys),
@@ -383,88 +408,183 @@
     )
 
 
-def entry_kernel(rows_ref, tokens_ref, weight_hbm, embed_hbm, parts_ref, weight_buf, embed_buf, sems):
-    codes, depth, width = weight_buf.shape
-    vocab = embed_buf.shape[1]
-    places = parts_ref.shape[0]
-    part = width // places
-    streams = rows_ref.shape[0]
-    weight = [pltpu.make_async_copy(weight_hbm.at[c], weight_buf.at[c], sems.at[0, c]) for c in range(codes)]
-    embed = [pltpu.make_async_copy(embed_hbm.at[c], embed_buf.at[c], sems.at[1, c]) for c in range(codes)]
-    for c in range(codes):
-        embed[c].start()
-        weight[c].start()
-    vocab_lane = lax.broadcasted_iota(jnp.int32, (streams, vocab), 1)
+def prepare_kernel(
+    place_ref, tokens_ref, hidden_hbm, embed_hbm, weight_hbm, resid_ref, embedded_ref, weight_ref, embed_buf, sem, sems
+):
+    codes, vocab, _ = embed_buf.shape
+    streams = tokens_ref.shape[0]
+    part = resid_ref.shape[1]
+    start = pl.multiple_of(place_ref[0] * part, part)
+    resid = pltpu.make_async_copy(hidden_hbm.at[:, pl.ds(start, part)], resid_ref, sem)
+    resid.start()
+    embed = [pltpu.make_async_copy(embed_hbm.at[c], embed_buf.at[c], sems.at[0, c]) for c in range(codes)]
+    weight = [pltpu.make_async_copy(weight_hbm.at[c], weight_ref.at[c], sems.at[1, c]) for c in range(codes)]
+    for copy in embed + weight:
+        copy.start()
+    vocab_lane = lax.broadcasted_iota(jnp.int32, (streams, vocab), 1) + place_ref[0] * vocab
     for c in range(codes):
         hit = tokens_ref[:, c : c + 1] == vocab_lane
         onehot = jnp.where(hit, 1.0, 0.0).astype(jnp.bfloat16)
         embed[c].wait()
-        total = product(onehot, embed_buf[c])
-        weight[c].wait()
-        total = (total + product(rows_ref[...], weight_buf[c])).astype(jnp.bfloat16)
-        for t in range(places):
-            parts_ref[t, c] = total[:, t * part : (t + 1) * part]
-
-
-def entry_parts(rows, local_tokens, weight, embed, places):
-    codes, depth, width = weight.shape
-    streams = rows.shape[0]
+        embedded_ref[c] = product(onehot, embed_buf[c])
+    for copy in weight:
+        copy.wait()
+    resid.wait()
+
+
+def prepared_entry(place, tokens, hidden_in, embed, weight, places):
+    codes, _, width = weight.shape
+    streams = tokens.shape[0]
+    resid_shape = (hidden_in.shape[0], hidden_in.shape[1] // places)
+    return pl.pallas_call(
+        prepare_kernel,
+        in_specs=[SMEM, VMEM, HBM, HBM, HBM],
+        out_specs=[VMEM] * 3,
+        out_shape=[
+            vmem(resid_shape, jnp.bfloat16),
+            vmem((codes, streams, width), jnp.float32),
+            vmem(weight.shape, jnp.bfloat16),
+        ],
+        scratch_shapes=[
+            pltpu.VMEM(embed.shape, jnp.bfloat16),
+            pltpu.SemaphoreType.DMA(()),
+            pltpu.SemaphoreType.DMA((2, codes)),
+        ],
+        compiler_params=params(16),
+        name="entry_prepare",
+    )(place, tokens, in_hbm(hidden_in), in_hbm(embed), in_hbm(weight))
+
+
+def near_kernel(
+    place_ref, gain_ref, qkv_hbm, out_hbm, head_hbm, own_ref, qkv_ref, out_ref, near_cols_ref, far_cols_ref, sems, col_sems
+):
+    copies = [
+        pltpu.make_async_copy(source.at[c], target.at[c], sems.at[i, c])
+        for i, (source, target) in enumerate(((qkv_hbm, qkv_ref), (out_hbm, out_ref)))
+        for c in range(source.shape[0])
+    ]
+    count, _, _, vocab_part = near_cols_ref.shape
+    odd = place_ref[0] % 2
+    place = place_ref[0] // 2
+    for n, (half, side) in enumerate(((far_cols_ref, 1 - odd), (near_cols_ref, odd))):
+        for k in range(count):
+            start = pl.multiple_of(((place ^ k) * 2 + side) * vocab_part, vocab_part)
+            copies.append(
+                pltpu.make_async_copy(head_hbm.at[:, :, pl.ds(start, vocab_part)], half.at[k], col_sems.at[n, k])
+            )
+    for copy in copies:
+        copy.start()
+    part = own_ref.shape[1]
+    own_ref[...] = gain_ref[:, pl.ds(pl.multiple_of(place_ref[0] * part, part), part)]
+    for copy in copies:
+        copy.wait()
+
+
+def brought_near(place, gain, qkv, out_weight, head_weight, places):
+    width = gain.shape[0]
+    codes, depth, vocab = head_weight.shape
+    half = vmem((places // 2, codes, depth, vocab // places), jnp.bfloat16)
+    return pl.pallas_call(
+        near_kernel,
+        in_specs=[SMEM, VMEM, HBM, HBM, HBM],
+        out_specs=[VMEM] * 5,
+        out_shape=[
+            vmem((1, width // places), jnp.float32),
+            vmem(qkv.shape, jnp.bfloat16),
+            vmem(out_weight.shape, jnp.bfloat16),
+            half,
+            half,
+        ],
+        scratch_shapes=[pltpu.SemaphoreType.DMA((2, codes)), pltpu.SemaphoreType.DMA((2, places // 2))],
+        compiler_params=params(16),
+        name="brought_near",
+    )(place, gain.reshape(1, width), in_hbm(qkv), in_hbm(out_weight), in_hbm(head_weight))
+
+
+def entry_kernel(place_ref, own_ref, other_ref, embedded_ref, weight_ref, kept_ref, sent_ref, total_buf):
+    codes = weight_ref.shape[0]
+    count, _, _, part = kept_ref.shape
+    odd = place_ref[0] % 2
+    place = place_ref[0] // 2
+    first_section = place_ref[1] == 0
+    own, other = own_ref[...], other_ref[...]
+    rows = jnp.concatenate(
+        [jnp.where(first_section, own, other), jnp.where(first_section, other, own)], axis=0
+    )
+    for c in range(codes):
+        total_buf[...] = embedded_ref[c] + product(rows, weight_ref[c])
+        for k in range(count):
+            pair = (place ^ k) * 2
+            kept_ref[k, c] = total_buf[:, pl.ds(pl.multiple_of((pair + odd) * part, part), part)]
+            sent = total_buf[:, pl.ds(pl.multiple_of((pair + 1 - odd) * part, part), part)]
+            sent_ref[k, c] = sent.astype(jnp.bfloat16)
+
+
+def entry_parts(place, own, other, embedded, weight, places):
+    codes, _, width = weight.shape
+    streams = 2 * own.shape[0]
+    block = (places // 2, codes, streams, width // places)
     return pl.pallas_call(
         entry_kernel,
-        in_specs=[VMEM, VMEM, HBM, HBM],
-        out_specs=VMEM,
-        out_shape=shape((places, codes, streams, width // places), jnp.bfloat16),
-        scratch_shapes=[
-            pltpu.VMEM(weight.shape, jnp.bfloat16),
-            pltpu.VMEM(embed.shape, jnp.bfloat16),
-            pltpu.SemaphoreType.DMA((2, codes)),
-        ],
-        compiler_params=params(24),
+        in_specs=[SMEM] + [VMEM] * 4,
+        out_specs=[VMEM, VMEM],
+        out_shape=[shape(block, jnp.float32), shape(block, jnp.bfloat16)],
+        scratch_shapes=[pltpu.VMEM((streams, width), jnp.float32)],
+        compiler_params=params(16),
         name="entry",
-    )(rows, local_tokens, weight, embed)
-
-
-def qkv_kernel(rows_ref, gain_ref, weight_hbm, queries_ref, pair_ref, weight_buf, sems):
-    codes, _, width, cols = weight_buf.shape
-    places = rows_ref.shape[0]
-    copies = [pltpu.make_async_copy(weight_hbm.at[c], weight_buf.at[c], sems.at[c]) for c in range(codes)]
-    for copy in copies:
-        copy.start()
-    inverse_gain = 1.0 / gain_ref[...]
+    )(place, own, other, embedded, weight)
+
+
+def qkv_kernel(
+    place_ref, near_ref, far_ref, gain_ref, weight_ref, columns_ref, queries_ref, pair_ref, passed_ref, sem
+):
+    passed = pltpu.make_async_copy(columns_ref, passed_ref, sem)
+    passed.start()
+    codes, _, width, cols = weight_ref.shape
+    count, _, _, part = near_ref.shape
+    odd = place_ref[0] % 2
+    place = place_ref[0] // 2
+    starts = [
+        pl.multiple_of(((place ^ k) * 2 + side) * part, part) for side in (odd, 1 - odd) for k in range(count)
+    ]
+    inverse_gain = 1.0 / jnp.concatenate([gain_ref[:, pl.ds(start, part)] for start in starts], axis=1)
     for c in range(codes):
-        row = jnp.concatenate([rows_ref[t, c] for t in range(places)], axis=1)
+        row = jnp.concatenate([ref[k, c] for ref in (near_ref, far_ref) for k in range(count)], axis=1)
         plain = row.astype(jnp.float32) * inverse_gain
         inv = lax.rsqrt(jnp.sum(plain * plain, axis=1, keepdims=True) / width + EPSILON)
-        copies[c].wait()
         for n in range(3):
-            value = (product(row, weight_buf[c, n]) * inv).astype(jnp.bfloat16)
+            weight = jnp.concatenate([weight_ref[c, n, pl.ds(start, part), :] for start in starts], axis=0)
+            value = (product(row, weight) * inv).astype(jnp.bfloat16)
             if n == 0:
                 queries_ref[c] = value
             else:
                 pair_ref[n - 1, c] = value
-
-
-def depth_projections(rows, gain, weight):
+    passed.wait()
+
+
+def depth_projections(place, near, far, gain, weight, columns):
     codes, _, width, cols = weight.shape
-    streams = rows.shape[2]
+    streams = near.shape[2]
     bf16 = jnp.bfloat16
     return pl.pallas_call(
         qkv_kernel,
-        in_specs=[VMEM, VMEM, HBM],
-        out_specs=[VMEM, VMEM],
-        out_shape=[shape((codes, streams, cols), bf16), shape((2, codes, streams, cols), bf16)],
-        scratch_shapes=[pltpu.VMEM(weight.shape, bf16), pltpu.SemaphoreType.DMA((codes,))],
+        in_specs=[SMEM] + [VMEM] * 5,
+        out_specs=[VMEM] * 3,
+        out_shape=[
+            shape((codes, streams, cols), bf16),
+            shape((2, codes, streams, cols), bf16),
+            vmem(columns.shape, bf16),
+        ],
+        scratch_shapes=[pltpu.SemaphoreType.DMA(())],
         compiler_params=params(16),
         name="depth_qkv",
-    )(rows, gain.reshape(1, width), weight)
-
-
-def mix_kernel(place_ref, queries_ref, own_ref, prior_ref, weight_hbm, kept_ref, *rest):
-    sends, (total_buf, weight_buf, sems) = rest[:-3], rest[-3:]
+    )(place, near, far, gain.reshape(1, width), weight, columns)
+
+
+def mix_kernel(place_ref, queries_ref, own_ref, prior_ref, weight_ref, kept_ref, *rest):
+    sends, total_buf = rest[:-1], rest[-1]
     codes, streams, cols = queries_ref.shape
     span = kept_ref.shape[2]
-    copy = pltpu.make_async_copy(weight_hbm, weight_buf, sems)
-    copy.start()
     has_prior = place_ref[1] > 0
     first = lax.broadcasted_iota(jnp.int32, (2 * cols, cols), 0) % cols
     second = lax.broadcasted_iota(jnp.int32, (2 * cols, cols), 1)
@@ -496,9 +616,8 @@
         for j in range(reach):
             total = total + (expo[j] * inverse).astype(jnp.bfloat16).astype(jnp.float32) * values[j]
         mixed.append(total.astype(jnp.bfloat16))
-    copy.wait()
     for q in range(codes):
-        total_buf[q] = product(mixed[q], weight_buf[q])
+        total_buf[q] = product(mixed[q], weight_ref[q])
     place = place_ref[0] // 2
     for k in range(len(sends) + 1):
         start = pl.multiple_of((place ^ k) * span, span)
@@ -515,94 +634,22 @@
     block = (codes, streams, width // (far + 1))
     return pl.pallas_call(
         mix_kernel,
-        in_specs=[SMEM, VMEM, VMEM, VMEM, HBM],
+        in_specs=[SMEM] + [VMEM] * 4,
         out_specs=[VMEM] * (far + 1),
         out_shape=[shape(block, jnp.float32)] + [shape(block, jnp.bfloat16)] * far,
-        scratch_shapes=[
-            pltpu.VMEM((codes, streams, width), jnp.float32),
-            pltpu.VMEM(weight.shape, jnp.bfloat16),
-            pltpu.SemaphoreType.DMA(()),
-        ],
+        scratch_shapes=[pltpu.VMEM((codes, streams, width), jnp.float32)],
         compiler_params=params(16),
         name="depth_mix",
     )(place, queries, own, prior, weight)
 
 
-def pair_sum_kernel(place_ref, entry_ref, kept_ref, *rest):
-    arrived, (total_ref, sent_ref) = rest[:-2], rest[-2:]
-    total = kept_ref[...]
-    for block in arrived:
-        total = total + block[...].astype(jnp.float32)
-    entry = entry_ref[...]
-    none = jnp.zeros_like(entry)
-    odd = place_ref[0] % 2 == 1
-    total = total + jnp.concatenate([jnp.where(odd, none, entry), jnp.where(odd, entry, none)], axis=2)
-    total_ref[...] = total
-    sent_ref[...] = total.astype(jnp.bfloat16)
-
-
-def pair_sums(place, entry, kept, arrived):
-    return pl.pallas_call(
-        pair_sum_kernel,
-        in_specs=[SMEM] + [VMEM] * (2 + len(arrived)),
-        out_specs=[VMEM, VMEM],
-        out_shape=[shape(kept.shape, jnp.float32), shape(kept.shape, jnp.bfloat16)],
-        compiler_params=params(16),
-        name="pair_sum",
-    )(place, entry, kept, *arrived)
-
-
-def swap_kernel(place_ref, weight_hbm, *rest):
-    halves, sems = rest[:-1], rest[-1]
-    count, codes, _, part = halves[0].shape
-    other = 1 - place_ref[0] % 2
-    copies = [
-        pltpu.make_async_copy(
-            weight_hbm.at[pl.ds(n * codes, codes), :, pl.ds(pl.multiple_of((2 * k + other) * part, part), part)],
-            half.at[k],
-            sems.at[n, k],
-        )
-        for n, half in enumerate(halves)
-        for k in range(count)
-    ]
-    for copy in copies:
-        copy.start()
-    for copy in copies:
-        copy.wait()
-
-
-def partner_columns(place, weight, places):
-    codes, depth, vocab = weight.shape
-    half = shape((places // 2, codes // 2, depth, vocab // places), jnp.bfloat16)
-    return pl.pallas_call(
-        swap_kernel,
-        in_specs=[SMEM, HBM],
-        out_specs=[VMEM, VMEM],
-        out_shape=[half, half],
-        scratch_shapes=[pltpu.SemaphoreType.DMA((2, places // 2))],
-        name="partner_columns",
-    )(place, in_hbm(weight))
-
-
 STAT_ROWS = 16
 
 
-def head_kernel(place_ref, gain_ref, total_ref, arrived_ref, own_hbm, early_ref, late_ref, kept_ref, stat_ref, *rest):
-    sends, (weight_buf, sems) = rest[:-2], rest[-2:]
+def head_kernel(place_ref, gain_ref, total_ref, arrived_ref, weight_ref, partner_ref, kept_ref, stat_ref, *sends):
     codes, streams, span = total_ref.shape
-    count, _, depth, part = weight_buf.shape
+    count, _, depth, part = weight_ref.shape
     odd = place_ref[0] % 2
-    place = place_ref[0] // 2
-    copies = [
-        pltpu.make_async_copy(
-            own_hbm.at[:, :, pl.ds(pl.multiple_of((2 * (place ^ k) + odd) * part, part), part)],
-            weight_buf.at[k],
-            sems.at[k],
-        )
-        for k in range(count)
-    ]
-    for copy in copies:
-        copy.start()
     resid = total_ref[...] + arrived_ref[...].astype(jnp.float32)
     flat = resid.reshape(codes * streams, span)
     squares = flat * flat
@@ -619,12 +666,13 @@
     ).astype(jnp.bfloat16)
     rows = codes * streams
     for k in range(count):
-        copies[k].wait()
-        blocks = []
-        for c in range(codes):
-            partner = early_ref[place ^ k, c] if c < codes // 2 else late_ref[place ^ k, c - codes // 2]
-            blocks.append(product(ordered[c], jnp.concatenate([weight_buf[k, c], partner], axis=0)))
-        block = jnp.concatenate(blocks, axis=0)
+        block = jnp.concatenate(
+            [
+                product(ordered[c], jnp.concatenate([weight_ref[k, c], partner_ref[k, c]], axis=0))
+                for c in range(codes)
+            ],
+            axis=0,
+        )
         if k == 0:
             kept_ref[...] = block
         else:
@@ -632,23 +680,19 @@
             sends[k - 1][pl.ds(rows, STAT_ROWS), :] = stat_block
 
 
-def head_parts(place, gain, total, arrived, weight, early, late):
+def head_parts(place, gain, total, arrived, weight, partner):
     codes, streams, span = total.shape
-    count, _, depth, part = early.shape
+    count, _, depth, part = weight.shape
     rows = codes * streams
     return pl.pallas_call(
         head_kernel,
-        in_specs=[SMEM, VMEM, VMEM, VMEM, HBM, VMEM, VMEM],
+        in_specs=[SMEM] + [VMEM] * 5,
         out_specs=[VMEM] * (count + 1),
         out_shape=[shape((rows, part), jnp.float32), shape((1, rows), jnp.float32)]
         + [shape((rows + STAT_ROWS, part), jnp.bfloat16)] * (count - 1),
-        scratch_shapes=[
-            pltpu.VMEM((count, codes, depth, part), jnp.bfloat16),
-            pltpu.SemaphoreType.DMA((count,)),
-        ],
         compiler_params=params(16),
         name="head",
-    )(place, gain, total, arrived, in_hbm(weight), early, late)
+    )(place, gain, total, arrived, weight, partner)
 
 
 def logits_kernel(width, kept_ref, stat_ref, *rest):
@@ -709,33 +753,47 @@
     def to_neighbour(block):
         return lax.ppermute(block, "tp", [(i, i ^ 1) for i in range(tp)])
 
-    early_half, late_half = partner_columns(place, head_weight, tp)
-    early = to_neighbour(early_half)
-    parts = temporal_parts(
-        hidden_in, temporal_gain, lengths, temporal_qkv, temporal_out_weight, cache_keys, cache_values, tp
-    )
-    slice_width = parts.shape[2]
-    parts, early = lax.optimization_barrier((parts, early))
-    summed = scattered_sum(parts)
-    resid_in = lax.dynamic_slice_in_dim(hidden_in, tp_place * slice_width, slice_width, 1)
-    temporal = (resid_in.astype(jnp.float32) + summed).astype(jnp.bfloat16)
-    all_rows = lax.all_gather(temporal, "section", axis=0, tiled=True)
+    def summed(kept, sent):
+        folded = kept + to_neighbour(sent).astype(jnp.float32)
+        arrived = to_pairs([folded[k].astype(jnp.bfloat16) for k in range(1, far + 1)])
+        return folded[0] + sum(block.astype(jnp.float32) for block in arrived)
+
+    kept, sent = temporal_parts(
+        place, hidden_in, temporal_gain, lengths, temporal_qkv, temporal_out_weight, cache_keys, cache_values, tp
+    )
+    sent, depth_in = lax.optimization_barrier((sent, depth_in))
+    resid_in, embedded, near_in = prepared_entry(place, tokens, hidden_in, depth_embed, depth_in, tp)
+    temporal = (resid_in.astype(jnp.float32) + summed(kept, sent)).astype(jnp.bfloat16)
+    other_rows = lax.ppermute(temporal, "section", [(0, 1), (1, 0)])
     codes = depth_in.shape[0]
     width = depth_in.shape[2]
     hidden_rows = head_weight.shape[1]
-    local_tokens = tokens - tp_place * depth_embed.shape[1]
-    entry = scattered_sum(entry_parts(all_rows, local_tokens, depth_in, depth_embed, tp))
-    own_gain = lax.dynamic_slice_in_dim(depth_gain, tp_place * hidden_rows, hidden_rows, 0)
-    rows = gathered((entry * own_gain).astype(jnp.bfloat16))
-    queries, own_pair = depth_projections(rows, depth_gain, depth_qkv)
+    kept, sent = entry_parts(place, temporal, other_rows, embedded, near_in, tp)
+    sent, depth_qkv = lax.optimization_barrier((sent, depth_qkv))
+    own_gain, near_qkv, near_out, own_columns, other_columns = brought_near(
+        place, depth_gain, depth_qkv, depth_out_weight, head_weight, tp
+    )
+    entry = summed(kept, sent)
+    scaled = (entry * own_gain[None]).astype(jnp.bfloat16)
+    near = jnp.stack([scaled] + to_pairs([scaled] * far))
+    queries, own_pair, other_columns = depth_projections(
+        place, near, to_neighbour(near), depth_gain, near_qkv, other_columns
+    )
     prior_pair = passed_along(own_pair, "section", 1)
-    kept, *blocks = mixed_parts(place, queries, own_pair, prior_pair, depth_out_weight, far)
-    late_half, kept = lax.optimization_barrier((late_half, kept))
-    late = to_neighbour(late_half)
-    total, sent = pair_sums(place, entry, kept, to_pairs(blocks))
+    partner_columns = to_neighbour(other_columns)
+    kept, *blocks = mixed_parts(place, queries, own_pair, prior_pair, near_out, far)
+    odd = tp_place % 2 == 1
+    none = jnp.zeros_like(entry)
+    total = kept + sum(block.astype(jnp.float32) for block in to_pairs(blocks))
+    total = total + jnp.concatenate([jnp.where(odd, none, entry), jnp.where(odd, entry, none)], axis=2)
     pair_gain = lax.dynamic_slice_in_dim(head_gain, tp_place // 2 * 2 * hidden_rows, 2 * hidden_rows, 0)
     kept, stat, *blocks = head_parts(
-        place, pair_gain.reshape(1, 1, -1), total, to_neighbour(sent), head_weight, early, late
+        place,
+        pair_gain.reshape(1, 1, -1),
+        total,
+        to_neighbour(total.astype(jnp.bfloat16)),
+        own_columns,
+        partner_columns,
     )
     logits = finished_logits(kept, stat, to_pairs(blocks), codes, width)
     return (temporal, logits)

time: 128 us -> 106 us (0.83)
  blocking collectives: 20 us -> 0 us
  starting transfers between devices: 26 us -> 32.5 us
  local copies, waits for them, and re-layouts: 6.54 us -> 0.89 us
  Pallas kernels: 26.7 us -> 24.3 us
    all_to_all x2 -> x0, waiting for transfers between devices: 23.5 us -> none  [scattered_sum(): moved = lax.all_to_all(parts.astype(jnp.bfloat16), 'tp', 0, 0)]
    all_to_all x1 -> x0, blocking collectives: 18.1 us -> none  [gathered(): lax.all_to_all(jnp.broadcast_to(block[None], (size,) + block.shape), 'tp'...]
    ppermute x3 -> x5, waiting for transfers between devices: 2.77 us -> 19.2 us  [to_neighbour(): return lax.ppermute(block, 'tp', [(i, i ^ 1) for i in range(tp)])]
    ppermute x6 -> x15, starting transfers between devices: 9.38 us -> 22.7 us  [to_pairs(): lax.ppermute(block, 'tp', [(i, i ^ 2 * (k + 1)) for i in range(tp)])]
    all_to_all x2 -> x0, starting transfers between devices: 9.29 us -> none  [scattered_sum(): moved = lax.all_to_all(parts.astype(jnp.bfloat16), 'tp', 0, 0)]
    ppermute x6 -> x15, waiting for transfers between devices: 17.5 us -> 24 us  [to_pairs(): lax.ppermute(block, 'tp', [(i, i ^ 2 * (k + 1)) for i in range(tp)])]
    unnamed x25 -> x7, local copies, waits for them, and re-layouts: 5.59 us -> 0.11 us
    pallas_call x7, Pallas kernels: 25.8 us -> 23.4 us  [the longest x1 10.4 us: temporal_parts(): pl.pallas_call(temporal_kernel, in_specs=[SMEM] + [HBM] * 7, out_specs=[V...]
  transfers between devices with their start and end apart: 12 -> 22, of which waited for: 8 -> 14; matrix products, arithmetic and copies ran while one was open for 1% -> 2% of each run, Pallas kernels for 12% -> 8%
where the time goes in v3:
time: 106 us
  waiting for transfers between devices  45.4 us (43%)
  starting transfers between devices  32.5 us (31%)
  Pallas kernels  24.3 us (23%)
  other arithmetic  1.97 us (2%)
    ppermute x15, waiting for transfers between devices, to_pairs(): lax.ppermute(block, 'tp', [(i, i ^ 2 * (k + 1)) for i in range(tp)])  24 us
    ppermute x15, starting transfers between devices, to_pairs(): lax.ppermute(block, 'tp', [(i, i ^ 2 * (k + 1)) for i in range(tp)])  22.7 us
    ppermute x5, waiting for transfers between devices, to_neighbour(): return lax.ppermute(block, 'tp', [(i, i ^ 1) for i in range(tp)])  19.2 us
    pallas_call x1, Pallas kernels, temporal_parts(): pl.pallas_call(temporal_kernel, in_specs=[SMEM] + [HBM] * 7, out_specs=[V...  10.4 us
    ppermute x5, starting transfers between devices, to_neighbour(): return lax.ppermute(block, 'tp', [(i, i ^ 1) for i in range(tp)])  8.37 us
    pallas_call x1, Pallas kernels, brought_near(): pl.pallas_call(near_kernel, in_specs=[SMEM, VMEM, HBM, HBM, HBM], out_spe...  3.46 us
    pallas_call x1, Pallas kernels, prepared_entry(): pl.pallas_call(prepare_kernel, in_specs=[SMEM, VMEM, HBM, HBM, HBM], out_...  3.44 us
    pallas_call x1, Pallas kernels, depth_projections(): pl.pallas_call(qkv_kernel, in_specs=[SMEM] + [VMEM] * 5, out_specs=[VMEM]...  2.25 us
  transfers between devices with their start and end apart: 22, of which 14 were waited for; matrix products, arithmetic and copies ran while one was open for 2% of the time, Pallas kernels for 8%

profile of v3, /device:TPU:0, one launch (start us, length us, event | category | flops | bytes accessed | tf_op | source)
XLA Modules:
  0.0 105.9 jit_solution(15299018576921679041)
XLA Ops:
  0.7 10.4 %temporal.1 = (f32[4,32,512]{2,1,0:T(8,128)S(1)}, bf16[4,32,512]{2,1,0:T(8,128)(2,1)S(1)}) custom-call(s32[2]{0:T(128)S(1)} %pad_add_fusion.place_ref, bf16[32,4096]{1,0:T(8,128)(2,1)} %hidden_hbm.3, f32[1,4096]{1,0:T(1,128)} %bitcast.44, s32[1,32]{1,0:T(1,128)} %bitcast.45, bf16[3,4096,512]{2,1,0:T(8,128)(2,1)} %qkv_hbm.1, bf16[512,4096]{1,0:T(8,128)(2,1)} %out_hbm.2, ...), custom_call_target="tpu_custom_call" | custom-call | tf_op jit(solution)/shard_map/temporal/pallas_call | solution.py:381
  11.1 3.0 %collective-permute-start = (bf16[4,32,512]{2,1,0:T(8,128)(2,1)S(1)}, bf16[4,32,512]{2,1,0:T(8,128)(2,1)S(1)}, u32[]{:S(2)}, u32[]{:S(2)}) collective-permute-start(bf16[4,32,512]{2,1,0:T(8,128)(2,1)S(1)} %get-tuple-element.34), channel_id=1, source_target_pairs={{0,2},{2,0},{4,6},{6,4},{8,10},{10,8},{12,14},{14,12},{1,3},{3,1},... | collective-permute-start | bytes 393224 | tf_op jit(solution)/shard_map/ppermute | solution.py:754
  14.2 3.5 %collective-permute-done = bf16[4,32,512]{2,1,0:T(8,128)(2,1)S(1)} collective-permute-done((bf16[4,32,512]{2,1,0:T(8,128)(2,1)S(1)}, bf16[4,32,512]{2,1,0:T(8,128)(2,1)S(1)}, u32[]{:S(2)}, u32[]{:S(2)}) %collective-permute-start) | collective-permute-done | bytes 131104 | tf_op jit(solution)/shard_map/ppermute | solution.py:754
  17.7 1.9 %collective-permute-start.1 = (bf16[32,512]{1,0:T(8,128)(2,1)S(1)}, bf16[32,512]{1,0:T(8,128)(2,1)S(1)}, u32[]{:S(2)}, u32[]{:S(2)}) collective-permute-start(bf16[32,512]{1,0:T(8,128)(2,1)S(1)} %get-tuple-element.71), channel_id=1, source_target_pairs={{0,4},{2,6},{4,0},{6,2},{8,12},{10,14},{12,8},{14,10},{1,5},{3,7},... | collective-permute-start | bytes 98312 | tf_op jit(solution)/shard_map/ppermute | solution.py:749
  19.6 2.6 %collective-permute-start.2 = (bf16[32,512]{1,0:T(8,128)(2,1)S(1)}, bf16[32,512]{1,0:T(8,128)(2,1)S(1)}, u32[]{:S(2)}, u32[]{:S(2)}) collective-permute-start(bf16[32,512]{1,0:T(8,128)(2,1)S(1)} %get-tuple-element.73), channel_id=1, source_target_pairs={{0,8},{2,10},{4,12},{6,14},{8,0},{10,2},{12,4},{14,6},{1,9},{3,11}... | collective-permute-start | bytes 98312 | tf_op jit(solution)/shard_map/ppermute | solution.py:749
  22.3 3.4 %entry_prepare.1 = (bf16[32,512]{1,0:T(8,128)(2,1)S(1)}, f32[4,64,1024]{2,1,0:T(8,128)S(1)}, bf16[4,512,1024]{2,1,0:T(8,128)(2,1)S(1)}) custom-call(s32[2]{0:T(128)S(1)} %pad_add_fusion.place_ref, s32[64,4]{1,0:T(8,128)S(1)} %copy.17.tokens_ref, bf16[32,4096]{1,0:T(8,128)(2,1)} %hidden_hbm.3, bf16[4,256,1024]{2,1,0:T(8,128)(2,1)} %embed_hbm.1, ...), custom_call_target="tpu_custom_call" | custom-call | tf_op jit(solution)/shard_map/entry_prepare/pallas_call | solution.py:439
  25.7 2.1 %collective-permute-done.3 = bf16[32,512]{1,0:T(8,128)(2,1)S(1)} collective-permute-done((bf16[32,512]{1,0:T(8,128)(2,1)S(1)}, bf16[32,512]{1,0:T(8,128)(2,1)S(1)}, u32[]{:S(2)}, u32[]{:S(2)}) %collective-permute-start.3) | collective-permute-done | bytes 32800 | tf_op jit(solution)/shard_map/ppermute | solution.py:749
  32.3 6.9 %collective-permute-done.5 = bf16[4,4,64,128]{3,2,1,0:T(8,128)(2,1)S(1)} collective-permute-done((bf16[4,4,64,128]{3,2,1,0:T(8,128)(2,1)S(1)}, bf16[4,4,64,128]{3,2,1,0:T(8,128)(2,1)S(1)}, u32[]{:S(2)}, u32[]{:S(2)}) %collective-permute-start.5) | collective-permute-done | bytes 262176 | tf_op jit(solution)/shard_map/ppermute | solution.py:754
  39.3 2.3 %collective-permute-start.7 = (bf16[4,64,128]{2,1,0:T(8,128)(2,1)S(1)}, bf16[4,64,128]{2,1,0:T(8,128)(2,1)S(1)}, u32[]{:S(2)}, u32[]{:S(2)}) collective-permute-start(bf16[4,64,128]{2,1,0:T(8,128)(2,1)S(1)} %get-tuple-element.68), channel_id=1, source_target_pairs={{0,8},{2,10},{4,12},{6,14},{8,0},{10,2},{12,4},{14,6},{1,9},{3,11}... | collective-permute-start | bytes 196616 | tf_op jit(solution)/shard_map/ppermute | solution.py:749
  41.6 2.1 %collective-permute-start.8 = (bf16[4,64,128]{2,1,0:T(8,128)(2,1)S(1)}, bf16[4,64,128]{2,1,0:T(8,128)(2,1)S(1)}, u32[]{:S(2)}, u32[]{:S(2)}) collective-permute-start(bf16[4,64,128]{2,1,0:T(8,128)(2,1)S(1)} %get-tuple-element.67), channel_id=1, source_target_pairs={{0,12},{2,14},{4,8},{6,10},{8,4},{10,6},{12,0},{14,2},{1,13},{3,15... | collective-permute-start | bytes 196616 | tf_op jit(solution)/shard_map/ppermute | solution.py:749
  43.7 3.5 %brought_near.1 = (f32[1,128]{1,0:T(1,128)S(1)}, bf16[4,3,1024,128]{3,2,1,0:T(8,128)(2,1)S(1)}, bf16[4,128,1024]{2,1,0:T(8,128)(2,1)S(1)}, bf16[4,4,128,256]{3,2...) custom-call(s32[2]{0:T(128)S(1)} %pad_add_fusion.place_ref, f32[1,1024]{1,0:T(1,128)S(1)} %bitcast.36, ...), custom_call_target="tpu_custom_call" | custom-call | tf_op jit(solution)/shard_map/brought_near/pallas_call | solution.py:487
  49.1 1.9 %collective-permute-start.10 = (bf16[4,64,128]{2,1,0:T(8,128)(2,1)S(1)}, bf16[4,64,128]{2,1,0:T(8,128)(2,1)S(1)}, u32[]{:S(2)}, u32[]{:S(2)}) collective-permute-start(bf16[4,64,128]{2,1,0:T(8,128)(2,1)S(1)} %get-tuple-element.60), channel_id=1, source_target_pairs={{0,8},{2,10},{4,12},{6,14},{8,0},{10,2},{12,4},{14,6},{1,9},{3,11}... | collective-permute-start | bytes 196616 | tf_op jit(solution)/shard_map/ppermute | solution.py:749
  51.0 1.8 %collective-permute-start.11 = (bf16[4,64,128]{2,1,0:T(8,128)(2,1)S(1)}, bf16[4,64,128]{2,1,0:T(8,128)(2,1)S(1)}, u32[]{:S(2)}, u32[]{:S(2)}) collective-permute-start(bf16[4,64,128]{2,1,0:T(8,128)(2,1)S(1)} %get-tuple-element.60), channel_id=1, source_target_pairs={{0,12},{2,14},{4,8},{6,10},{8,4},{10,6},{12,0},{14,2},{1,13},{3,15... | collective-permute-start | bytes 196616 | tf_op jit(solution)/shard_map/ppermute | solution.py:749
  52.8 2.5 %collective-permute-done.10 = bf16[4,64,128]{2,1,0:T(8,128)(2,1)S(1)} collective-permute-done((bf16[4,64,128]{2,1,0:T(8,128)(2,1)S(1)}, bf16[4,64,128]{2,1,0:T(8,128)(2,1)S(1)}, u32[]{:S(2)}, u32[]{:S(2)}) %collective-permute-start.10) | collective-permute-done | bytes 65568 | tf_op jit(solution)/shard_map/ppermute | solution.py:749
  58.7 4.9 %collective-permute-done.12.far_ref = bf16[4,4,64,128]{3,2,1,0:T(8,128)(2,1)S(1)} collective-permute-done((bf16[4,4,64,128]{3,2,1,0:T(8,128)(2,1)S(1)}, bf16[4,4,64,128]{3,2,1,0:T(8,128)(2,1)S(1)}, u32[]{:S(2)}, u32[]{:S(2)}) %collective-permute-start.12) | collective-permute-done | bytes 262176 | tf_op jit(solution)/shard_map/ppermute | solution.py:754
  63.6 2.2 %depth_qkv.1 = (bf16[4,64,128]{2,1,0:T(8,128)(2,1)S(1)}, bf16[2,4,64,128]{3,2,1,0:T(8,128)(2,1)S(1)}, bf16[4,4,128,256]{3,2,1,0:T(8,128)(2,1)}) custom-call(s32[2]{0:T(128)S(1)} %pad_add_fusion.place_ref, bf16[4,4,64,128]{3,2,1,0:T(8,128)(2,1)S(1)} %pad_maximum_fusion.near_ref, bf16[4,4,64,128]{3,2,1,0:T(8,128)(2,1)S(1)} %collective-permute-done.12.far_ref, ...), custom_call_target="tpu_custom_call" | custom-call | tf_op jit(solution)/shard_map/depth_qkv/pallas_call | solution.py:569
  71.1 2.4 %collective-permute-start.15 = (bf16[4,64,256]{2,1,0:T(8,128)(2,1)S(1)}, bf16[4,64,256]{2,1,0:T(8,128)(2,1)S(1)}, u32[]{:S(2)}, u32[]{:S(2)}) collective-permute-start(bf16[4,64,256]{2,1,0:T(8,128)(2,1)S(1)} %get-tuple-element.49), channel_id=1, source_target_pairs={{0,8},{2,10},{4,12},{6,14},{8,0},{10,2},{12,4},{14,6},{1,9},{3,11}... | collective-permute-start | bytes 393224 | tf_op jit(solution)/shard_map/ppermute | solution.py:749
  73.4 2.0 %collective-permute-start.16 = (bf16[4,64,256]{2,1,0:T(8,128)(2,1)S(1)}, bf16[4,64,256]{2,1,0:T(8,128)(2,1)S(1)}, u32[]{:S(2)}, u32[]{:S(2)}) collective-permute-start(bf16[4,64,256]{2,1,0:T(8,128)(2,1)S(1)} %get-tuple-element.50), channel_id=1, source_target_pairs={{0,12},{2,14},{4,8},{6,10},{8,4},{10,6},{12,0},{14,2},{1,13},{3,15... | collective-permute-start | bytes 393224 | tf_op jit(solution)/shard_map/ppermute | solution.py:749
  76.4 2.4 %collective-permute-done.14 = bf16[4,64,256]{2,1,0:T(8,128)(2,1)S(1)} collective-permute-done((bf16[4,64,256]{2,1,0:T(8,128)(2,1)S(1)}, bf16[4,64,256]{2,1,0:T(8,128)(2,1)S(1)}, u32[]{:S(2)}, u32[]{:S(2)}) %collective-permute-start.14) | collective-permute-done | bytes 131104 | tf_op jit(solution)/shard_map/ppermute | solution.py:749
  78.8 5.3 %collective-permute-done.15 = bf16[4,64,256]{2,1,0:T(8,128)(2,1)S(1)} collective-permute-done((bf16[4,64,256]{2,1,0:T(8,128)(2,1)S(1)}, bf16[4,64,256]{2,1,0:T(8,128)(2,1)S(1)}, u32[]{:S(2)}, u32[]{:S(2)}) %collective-permute-start.15) | collective-permute-done | bytes 131104 | tf_op jit(solution)/shard_map/ppermute | solution.py:749
  85.5 4.0 %collective-permute-done.17.arrived_ref = bf16[4,64,256]{2,1,0:T(8,128)(2,1)S(1)} collective-permute-done((bf16[4,64,256]{2,1,0:T(8,128)(2,1)S(1)}, bf16[4,64,256]{2,1,0:T(8,128)(2,1)S(1)}, u32[]{:S(2)}, u32[]{:S(2)}) %collective-permute-start.17) | collective-permute-done | bytes 131104 | tf_op jit(solution)/shard_map/ppermute | solution.py:754
  90.5 2.6 %collective-permute-start.19 = (bf16[272,256]{1,0:T(8,128)(2,1)S(1)}, bf16[272,256]{1,0:T(8,128)(2,1)S(1)}, u32[]{:S(2)}, u32[]{:S(2)}) collective-permute-start(bf16[272,256]{1,0:T(8,128)(2,1)S(1)} %get-tuple-element.55), channel_id=1, source_target_pairs={{0,4},{2,6},{4,0},{6,2},{8,12},{10,14},{12,8},{14,10},{1,5},{3,7},... | collective-permute-start | bytes 417800 | tf_op jit(solution)/shard_map/ppermute | solution.py:749
  93.5 2.0 %collective-permute-start.21 = (bf16[272,256]{1,0:T(8,128)(2,1)S(1)}, bf16[272,256]{1,0:T(8,128)(2,1)S(1)}, u32[]{:S(2)}, u32[]{:S(2)}) collective-permute-start(bf16[272,256]{1,0:T(8,128)(2,1)S(1)} %get-tuple-element.57), channel_id=1, source_target_pairs={{0,12},{2,14},{4,8},{6,10},{8,4},{10,6},{12,0},{14,2},{1,13},{3,15... | collective-permute-start | bytes 417800 | tf_op jit(solution)/shard_map/ppermute | solution.py:749
  97.2 7.7 %collective-permute-done.20.rest_1_ = bf16[272,256]{1,0:T(8,128)(2,1)S(1)} collective-permute-done((bf16[272,256]{1,0:T(8,128)(2,1)S(1)}, bf16[272,256]{1,0:T(8,128)(2,1)S(1)}, u32[]{:S(2)}, u32[]{:S(2)}) %collective-permute-start.20) | collective-permute-done | bytes 139296 | tf_op jit(solution)/shard_map/ppermute | solution.py:749
  (46 shorter events, 21.7 us)
Async XLA Ops:
  0.7 21.5 %copy-start.2 = (s32[64,4]{0,1:T(4,128)S(1)}, s32[64,4]{0,1:T(4,128)}, u32[]{:S(2)}) copy-start(s32[64,4]{0,1:T(4,128)} %param.29) | copy-start | bytes 3076
  11.1 6.5 %collective-permute-start = (bf16[4,32,512]{2,1,0:T(8,128)(2,1)S(1)}, bf16[4,32,512]{2,1,0:T(8,128)(2,1)S(1)}, u32[]{:S(2)}, u32[]{:S(2)}) collective-permute-start(bf16[4,32,512]{2,1,0:T(8,128)(2,1)S(1)} %get-tuple-element.34), channel_id=1, source_target_pairs={{0,2},{2,0},{4,6},{6,4},{8,10},{10,8},{12,14},{14,12},{1,3},{3,1},... | collective-permute-start | bytes 393224 | tf_op jit(solution)/shard_map/ppermute | solution.py:754
  17.7 8.0 %collective-permute-start.1 = (bf16[32,512]{1,0:T(8,128)(2,1)S(1)}, bf16[32,512]{1,0:T(8,128)(2,1)S(1)}, u32[]{:S(2)}, u32[]{:S(2)}) collective-permute-start(bf16[32,512]{1,0:T(8,128)(2,1)S(1)} %get-tuple-element.71), channel_id=1, source_target_pairs={{0,4},{2,6},{4,0},{6,2},{8,12},{10,14},{12,8},{14,10},{1,5},{3,7},... | collective-permute-start | bytes 98312 | tf_op jit(solution)/shard_map/ppermute | solution.py:749
  19.6 6.2 %collective-permute-start.2 = (bf16[32,512]{1,0:T(8,128)(2,1)S(1)}, bf16[32,512]{1,0:T(8,128)(2,1)S(1)}, u32[]{:S(2)}, u32[]{:S(2)}) collective-permute-start(bf16[32,512]{1,0:T(8,128)(2,1)S(1)} %get-tuple-element.73), channel_id=1, source_target_pairs={{0,8},{2,10},{4,12},{6,14},{8,0},{10,2},{12,4},{14,6},{1,9},{3,11}... | collective-permute-start | bytes 98312 | tf_op jit(solution)/shard_map/ppermute | solution.py:749
  22.2 5.7 %collective-permute-start.3 = (bf16[32,512]{1,0:T(8,128)(2,1)S(1)}, bf16[32,512]{1,0:T(8,128)(2,1)S(1)}, u32[]{:S(2)}, u32[]{:S(2)}) collective-permute-start(bf16[32,512]{1,0:T(8,128)(2,1)S(1)} %get-tuple-element.72), channel_id=1, source_target_pairs={{0,12},{2,14},{4,8},{6,10},{8,4},{10,6},{12,0},{14,2},{1,13},{3,15... | collective-permute-start | bytes 98312 | tf_op jit(solution)/shard_map/ppermute | solution.py:749
  27.9 1.3 %collective-permute-start.4 = (bf16[32,512]{1,0:T(8,128)(2,1)S(1)}, bf16[32,512]{1,0:T(8,128)(2,1)S(1)}, u32[]{:S(2)}, u32[]{:S(2)}) collective-permute-start(bf16[32,512]{1,0:T(8,128)(2,1)S(1)} %fusion.3.own_ref), channel_id=1, source_target_pairs={{0,1},{1,0},{2,3},{3,2},{4,5},{5,4},{6,7},{7,6},{8,9},{9,8},{10,11... | collective-permute-start | bytes 98312 | tf_op jit(solution)/shard_map/ppermute | solution.py:767
  29.2 14.5 %copy-start.1 = (f32[1024]{0:T(1024)S(1)}, f32[1024]{0:T(1024)}, u32[]{:S(2)}) copy-start(f32[1024]{0:T(1024)} %param.24) | copy-start | bytes 12292
  30.7 8.4 %collective-permute-start.5 = (bf16[4,4,64,128]{3,2,1,0:T(8,128)(2,1)S(1)}, bf16[4,4,64,128]{3,2,1,0:T(8,128)(2,1)S(1)}, u32[]{:S(2)}, u32[]{:S(2)}) collective-permute-start(bf16[4,4,64,128]{3,2,1,0:T(8,128)(2,1)S(1)} %get-tuple-element.39), channel_id=1, source_target_pairs={{0,2},{2,0},{4,6},{6,4},{8,10},{10,8},{12,14},{14,12},{1,3},{3,1},... | collective-permute-start | bytes 786440 | tf_op jit(solution)/shard_map/ppermute | solution.py:754
  39.2 7.9 %collective-permute-start.6 = (bf16[4,64,128]{2,1,0:T(8,128)(2,1)S(1)}, bf16[4,64,128]{2,1,0:T(8,128)(2,1)S(1)}, u32[]{:S(2)}, u32[]{:S(2)}) collective-permute-start(bf16[4,64,128]{2,1,0:T(8,128)(2,1)S(1)} %get-tuple-element.66), channel_id=1, source_target_pairs={{0,4},{2,6},{4,0},{6,2},{8,12},{10,14},{12,8},{14,10},{1,5},{3,7},... | collective-permute-start | bytes 196616 | tf_op jit(solution)/shard_map/ppermute | solution.py:749
  39.3 7.9 %collective-permute-start.7 = (bf16[4,64,128]{2,1,0:T(8,128)(2,1)S(1)}, bf16[4,64,128]{2,1,0:T(8,128)(2,1)S(1)}, u32[]{:S(2)}, u32[]{:S(2)}) collective-permute-start(bf16[4,64,128]{2,1,0:T(8,128)(2,1)S(1)} %get-tuple-element.68), channel_id=1, source_target_pairs={{0,8},{2,10},{4,12},{6,14},{8,0},{10,2},{12,4},{14,6},{1,9},{3,11}... | collective-permute-start | bytes 196616 | tf_op jit(solution)/shard_map/ppermute | solution.py:749
  41.6 6.2 %collective-permute-start.8 = (bf16[4,64,128]{2,1,0:T(8,128)(2,1)S(1)}, bf16[4,64,128]{2,1,0:T(8,128)(2,1)S(1)}, u32[]{:S(2)}, u32[]{:S(2)}) collective-permute-start(bf16[4,64,128]{2,1,0:T(8,128)(2,1)S(1)} %get-tuple-element.67), channel_id=1, source_target_pairs={{0,12},{2,14},{4,8},{6,10},{8,4},{10,6},{12,0},{14,2},{1,13},{3,15... | collective-permute-start | bytes 196616 | tf_op jit(solution)/shard_map/ppermute | solution.py:749
  48.4 4.4 %collective-permute-start.9 = (bf16[4,64,128]{2,1,0:T(8,128)(2,1)S(1)}, bf16[4,64,128]{2,1,0:T(8,128)(2,1)S(1)}, u32[]{:S(2)}, u32[]{:S(2)}) collective-permute-start(bf16[4,64,128]{2,1,0:T(8,128)(2,1)S(1)} %get-tuple-element.60), channel_id=1, source_target_pairs={{0,4},{2,6},{4,0},{6,2},{8,12},{10,14},{12,8},{14,10},{1,5},{3,7},... | collective-permute-start | bytes 196616 | tf_op jit(solution)/shard_map/ppermute | solution.py:749
  49.1 6.2 %collective-permute-start.10 = (bf16[4,64,128]{2,1,0:T(8,128)(2,1)S(1)}, bf16[4,64,128]{2,1,0:T(8,128)(2,1)S(1)}, u32[]{:S(2)}, u32[]{:S(2)}) collective-permute-start(bf16[4,64,128]{2,1,0:T(8,128)(2,1)S(1)} %get-tuple-element.60), channel_id=1, source_target_pairs={{0,8},{2,10},{4,12},{6,14},{8,0},{10,2},{12,4},{14,6},{1,9},{3,11}... | collective-permute-start | bytes 196616 | tf_op jit(solution)/shard_map/ppermute | solution.py:749
  51.0 6.1 %collective-permute-start.11 = (bf16[4,64,128]{2,1,0:T(8,128)(2,1)S(1)}, bf16[4,64,128]{2,1,0:T(8,128)(2,1)S(1)}, u32[]{:S(2)}, u32[]{:S(2)}) collective-permute-start(bf16[4,64,128]{2,1,0:T(8,128)(2,1)S(1)} %get-tuple-element.60), channel_id=1, source_target_pairs={{0,12},{2,14},{4,8},{6,10},{8,4},{10,6},{12,0},{14,2},{1,13},{3,15... | collective-permute-start | bytes 196616 | tf_op jit(solution)/shard_map/ppermute | solution.py:749
  57.1 6.4 %collective-permute-start.12 = (bf16[4,4,64,128]{3,2,1,0:T(8,128)(2,1)S(1)}, bf16[4,4,64,128]{3,2,1,0:T(8,128)(2,1)S(1)}, u32[]{:S(2)}, u32[]{:S(2)}) collective-permute-start(bf16[4,4,64,128]{3,2,1,0:T(8,128)(2,1)S(1)} %pad_maximum_fusion.near_ref), channel_id=1, source_target_pairs={{0,2},{2,0},{4,6},{6,4},{8,10},{10,8},{12,14},{14,12},{1,3},{3,1},... | collective-permute-start | bytes 786440 | tf_op jit(solution)/shard_map/ppermute | solution.py:754
  65.8 23.7 %collective-permute-start.18 = (bf16[4,4,128,256]{3,2,1,0:T(8,128)(2,1)}, bf16[4,4,128,256]{3,2,1,0:T(8,128)(2,1)S(1)}, u32[]{:S(2)}, u32[]{:S(2)}) collective-permute-start(bf16[4,4,128,256]{3,2,1,0:T(8,128)(2,1)} %get-tuple-element.52), channel_id=1, source_target_pairs={{0,2},{2,0},{4,6},{6,4},{8,10},{10,8},{12,14},{14,12},{1,3},{3,1},... | collective-permute-start | bytes 3145736 | tf_op jit(solution)/shard_map/ppermute | solution.py:754
  67.4 2.3 %collective-permute-start.13 = (bf16[2,4,64,128]{3,2,1,0:T(8,128)(2,1)S(1)}, bf16[2,4,64,128]{3,2,1,0:T(8,128)(2,1)S(1)}, u32[]{:S(2)}, u32[]{:S(2)}) collective-permute-start(bf16[2,4,64,128]{3,2,1,0:T(8,128)(2,1)S(1)} %get-tuple-element.45.own_ref), channel_id=1, source_target_pairs={{0,1},{2,3},{4,5},{6,7},{8,9},{10,11},{12,13},{14,15},{16,17},{18,... | collective-permute-start | bytes 393224 | tf_op jit(solution)/shard_map/ppermute | solution.py:21
  71.0 7.8 %collective-permute-start.14 = (bf16[4,64,256]{2,1,0:T(8,128)(2,1)S(1)}, bf16[4,64,256]{2,1,0:T(8,128)(2,1)S(1)}, u32[]{:S(2)}, u32[]{:S(2)}) collective-permute-start(bf16[4,64,256]{2,1,0:T(8,128)(2,1)S(1)} %get-tuple-element.48), channel_id=1, source_target_pairs={{0,4},{2,6},{4,0},{6,2},{8,12},{10,14},{12,8},{14,10},{1,5},{3,7},... | collective-permute-start | bytes 393224 | tf_op jit(solution)/shard_map/ppermute | solution.py:749
  71.1 13.0 %collective-permute-start.15 = (bf16[4,64,256]{2,1,0:T(8,128)(2,1)S(1)}, bf16[4,64,256]{2,1,0:T(8,128)(2,1)S(1)}, u32[]{:S(2)}, u32[]{:S(2)}) collective-permute-start(bf16[4,64,256]{2,1,0:T(8,128)(2,1)S(1)} %get-tuple-element.49), channel_id=1, source_target_pairs={{0,8},{2,10},{4,12},{6,14},{8,0},{10,2},{12,4},{14,6},{1,9},{3,11}... | collective-permute-start | bytes 393224 | tf_op jit(solution)/shard_map/ppermute | solution.py:749
  73.4 10.6 %collective-permute-start.16 = (bf16[4,64,256]{2,1,0:T(8,128)(2,1)S(1)}, bf16[4,64,256]{2,1,0:T(8,128)(2,1)S(1)}, u32[]{:S(2)}, u32[]{:S(2)}) collective-permute-start(bf16[4,64,256]{2,1,0:T(8,128)(2,1)S(1)} %get-tuple-element.50), channel_id=1, source_target_pairs={{0,12},{2,14},{4,8},{6,10},{8,4},{10,6},{12,0},{14,2},{1,13},{3,15... | collective-permute-start | bytes 393224 | tf_op jit(solution)/shard_map/ppermute | solution.py:749
  84.1 5.3 %collective-permute-start.17 = (bf16[4,64,256]{2,1,0:T(8,128)(2,1)S(1)}, bf16[4,64,256]{2,1,0:T(8,128)(2,1)S(1)}, u32[]{:S(2)}, u32[]{:S(2)}) collective-permute-start(bf16[4,64,256]{2,1,0:T(8,128)(2,1)S(1)} %get-tuple-element.58), channel_id=1, source_target_pairs={{0,2},{2,0},{4,6},{6,4},{8,10},{10,8},{12,14},{14,12},{1,3},{3,1},... | collective-permute-start | bytes 393224 | tf_op jit(solution)/shard_map/ppermute | solution.py:754
  90.5 6.7 %collective-permute-start.19 = (bf16[272,256]{1,0:T(8,128)(2,1)S(1)}, bf16[272,256]{1,0:T(8,128)(2,1)S(1)}, u32[]{:S(2)}, u32[]{:S(2)}) collective-permute-start(bf16[272,256]{1,0:T(8,128)(2,1)S(1)} %get-tuple-element.55), channel_id=1, source_target_pairs={{0,4},{2,6},{4,0},{6,2},{8,12},{10,14},{12,8},{14,10},{1,5},{3,7},... | collective-permute-start | bytes 417800 | tf_op jit(solution)/shard_map/ppermute | solution.py:749
  93.1 11.9 %collective-permute-start.20 = (bf16[272,256]{1,0:T(8,128)(2,1)S(1)}, bf16[272,256]{1,0:T(8,128)(2,1)S(1)}, u32[]{:S(2)}, u32[]{:S(2)}) collective-permute-start(bf16[272,256]{1,0:T(8,128)(2,1)S(1)} %get-tuple-element.56), channel_id=1, source_target_pairs={{0,8},{2,10},{4,12},{6,14},{8,0},{10,2},{12,4},{14,6},{1,9},{3,11}... | collective-permute-start | bytes 417800 | tf_op jit(solution)/shard_map/ppermute | solution.py:749
  93.5 11.4 %collective-permute-start.21 = (bf16[272,256]{1,0:T(8,128)(2,1)S(1)}, bf16[272,256]{1,0:T(8,128)(2,1)S(1)}, u32[]{:S(2)}, u32[]{:S(2)}) collective-permute-start(bf16[272,256]{1,0:T(8,128)(2,1)S(1)} %get-tuple-element.57), channel_id=1, source_target_pairs={{0,12},{2,14},{4,8},{6,10},{8,4},{10,6},{12,0},{14,2},{1,13},{3,15... | collective-permute-start | bytes 417800 | tf_op jit(solution)/shard_map/ppermute | solution.py:749
  (1 other events, 11.3 us)

commit v4 on v3

--- a/solution.py
+++ b/solution.py
@@ -231,25 +231,28 @@
 
 
 IN_FLIGHT = 6
+IN_FLIGHT_BESIDE = 6
+CHUNKS = 1
 
 
 class Stream:
-    def __init__(self, copies):
+    def __init__(self, copies, in_flight):
         self.copies = copies
+        self.in_flight = in_flight
         self.done = 0
-        for copy in copies[:IN_FLIGHT]:
+        for copy in copies[:in_flight]:
             copy.start()
 
     def arrived(self, upto):
         while self.done <= upto:
             self.copies[self.done].wait()
-            if self.done + IN_FLIGHT < len(self.copies):
-                self.copies[self.done + IN_FLIGHT].start()
+            if self.done + self.in_flight < len(self.copies):
+                self.copies[self.done + self.in_flight].start()
             self.done += 1
 
 
 def temporal_kernel(
-    place_ref, hidden_hbm, gain_hbm, lengths_hbm, qkv_hbm, out_hbm, keys_hbm, values_hbm, kept_ref, sent_ref,
+    place_ref, hidden_hbm, gain_hbm, lengths_hbm, qkv_hbm, out_hbm, keys_hbm, values_hbm, kept_ref, last_ref, sent_ref,
     hidden_buf, gain_buf, lengths_buf, qkv_buf, out_buf, keys_buf, values_buf, small_sems, sems,
 ):
     streams, depth = hidden_buf.shape
@@ -279,7 +282,7 @@
         (out_hbm.at[:, pl.ds(pl.multiple_of((place ^ k) * 2 * width, 2 * width), 2 * width)], out_buf.at[k])
         for k in range(count)
     ]
-    stream = Stream([pltpu.make_async_copy(src, dst, sems.at[i]) for i, (src, dst) in enumerate(pairs)])
+    stream = Stream([pltpu.make_async_copy(src, dst, sems.at[i]) for i, (src, dst) in enumerate(pairs)], IN_FLIGHT)
     first_of = (0, steps, 2 * steps + halves)
     keys_end = 2 * steps + halves - 1
     values_end = 3 * steps + 2 * halves - 1
@@ -366,7 +369,11 @@
         block = product(mixed, out_buf[k])
         even_side, odd_side = block[:, :width], block[:, width:]
         kept_ref[k] = jnp.where(odd == 1, odd_side, even_side)
-        sent_ref[k] = jnp.where(odd == 1, even_side, odd_side).astype(jnp.bfloat16)
+        sent = jnp.where(odd == 1, even_side, odd_side).astype(jnp.bfloat16)
+        if k == 0:
+            last_ref[...] = sent
+        else:
+            sent_ref[k - 1] = sent
 
 
 QKV_STEPS = 4
@@ -381,8 +388,8 @@
     return pl.pallas_call(
         temporal_kernel,
         in_specs=[SMEM] + [HBM] * 7,
-        out_specs=[VMEM, VMEM],
-        out_shape=[vmem(block, jnp.float32), vmem(block, bf16)],
+        out_specs=[VMEM] * 3,
+        out_shape=[vmem(block, jnp.float32), vmem(block[1:], bf16), vmem((count - 1,) + block[1:], bf16)],
         scratch_shapes=[
             pltpu.VMEM(hidden_in.shape, bf16),
             pltpu.VMEM((1, depth), jnp.float32),
@@ -419,16 +426,14 @@
     resid.start()
     embed = [pltpu.make_async_copy(embed_hbm.at[c], embed_buf.at[c], sems.at[0, c]) for c in range(codes)]
     weight = [pltpu.make_async_copy(weight_hbm.at[c], weight_ref.at[c], sems.at[1, c]) for c in range(codes)]
-    for copy in embed + weight:
-        copy.start()
+    stream = Stream(embed + weight, IN_FLIGHT_BESIDE)
     vocab_lane = lax.broadcasted_iota(jnp.int32, (streams, vocab), 1) + place_ref[0] * vocab
     for c in range(codes):
         hit = tokens_ref[:, c : c + 1] == vocab_lane
         onehot = jnp.where(hit, 1.0, 0.0).astype(jnp.bfloat16)
-        embed[c].wait()
+        stream.arrived(c)
         embedded_ref[c] = product(onehot, embed_buf[c])
-    for copy in weight:
-        copy.wait()
+    stream.arrived(2 * codes - 1)
     resid.wait()
 
 
@@ -455,53 +460,79 @@
     )(place, tokens, in_hbm(hidden_in), in_hbm(embed), in_hbm(weight))
 
 
-def near_kernel(
-    place_ref, gain_ref, qkv_hbm, out_hbm, head_hbm, own_ref, qkv_ref, out_ref, near_cols_ref, far_cols_ref, sems, col_sems
-):
+def near_kernel(place_ref, token_ref, gain_ref, qkv_hbm, out_hbm, own_ref, qkv_ref, out_ref, sems):
+    del token_ref
     copies = [
         pltpu.make_async_copy(source.at[c], target.at[c], sems.at[i, c])
         for i, (source, target) in enumerate(((qkv_hbm, qkv_ref), (out_hbm, out_ref)))
         for c in range(source.shape[0])
     ]
-    count, _, _, vocab_part = near_cols_ref.shape
-    odd = place_ref[0] % 2
-    place = place_ref[0] // 2
-    for n, (half, side) in enumerate(((far_cols_ref, 1 - odd), (near_cols_ref, odd))):
-        for k in range(count):
-            start = pl.multiple_of(((place ^ k) * 2 + side) * vocab_part, vocab_part)
-            copies.append(
-                pltpu.make_async_copy(head_hbm.at[:, :, pl.ds(start, vocab_part)], half.at[k], col_sems.at[n, k])
-            )
-    for copy in copies:
-        copy.start()
+    stream = Stream(copies, IN_FLIGHT_BESIDE)
     part = own_ref.shape[1]
     own_ref[...] = gain_ref[:, pl.ds(pl.multiple_of(place_ref[0] * part, part), part)]
-    for copy in copies:
-        copy.wait()
-
-
-def brought_near(place, gain, qkv, out_weight, head_weight, places):
+    stream.arrived(len(copies) - 1)
+
+
+def brought_near(place, token, gain, qkv, out_weight, places):
     width = gain.shape[0]
-    codes, depth, vocab = head_weight.shape
-    half = vmem((places // 2, codes, depth, vocab // places), jnp.bfloat16)
     return pl.pallas_call(
         near_kernel,
-        in_specs=[SMEM, VMEM, HBM, HBM, HBM],
-        out_specs=[VMEM] * 5,
+        in_specs=[SMEM, VMEM, VMEM, HBM, HBM],
+        out_specs=[VMEM] * 3,
         out_shape=[
             vmem((1, width // places), jnp.float32),
             vmem(qkv.shape, jnp.bfloat16),
             vmem(out_weight.shape, jnp.bfloat16),
-            half,
-            half,
         ],
-        scratch_shapes=[pltpu.SemaphoreType.DMA((2, codes)), pltpu.SemaphoreType.DMA((2, places // 2))],
+        scratch_shapes=[pltpu.SemaphoreType.DMA((2, qkv.shape[0]))],
         compiler_params=params(16),
         name="brought_near",
-    )(place, gain.reshape(1, width), in_hbm(qkv), in_hbm(out_weight), in_hbm(head_weight))
-
-
-def entry_kernel(place_ref, own_ref, other_ref, embedded_ref, weight_ref, kept_ref, sent_ref, total_buf):
+    )(place, token, gain.reshape(1, width), in_hbm(qkv), in_hbm(out_weight))
+
+
+def split_kernel(place_ref, head_hbm, far_ref, *rest):
+    outs, sems = rest[:-1], rest[-1]
+    count, half, _, part = far_ref.shape
+    each = outs[0].shape[1]
+    odd = place_ref[0] % 2
+    place = place_ref[0] // 2
+    blocks = [(far_ref, place_ref[2] * half, half, 1 - odd)]
+    blocks += [(out, n * each, each, odd) for n, out in enumerate(outs)]
+    copies = []
+    for n, (out, first, size, side) in enumerate(blocks):
+        for k in range(count):
+            start = pl.multiple_of(((place ^ k) * 2 + side) * part, part)
+            copies.append(
+                pltpu.make_async_copy(
+                    head_hbm.at[pl.ds(first, size), :, pl.ds(start, part)], out.at[k], sems.at[n, k]
+                )
+            )
+    for copy in copies:
+        copy.start()
+    for copy in copies:
+        copy.wait()
+
+
+def split_columns(place, weight, places):
+    codes, depth, vocab = weight.shape
+
+    def block(size):
+        return vmem((places // 2, size, depth, vocab // places), jnp.bfloat16)
+
+    return pl.pallas_call(
+        split_kernel,
+        in_specs=[SMEM, HBM],
+        out_specs=[VMEM] * (1 + CHUNKS),
+        out_shape=[block(codes // 2)] + [block(codes // CHUNKS)] * CHUNKS,
+        scratch_shapes=[pltpu.SemaphoreType.DMA((1 + CHUNKS, places // 2))],
+        compiler_params=params(16),
+        name="split_columns",
+    )(place, in_hbm(weight))
+
+
+def entry_kernel(place_ref, own_ref, other_ref, embedded_ref, weight_ref, after_ref, kept_ref, last_ref, sent_ref, token_ref, total_buf):
+    del after_ref
+    token_ref[...] = jnp.zeros_like(token_ref)
     codes = weight_ref.shape[0]
     count, _, _, part = kept_ref.shape
     odd = place_ref[0] % 2
@@ -516,32 +547,37 @@
         for k in range(count):
             pair = (place ^ k) * 2
             kept_ref[k, c] = total_buf[:, pl.ds(pl.multiple_of((pair + odd) * part, part), part)]
-            sent = total_buf[:, pl.ds(pl.multiple_of((pair + 1 - odd) * part, part), part)]
-            sent_ref[k, c] = sent.astype(jnp.bfloat16)
-
-
-def entry_parts(place, own, other, embedded, weight, places):
+            sent = total_buf[:, pl.ds(pl.multiple_of((pair + 1 - odd) * part, part), part)].astype(jnp.bfloat16)
+            if k == 0:
+                last_ref[c] = sent
+            else:
+                sent_ref[k - 1, c] = sent
+
+
+def entry_parts(place, own, other, embedded, weight, after, places):
     codes, _, width = weight.shape
     streams = 2 * own.shape[0]
     block = (places // 2, codes, streams, width // places)
     return pl.pallas_call(
         entry_kernel,
-        in_specs=[SMEM] + [VMEM] * 4,
-        out_specs=[VMEM, VMEM],
-        out_shape=[shape(block, jnp.float32), shape(block, jnp.bfloat16)],
+        in_specs=[SMEM] + [VMEM] * 5,
+        out_specs=[VMEM] * 4,
+        out_shape=[
+            vmem(block, jnp.float32),
+            vmem(block[1:], jnp.bfloat16),
+            vmem((places // 2 - 1,) + block[1:], jnp.bfloat16),
+            vmem((8, 128), jnp.float32),
+        ],
         scratch_shapes=[pltpu.VMEM((streams, width), jnp.float32)],
         compiler_params=params(16),
         name="entry",
-    )(place, own, other, embedded, weight)
-
-
-def qkv_kernel(
-    place_ref, near_ref, far_ref, gain_ref, weight_ref, columns_ref, queries_ref, pair_ref, passed_ref, sem
-):
-    passed = pltpu.make_async_copy(columns_ref, passed_ref, sem)
-    passed.start()
+    )(place, own, other, embedded, weight, after)
+
+
+def qkv_kernel(count, place_ref, gain_ref, weight_ref, far_ref, *rest):
+    near_refs, (last_ref, queries_ref, pair_ref) = rest[:count], rest[count:]
     codes, _, width, cols = weight_ref.shape
-    count, _, _, part = near_ref.shape
+    part = last_ref.shape[2]
     odd = place_ref[0] % 2
     place = place_ref[0] // 2
     starts = [
@@ -549,7 +585,8 @@
     ]
     inverse_gain = 1.0 / jnp.concatenate([gain_ref[:, pl.ds(start, part)] for start in starts], axis=1)
     for c in range(codes):
-        row = jnp.concatenate([ref[k, c] for ref in (near_ref, far_ref) for k in range(count)], axis=1)
+        blocks = [ref[c] for ref in near_refs] + [last_ref[c]] + [far_ref[k, c] for k in range(count - 1)]
+        row = jnp.concatenate(blocks, axis=1)
         plain = row.astype(jnp.float32) * inverse_gain
         inv = lax.rsqrt(jnp.sum(plain * plain, axis=1, keepdims=True) / width + EPSILON)
         for n in range(3):
@@ -559,32 +596,27 @@
                 queries_ref[c] = value
             else:
                 pair_ref[n - 1, c] = value
-    passed.wait()
-
-
-def depth_projections(place, near, far, gain, weight, columns):
+
+
+def depth_projections(place, near, last, far, gain, weight):
     codes, _, width, cols = weight.shape
-    streams = near.shape[2]
+    streams = last.shape[1]
     bf16 = jnp.bfloat16
     return pl.pallas_call(
-        qkv_kernel,
-        in_specs=[SMEM] + [VMEM] * 5,
-        out_specs=[VMEM] * 3,
-        out_shape=[
-            shape((codes, streams, cols), bf16),
-            shape((2, codes, streams, cols), bf16),
-            vmem(columns.shape, bf16),
-        ],
-        scratch_shapes=[pltpu.SemaphoreType.DMA(())],
+        functools.partial(qkv_kernel, len(near)),
+        in_specs=[SMEM] + [VMEM] * (4 + len(near)),
+        out_specs=[VMEM] * 2,
+        out_shape=[vmem((codes, streams, cols), bf16), vmem((2, codes, streams, cols), bf16)],
         compiler_params=params(16),
         name="depth_qkv",
-    )(place, near, far, gain.reshape(1, width), weight, columns)
-
-
-def mix_kernel(place_ref, queries_ref, own_ref, prior_ref, weight_ref, kept_ref, *rest):
-    sends, total_buf = rest[:-1], rest[-1]
+    )(place, gain.reshape(1, width), weight, far, *near, last)
+
+
+def mix_kernel(terms, place_ref, queries_ref, own_ref, prior_ref, weight_ref, *rest):
+    entry_refs, outs, total_buf = rest[:terms], rest[terms:-1], rest[-1]
     codes, streams, cols = queries_ref.shape
-    span = kept_ref.shape[2]
+    each, _, span = outs[0].shape
+    count = len(outs) // CHUNKS
     has_prior = place_ref[1] > 0
     first = lax.broadcasted_iota(jnp.int32, (2 * cols, cols), 0) % cols
     second = lax.broadcasted_iota(jnp.int32, (2 * cols, cols), 1)
@@ -618,35 +650,45 @@
         mixed.append(total.astype(jnp.bfloat16))
     for q in range(codes):
         total_buf[q] = product(mixed[q], weight_ref[q])
+    part = entry_refs[0].shape[2]
+    own_part = pl.ds(pl.multiple_of(place_ref[0] * part, part), part)
+    total_buf[:, :, own_part] += sum(ref[...].astype(jnp.float32) for ref in entry_refs)
     place = place_ref[0] // 2
-    for k in range(len(sends) + 1):
+    for n, out in enumerate(outs):
+        chunk, k = divmod(n, count)
         start = pl.multiple_of((place ^ k) * span, span)
-        block = total_buf[:, :, pl.ds(start, span)]
-        if k == 0:
-            kept_ref[...] = block
-        else:
-            sends[k - 1][...] = block.astype(jnp.bfloat16)
-
-
-def mixed_parts(place, queries, own, prior, weight, far):
+        block = total_buf[pl.ds(chunk * each, each), :, pl.ds(start, span)]
+        out[...] = block if k == 0 else block.astype(jnp.bfloat16)
+
+
+def mixed_parts(place, queries, own, prior, weight, entry_terms, far):
     codes, streams, cols = queries.shape
     width = weight.shape[2]
-    block = (codes, streams, width // (far + 1))
-    return pl.pallas_call(
-        mix_kernel,
-        in_specs=[SMEM] + [VMEM] * 4,
-        out_specs=[VMEM] * (far + 1),
-        out_shape=[shape(block, jnp.float32)] + [shape(block, jnp.bfloat16)] * far,
+    block = (codes // CHUNKS, streams, width // (far + 1))
+    outs = pl.pallas_call(
+        functools.partial(mix_kernel, len(entry_terms)),
+        in_specs=[SMEM] + [VMEM] * (4 + len(entry_terms)),
+        out_specs=[VMEM] * ((far + 1) * CHUNKS),
+        out_shape=([vmem(block, jnp.float32)] + [vmem(block, jnp.bfloat16)] * far) * CHUNKS,
         scratch_shapes=[pltpu.VMEM((codes, streams, width), jnp.float32)],
         compiler_params=params(16),
         name="depth_mix",
-    )(place, queries, own, prior, weight)
+    )(place, queries, own, prior, weight, *entry_terms)
+    return [outs[n * (far + 1) : (n + 1) * (far + 1)] for n in range(CHUNKS)]
 
 
 STAT_ROWS = 16
 
 
-def head_kernel(place_ref, gain_ref, total_ref, arrived_ref, weight_ref, partner_ref, kept_ref, stat_ref, *sends):
+def head_kernel(
+    first, place_ref, gain_ref, total_ref, arrived_ref, weight_ref, early_ref, late_ref, kept_ref, stat_ref, *sends
+):
+    half = early_ref.shape[1]
+
+    def partner(k, c):
+        side, index = divmod(first + c, half)
+        return jnp.where(place_ref[2] == side, early_ref[k, index], late_ref[k, index])
+
     codes, streams, span = total_ref.shape
     count, _, depth, part = weight_ref.shape
     odd = place_ref[0] % 2
@@ -658,6 +700,9 @@
     high = stat.astype(jnp.bfloat16).astype(jnp.float32)
     stat_row = lax.broadcasted_iota(jnp.int32, (STAT_ROWS, codes * streams), 0)
     stat_block = jnp.where(stat_row == 0, high, jnp.where(stat_row == 1, stat - high, 0.0))
+    if part > codes * streams:
+        rest = jnp.zeros((STAT_ROWS, part - codes * streams), jnp.float32)
+        stat_block = jnp.concatenate([stat_block, rest], axis=1)
     stat_block = stat_block.astype(jnp.bfloat16)
     scaled = resid * gain_ref[...]
     low_half, high_half = scaled[:, :, :depth], scaled[:, :, depth:]
@@ -668,7 +713,7 @@
     for k in range(count):
         block = jnp.concatenate(
             [
-                product(ordered[c], jnp.concatenate([weight_ref[k, c], partner_ref[k, c]], axis=0))
+                product(ordered[c], jnp.concatenate([weight_ref[k, c], partner(k, c)], axis=0))
                 for c in range(codes)
             ],
             axis=0,
@@ -680,46 +725,51 @@
             sends[k - 1][pl.ds(rows, STAT_ROWS), :] = stat_block
 
 
-def head_parts(place, gain, total, arrived, weight, partner):
+def head_parts(first, place, gain, total, arrived, weight, early, late):
     codes, streams, span = total.shape
     count, _, depth, part = weight.shape
     rows = codes * streams
     return pl.pallas_call(
-        head_kernel,
-        in_specs=[SMEM] + [VMEM] * 5,
+        functools.partial(head_kernel, first),
+        in_specs=[SMEM] + [VMEM] * 6,
         out_specs=[VMEM] * (count + 1),
-        out_shape=[shape((rows, part), jnp.float32), shape((1, rows), jnp.float32)]
-        + [shape((rows + STAT_ROWS, part), jnp.bfloat16)] * (count - 1),
+        out_shape=[vmem((rows, part), jnp.float32), vmem((1, rows), jnp.float32)]
+        + [vmem((rows + STAT_ROWS, part), jnp.bfloat16)] * (count - 1),
         compiler_params=params(16),
         name="head",
-    )(place, gain, total, arrived, weight, partner)
-
-
-def logits_kernel(width, kept_ref, stat_ref, *rest):
-    arrived, out_ref = rest[:-1], rest[-1]
+    )(place, gain, total, arrived, weight, early, late)
+
+
+def logits_kernel(width, *refs):
+    out_ref = refs[-1]
     streams, codes, part = out_ref.shape
-    rows = codes * streams
-    total = kept_ref[...]
-    stat = stat_ref[...]
-    for block in arrived:
-        wide = block[...].astype(jnp.float32)
-        total = total + wide[:rows]
-        stat = stat + wide[rows : rows + 1] + wide[rows + 1 : rows + 2]
-    total = total * column_of(lax.rsqrt(stat / width + EPSILON))
-    for c in range(codes):
-        out_ref[:, c, :] = total[c * streams : (c + 1) * streams]
-
-
-def finished_logits(kept, stat, arrived, codes, width):
-    rows, part = kept.shape
+    each = codes // CHUNKS
+    rows = each * streams
+    count = (len(refs) - 1) // CHUNKS
+    for n in range(CHUNKS):
+        kept_ref, stat_ref, *arrived = refs[n * count : (n + 1) * count]
+        total = kept_ref[...]
+        stat = stat_ref[...]
+        for block in arrived:
+            wide = block[...].astype(jnp.float32)
+            total = total + wide[:rows]
+            stat = stat + wide[rows : rows + 1, :rows] + wide[rows + 1 : rows + 2, :rows]
+        total = total * column_of(lax.rsqrt(stat / width + EPSILON))
+        for c in range(each):
+            out_ref[:, n * each + c, :] = total[c * streams : (c + 1) * streams]
+
+
+def finished_logits(chunks, streams, codes, width):
+    part = chunks[0][0].shape[1]
+    arrays = [array for chunk in chunks for array in chunk]
     return pl.pallas_call(
         functools.partial(logits_kernel, width),
-        in_specs=[VMEM] * (2 + len(arrived)),
+        in_specs=[VMEM] * len(arrays),
         out_specs=VMEM,
-        out_shape=shape((rows // codes, codes, part), jnp.float32),
+        out_shape=shape((streams, codes, part), jnp.float32),
         compiler_params=params(16),
         name="logits",
-    )(kept, stat, *arrived)
+    )(*arrays)
 
 
 def paired_device(
@@ -741,66 +791,69 @@
 ):
     tp = lax.axis_size("tp")
     tp_place = lax.axis_index("tp")
-    place = jnp.stack([tp_place, lax.axis_index("section")])
+    place = jnp.stack([tp_place, lax.axis_index("section"), lax.axis_index("grp") % 2])
     far = tp // 2 - 1
 
     def to_pairs(blocks):
-        return [
-            lax.ppermute(block, "tp", [(i, i ^ 2 * (k + 1)) for i in range(tp)])
-            for k, block in enumerate(blocks)
-        ]
+        arrived = [None] * len(blocks)
+        for k in reversed(range(len(blocks))):
+            arrived[k] = lax.ppermute(blocks[k], "tp", [(i, i ^ 2 * (k + 1)) for i in range(tp)])
+        return arrived
 
     def to_neighbour(block):
         return lax.ppermute(block, "tp", [(i, i ^ 1) for i in range(tp)])
 
-    def summed(kept, sent):
-        folded = kept + to_neighbour(sent).astype(jnp.float32)
-        arrived = to_pairs([folded[k].astype(jnp.bfloat16) for k in range(1, far + 1)])
-        return folded[0] + sum(block.astype(jnp.float32) for block in arrived)
-
-    kept, sent = temporal_parts(
+    def summed(kept, last, sent):
+        folded = kept[1:] + to_neighbour(sent).astype(jnp.float32)
+        arrived = to_pairs([folded[k].astype(jnp.bfloat16) for k in range(far)])
+        return [kept[0]] + arrived + [to_neighbour(last)]
+
+    def added(terms):
+        return sum(term.astype(jnp.float32) for term in terms)
+
+    kept, last, sent = temporal_parts(
         place, hidden_in, temporal_gain, lengths, temporal_qkv, temporal_out_weight, cache_keys, cache_values, tp
     )
-    sent, depth_in = lax.optimization_barrier((sent, depth_in))
+    sent, depth_in, head_weight = lax.optimization_barrier((sent, depth_in, head_weight))
+    neighbour_columns, *own_columns = split_columns(place, head_weight, tp)
+    early = to_neighbour(neighbour_columns)
     resid_in, embedded, near_in = prepared_entry(place, tokens, hidden_in, depth_embed, depth_in, tp)
-    temporal = (resid_in.astype(jnp.float32) + summed(kept, sent)).astype(jnp.bfloat16)
+    temporal = (resid_in.astype(jnp.float32) + added(summed(kept, last, sent))).astype(jnp.bfloat16)
     other_rows = lax.ppermute(temporal, "section", [(0, 1), (1, 0)])
     codes = depth_in.shape[0]
     width = depth_in.shape[2]
     hidden_rows = head_weight.shape[1]
-    kept, sent = entry_parts(place, temporal, other_rows, embedded, near_in, tp)
-    sent, depth_qkv = lax.optimization_barrier((sent, depth_qkv))
-    own_gain, near_qkv, near_out, own_columns, other_columns = brought_near(
-        place, depth_gain, depth_qkv, depth_out_weight, head_weight, tp
-    )
-    entry = summed(kept, sent)
-    scaled = (entry * own_gain[None]).astype(jnp.bfloat16)
-    near = jnp.stack([scaled] + to_pairs([scaled] * far))
-    queries, own_pair, other_columns = depth_projections(
-        place, near, to_neighbour(near), depth_gain, near_qkv, other_columns
+    kept, last, sent, token = entry_parts(place, temporal, other_rows, embedded, near_in, early, tp)
+    late = lax.ppermute(early, "grp", [(i, i ^ 1) for i in range(lax.axis_size("grp"))])
+    own_gain, near_qkv, near_out = brought_near(place, token, depth_gain, depth_qkv, depth_out_weight, tp)
+    entry_terms = summed(kept, last, sent)
+    scaled = (added(entry_terms) * own_gain[None]).astype(jnp.bfloat16)
+    near = [scaled] + to_pairs([scaled] * far)
+    last = to_neighbour(scaled)
+    queries, own_pair = depth_projections(
+        place, near, last, to_neighbour(jnp.stack(near[1:])), depth_gain, near_qkv
     )
     prior_pair = passed_along(own_pair, "section", 1)
-    partner_columns = to_neighbour(other_columns)
-    kept, *blocks = mixed_parts(place, queries, own_pair, prior_pair, near_out, far)
-    odd = tp_place % 2 == 1
-    none = jnp.zeros_like(entry)
-    total = kept + sum(block.astype(jnp.float32) for block in to_pairs(blocks))
-    total = total + jnp.concatenate([jnp.where(odd, none, entry), jnp.where(odd, entry, none)], axis=2)
+    chunks = mixed_parts(place, queries, own_pair, prior_pair, near_out, entry_terms, far)
     pair_gain = lax.dynamic_slice_in_dim(head_gain, tp_place // 2 * 2 * hidden_rows, 2 * hidden_rows, 0)
-    kept, stat, *blocks = head_parts(
-        place,
-        pair_gain.reshape(1, 1, -1),
-        total,
-        to_neighbour(total.astype(jnp.bfloat16)),
-        own_columns,
-        partner_columns,
-    )
-    logits = finished_logits(kept, stat, to_pairs(blocks), codes, width)
+    each = codes // CHUNKS
+    arrived = [to_pairs(blocks) for _, *blocks in chunks]
+    totals = [
+        kept + added(blocks) for (kept, *_), blocks in zip(chunks, arrived)
+    ]
+    others = [to_neighbour(total.astype(jnp.bfloat16)) for total in totals]
+    heads = [
+        head_parts(n * each, place, pair_gain.reshape(1, 1, -1), total, other, own, early, late)
+        for n, (total, other, own) in enumerate(zip(totals, others, own_columns))
+    ]
+    finished = [[kept, stat, *to_pairs(blocks)] for kept, stat, *blocks in heads]
+    logits = finished_logits(finished, sent.shape[2], codes, width)
     return (temporal, logits)
 
 
 def per_device(*arrays):
     hidden_in, temporal_qkv, depth_qkv, head_weight = arrays[0], arrays[2], arrays[10], arrays[13]
+    depth_in, tokens = arrays[7], arrays[14]
     tp = lax.axis_size("tp")
     pairs = hidden_in.shape[0] * (temporal_qkv.shape[2] // HEAD_DIM)
     whole_tiles = (
@@ -810,6 +863,9 @@
         and head_weight.shape[2] // tp % 128 == 0
         and depth_qkv.shape[3] % 128 == 0
         and tp >= 4
+        and depth_in.shape[0] % (2 * CHUNKS) == 0
+        and lax.axis_size("grp") % 2 == 0
+        and depth_in.shape[0] // CHUNKS * tokens.shape[0] <= head_weight.shape[2] // tp
         and tp & (tp - 1) == 0
     )
     return (paired_device if whole_tiles else general_device)(*arrays)

time: 106 us -> 102 us (0.962)
  waiting for transfers between devices: 45.4 us -> 38 us
  starting transfers between devices: 32.5 us -> 36.7 us
  other arithmetic: 1.97 us -> 0.31 us
    ppermute x5 -> x8, waiting for transfers between devices: 19.2 us -> 11.1 us  [to_neighbour(): return lax.ppermute(block, 'tp', [(i, i ^ 1) for i in range(tp)])]
    ppermute x5 -> x8, starting transfers between devices: 8.37 us -> 10.9 us  [to_neighbour(): return lax.ppermute(block, 'tp', [(i, i ^ 1) for i in range(tp)])]
    ppermute x15 -> x16, starting transfers between devices: 22.7 us -> 24.4 us  [the longest x15 22.8 us: to_pairs(): lax.ppermute(blocks[k], 'tp', [(i, i ^ 2 * (k + 1)) for i in range(tp)])]
    ppermute x15 -> x16, waiting for transfers between devices: 24 us -> 24.8 us  [the longest x15 24.8 us: to_pairs(): lax.ppermute(blocks[k], 'tp', [(i, i ^ 2 * (k + 1)) for i in range(tp)])]
    pallas_call x5 -> x6, Pallas kernels: 9.56 us -> 10.3 us  [the longest x1 3.09 us: brought_near(): pl.pallas_call(near_kernel, in_specs=[SMEM, VMEM, VMEM, HBM, HBM], out_sp...]
  transfers between devices with their start and end apart: 22 -> 26, of which waited for: 14 -> 14; matrix products, arithmetic and copies ran while one was open for 2% -> 1% of each run, Pallas kernels for 8% -> 11%
where the time goes in v4:
time: 102 us
  waiting for transfers between devices  38 us (37%)
  starting transfers between devices  36.7 us (36%)
  Pallas kernels  25.2 us (25%)
    ppermute x15, waiting for transfers between devices, to_pairs(): lax.ppermute(blocks[k], 'tp', [(i, i ^ 2 * (k + 1)) for i in range(tp)])  24.8 us
    ppermute x15, starting transfers between devices, to_pairs(): lax.ppermute(blocks[k], 'tp', [(i, i ^ 2 * (k + 1)) for i in range(tp)])  22.8 us
    ppermute x8, waiting for transfers between devices, to_neighbour(): return lax.ppermute(block, 'tp', [(i, i ^ 1) for i in range(tp)])  11.1 us
    ppermute x8, starting transfers between devices, to_neighbour(): return lax.ppermute(block, 'tp', [(i, i ^ 1) for i in range(tp)])  10.9 us
    pallas_call x1, Pallas kernels, temporal_parts(): pl.pallas_call(temporal_kernel, in_specs=[SMEM] + [HBM] * 7, out_specs=[V...  10.4 us
    pallas_call x1, Pallas kernels, prepared_entry(): pl.pallas_call(prepare_kernel, in_specs=[SMEM, VMEM, HBM, HBM, HBM], out_...  3.66 us
    pallas_call x1, Pallas kernels, brought_near(): pl.pallas_call(near_kernel, in_specs=[SMEM, VMEM, VMEM, HBM, HBM], out_sp...  3.09 us
    pallas_call x1, Pallas kernels, split_columns(): pl.pallas_call(split_kernel, in_specs=[SMEM, HBM], out_specs=[VMEM] * (1...  2.09 us
  transfers between devices with their start and end apart: 26, of which 14 were waited for; matrix products, arithmetic and copies ran while one was open for 1% of the time, Pallas kernels for 11%

profile of v4, /device:TPU:0, one launch (start us, length us, event | category | flops | bytes accessed | tf_op | source)
XLA Modules:
  0.0 102.0 jit_solution(8895891522966876274)
XLA Ops:
  0.7 10.4 %temporal.1 = (f32[4,32,512]{2,1,0:T(8,128)S(1)}, bf16[32,512]{1,0:T(8,128)(2,1)S(1)}, bf16[3,32,512]{2,1,0:T(8,128)(2,1)S(1)}) custom-call(s32[3]{0:T(128)S(1)} %pad_add_fusion.place_ref, bf16[32,4096]{1,0:T(8,128)(2,1)} %hidden_hbm.3, f32[1,4096]{1,0:T(1,128)} %bitcast.46, s32[1,32]{1,0:T(1,128)} %bitcast.47, bf16[3,4096,512]{2,1,0:T(8,128)(2,1)} %qkv_hbm.2, ...), custom_call_target="tpu_custom_call" | custom-call | tf_op jit(solution)/shard_map/temporal/pallas_call | solution.py:388
  11.1 3.0 %collective-permute-start = (bf16[3,32,512]{2,1,0:T(8,128)(2,1)S(1)}, bf16[3,32,512]{2,1,0:T(8,128)(2,1)S(1)}, u32[]{:S(2)}, u32[]{:S(2)}) collective-permute-start(bf16[3,32,512]{2,1,0:T(8,128)(2,1)S(1)} %get-tuple-element.35), channel_id=1, source_target_pairs={{0,2},{2,0},{4,6},{6,4},{8,10},{10,8},{12,14},{14,12},{1,3},{3,1},... | collective-permute-start | bytes 294920 | tf_op jit(solution)/shard_map/ppermute | solution.py:804
  14.2 2.1 %split_columns.1 = (bf16[4,2,128,256]{3,2,1,0:T(8,128)(2,1)S(1)}, bf16[4,4,128,256]{3,2,1,0:T(8,128)(2,1)S(1)}) custom-call(s32[3]{0:T(128)S(1)} %pad_add_fusion.place_ref, bf16[4,128,2048]{2,1,0:T(8,128)(2,1)} %head_hbm), custom_call_target="tpu_custom_call" | custom-call | tf_op jit(solution)/shard_map/split_columns/pallas_call | solution.py:522
  16.3 2.0 %collective-permute-start.6 = (bf16[4,2,128,256]{3,2,1,0:T(8,128)(2,1)S(1)}, bf16[4,2,128,256]{3,2,1,0:T(8,128)(2,1)S(1)}, u32[]{:S(2)}, u32[]{:S(2)}) collective-permute-start(bf16[4,2,128,256]{3,2,1,0:T(8,128)(2,1)S(1)} %get-tuple-element.40), channel_id=1, source_target_pairs={{0,2},{2,0},{4,6},{6,4},{8,10},{10,8},{12,14},{14,12},{1,3},{3,1},... | collective-permute-start | bytes 1572872 | tf_op jit(solution)/shard_map/ppermute | solution.py:804
  20.0 2.6 %collective-permute-start.2 = (bf16[32,512]{1,0:T(8,128)(2,1)S(1)}, bf16[32,512]{1,0:T(8,128)(2,1)S(1)}, u32[]{:S(2)}, u32[]{:S(2)}) collective-permute-start(bf16[32,512]{1,0:T(8,128)(2,1)S(1)} %get-tuple-element.67), channel_id=1, source_target_pairs={{0,8},{2,10},{4,12},{6,14},{8,0},{10,2},{12,4},{14,6},{1,9},{3,11}... | collective-permute-start | bytes 98312 | tf_op jit(solution)/shard_map/ppermute | solution.py:800
  23.0 3.7 %entry_prepare.1 = (bf16[32,512]{1,0:T(8,128)(2,1)S(1)}, f32[4,64,1024]{2,1,0:T(8,128)S(1)}, bf16[4,512,1024]{2,1,0:T(8,128)(2,1)S(1)}) custom-call(s32[3]{0:T(128)S(1)} %pad_add_fusion.place_ref, s32[64,4]{1,0:T(8,128)S(1)} %copy.17.tokens_ref, bf16[32,4096]{1,0:T(8,128)(2,1)} %hidden_hbm.3, bf16[4,256,1024]{2,1,0:T(8,128)(2,1)} %embed_hbm.1, ...), custom_call_target="tpu_custom_call" | custom-call | tf_op jit(solution)/shard_map/entry_prepare/pallas_call | solution.py:444
  26.7 1.7 %collective-permute-done.3 = bf16[32,512]{1,0:T(8,128)(2,1)S(1)} collective-permute-done((bf16[32,512]{1,0:T(8,128)(2,1)S(1)}, bf16[32,512]{1,0:T(8,128)(2,1)S(1)}, u32[]{:S(2)}, u32[]{:S(2)}) %collective-permute-start.3) | collective-permute-done | bytes 32800 | tf_op jit(solution)/shard_map/ppermute | solution.py:800
  31.3 1.7 %collective-permute-start.7 = (bf16[3,4,64,128]{3,2,1,0:T(8,128)(2,1)S(1)}, bf16[3,4,64,128]{3,2,1,0:T(8,128)(2,1)S(1)}, u32[]{:S(2)}, u32[]{:S(2)}) collective-permute-start(bf16[3,4,64,128]{3,2,1,0:T(8,128)(2,1)S(1)} %get-tuple-element.44), channel_id=1, source_target_pairs={{0,2},{2,0},{4,6},{6,4},{8,10},{10,8},{12,14},{14,12},{1,3},{3,1},... | collective-permute-start | bytes 589832 | tf_op jit(solution)/shard_map/ppermute | solution.py:804
  33.4 5.5 %collective-permute-done.7 = bf16[3,4,64,128]{3,2,1,0:T(8,128)(2,1)S(1)} collective-permute-done((bf16[3,4,64,128]{3,2,1,0:T(8,128)(2,1)S(1)}, bf16[3,4,64,128]{3,2,1,0:T(8,128)(2,1)S(1)}, u32[]{:S(2)}, u32[]{:S(2)}) %collective-permute-start.7) | collective-permute-done | bytes 196640 | tf_op jit(solution)/shard_map/ppermute | solution.py:804
  39.0 2.1 %collective-permute-start.10 = (bf16[4,64,128]{2,1,0:T(8,128)(2,1)S(1)}, bf16[4,64,128]{2,1,0:T(8,128)(2,1)S(1)}, u32[]{:S(2)}, u32[]{:S(2)}) collective-permute-start(bf16[4,64,128]{2,1,0:T(8,128)(2,1)S(1)} %get-tuple-element.63), channel_id=1, source_target_pairs={{0,12},{2,14},{4,8},{6,10},{8,4},{10,6},{12,0},{14,2},{1,13},{3,15... | collective-permute-start | bytes 196616 | tf_op jit(solution)/shard_map/ppermute | solution.py:800
  41.1 2.3 %collective-permute-start.9 = (bf16[4,64,128]{2,1,0:T(8,128)(2,1)S(1)}, bf16[4,64,128]{2,1,0:T(8,128)(2,1)S(1)}, u32[]{:S(2)}, u32[]{:S(2)}) collective-permute-start(bf16[4,64,128]{2,1,0:T(8,128)(2,1)S(1)} %get-tuple-element.64), channel_id=1, source_target_pairs={{0,8},{2,10},{4,12},{6,14},{8,0},{10,2},{12,4},{14,6},{1,9},{3,11}... | collective-permute-start | bytes 196616 | tf_op jit(solution)/shard_map/ppermute | solution.py:800
  43.4 3.1 %brought_near.1 = (f32[1,128]{1,0:T(1,128)S(1)}, bf16[4,3,1024,128]{3,2,1,0:T(8,128)(2,1)S(1)}, bf16[4,128,1024]{2,1,0:T(8,128)(2,1)S(1)}) custom-call(s32[3]{0:T(128)S(1)} %pad_add_fusion.place_ref, f32[8,128]{1,0:T(8,128)S(1)} %get-tuple-element.41.token_ref, f32[1,1024]{1,0:T(1,128)S(1)} %bitcast.42, bf16[4,3,1024,128]{3,2,1,0:T(8,128)(2,1)} %qkv_hbm.3, ...), custom_call_target="tpu_custom_call" | custom-call | tf_op jit(solution)/shard_map/brought_near/pallas_call | solution.py:478
  46.7 1.7 %collective-permute-start.12 = (bf16[4,64,128]{2,1,0:T(8,128)(2,1)S(1)}, bf16[4,64,128]{2,1,0:T(8,128)(2,1)S(1)}, u32[]{:S(2)}, u32[]{:S(2)}) collective-permute-start(bf16[4,64,128]{2,1,0:T(8,128)(2,1)S(1)} %multiply_convert_fusion.rest_0_), channel_id=1, source_target_pairs={{0,4},{2,6},{4,0},{6,2},{8,12},{10,14},{12,8},{14,10},{1,5},{3,7},... | collective-permute-start | bytes 196616 | tf_op jit(solution)/shard_map/ppermute | solution.py:800
  49.3 1.9 %collective-permute-start.14 = (bf16[4,64,128]{2,1,0:T(8,128)(2,1)S(1)}, bf16[4,64,128]{2,1,0:T(8,128)(2,1)S(1)}, u32[]{:S(2)}, u32[]{:S(2)}) collective-permute-start(bf16[4,64,128]{2,1,0:T(8,128)(2,1)S(1)} %multiply_convert_fusion.rest_0_), channel_id=1, source_target_pairs={{0,12},{2,14},{4,8},{6,10},{8,4},{10,6},{12,0},{14,2},{1,13},{3,15... | collective-permute-start | bytes 196616 | tf_op jit(solution)/shard_map/ppermute | solution.py:800
  51.2 3.3 %collective-permute-done.13.rest_2_ = bf16[4,64,128]{2,1,0:T(8,128)(2,1)S(1)} collective-permute-done((bf16[4,64,128]{2,1,0:T(8,128)(2,1)S(1)}, bf16[4,64,128]{2,1,0:T(8,128)(2,1)S(1)}, u32[]{:S(2)}, u32[]{:S(2)}) %collective-permute-start.13) | collective-permute-done | bytes 65568 | tf_op jit(solution)/shard_map/ppermute | solution.py:800
  59.2 2.8 %collective-permute-done.16.rest_4_ = bf16[4,64,128]{2,1,0:T(8,128)(2,1)S(1)} collective-permute-done((bf16[4,64,128]{2,1,0:T(8,128)(2,1)S(1)}, bf16[4,64,128]{2,1,0:T(8,128)(2,1)S(1)}, u32[]{:S(2)}, u32[]{:S(2)}) %collective-permute-start.16) | collective-permute-done | bytes 65568 | tf_op jit(solution)/shard_map/ppermute | solution.py:804
  69.3 2.0 %collective-permute-start.20 = (bf16[4,64,256]{2,1,0:T(8,128)(2,1)S(1)}, bf16[4,64,256]{2,1,0:T(8,128)(2,1)S(1)}, u32[]{:S(2)}, u32[]{:S(2)}) collective-permute-start(bf16[4,64,256]{2,1,0:T(8,128)(2,1)S(1)} %get-tuple-element.53), channel_id=1, source_target_pairs={{0,12},{2,14},{4,8},{6,10},{8,4},{10,6},{12,0},{14,2},{1,13},{3,15... | collective-permute-start | bytes 393224 | tf_op jit(solution)/shard_map/ppermute | solution.py:800
  71.3 3.3 %collective-permute-done.18 = bf16[4,64,256]{2,1,0:T(8,128)(2,1)S(1)} collective-permute-done((bf16[4,64,256]{2,1,0:T(8,128)(2,1)S(1)}, bf16[4,64,256]{2,1,0:T(8,128)(2,1)S(1)}, u32[]{:S(2)}, u32[]{:S(2)}) %collective-permute-start.18) | collective-permute-done | bytes 131104 | tf_op jit(solution)/shard_map/ppermute | solution.py:800
  74.5 6.2 %collective-permute-done.19 = bf16[4,64,256]{2,1,0:T(8,128)(2,1)S(1)} collective-permute-done((bf16[4,64,256]{2,1,0:T(8,128)(2,1)S(1)}, bf16[4,64,256]{2,1,0:T(8,128)(2,1)S(1)}, u32[]{:S(2)}, u32[]{:S(2)}) %collective-permute-start.19) | collective-permute-done | bytes 131104 | tf_op jit(solution)/shard_map/ppermute | solution.py:800
  83.2 2.7 %collective-permute-done.21.arrived_ref = bf16[4,64,256]{2,1,0:T(8,128)(2,1)S(1)} collective-permute-done((bf16[4,64,256]{2,1,0:T(8,128)(2,1)S(1)}, bf16[4,64,256]{2,1,0:T(8,128)(2,1)S(1)}, u32[]{:S(2)}, u32[]{:S(2)}) %collective-permute-start.21) | collective-permute-done | bytes 131104 | tf_op jit(solution)/shard_map/ppermute | solution.py:804
  86.9 2.6 %collective-permute-start.23 = (bf16[272,256]{1,0:T(8,128)(2,1)S(1)}, bf16[272,256]{1,0:T(8,128)(2,1)S(1)}, u32[]{:S(2)}, u32[]{:S(2)}) collective-permute-start(bf16[272,256]{1,0:T(8,128)(2,1)S(1)} %get-tuple-element.57), channel_id=1, source_target_pairs={{0,4},{2,6},{4,0},{6,2},{8,12},{10,14},{12,8},{14,10},{1,5},{3,7},... | collective-permute-start | bytes 417800 | tf_op jit(solution)/shard_map/ppermute | solution.py:800
  89.7 2.2 %collective-permute-start.25 = (bf16[272,256]{1,0:T(8,128)(2,1)S(1)}, bf16[272,256]{1,0:T(8,128)(2,1)S(1)}, u32[]{:S(2)}, u32[]{:S(2)}) collective-permute-start(bf16[272,256]{1,0:T(8,128)(2,1)S(1)} %get-tuple-element.59), channel_id=1, source_target_pairs={{0,12},{2,14},{4,8},{6,10},{8,4},{10,6},{12,0},{14,2},{1,13},{3,15... | collective-permute-start | bytes 417800 | tf_op jit(solution)/shard_map/ppermute | solution.py:800
  91.9 1.7 %collective-permute-done.23.refs_2_ = bf16[272,256]{1,0:T(8,128)(2,1)S(1)} collective-permute-done((bf16[272,256]{1,0:T(8,128)(2,1)S(1)}, bf16[272,256]{1,0:T(8,128)(2,1)S(1)}, u32[]{:S(2)}, u32[]{:S(2)}) %collective-permute-start.23) | collective-permute-done | bytes 139296 | tf_op jit(solution)/shard_map/ppermute | solution.py:800
  93.6 7.5 %collective-permute-done.24.refs_3_ = bf16[272,256]{1,0:T(8,128)(2,1)S(1)} collective-permute-done((bf16[272,256]{1,0:T(8,128)(2,1)S(1)}, bf16[272,256]{1,0:T(8,128)(2,1)S(1)}, u32[]{:S(2)}, u32[]{:S(2)}) %collective-permute-start.24) | collective-permute-done | bytes 139296 | tf_op jit(solution)/shard_map/ppermute | solution.py:800
  (55 shorter events, 23.3 us)
Async XLA Ops:
  11.1 7.2 %collective-permute-start = (bf16[3,32,512]{2,1,0:T(8,128)(2,1)S(1)}, bf16[3,32,512]{2,1,0:T(8,128)(2,1)S(1)}, u32[]{:S(2)}, u32[]{:S(2)}) collective-permute-start(bf16[3,32,512]{2,1,0:T(8,128)(2,1)S(1)} %get-tuple-element.35), channel_id=1, source_target_pairs={{0,2},{2,0},{4,6},{6,4},{8,10},{10,8},{12,14},{14,12},{1,3},{3,1},... | collective-permute-start | bytes 294920 | tf_op jit(solution)/shard_map/ppermute | solution.py:804
  14.2 12.5 %collective-permute-start.4 = (bf16[32,512]{1,0:T(8,128)(2,1)S(1)}, bf16[32,512]{1,0:T(8,128)(2,1)S(1)}, u32[]{:S(2)}, u32[]{:S(2)}) collective-permute-start(bf16[32,512]{1,0:T(8,128)(2,1)S(1)} %get-tuple-element.36), channel_id=1, source_target_pairs={{0,2},{2,0},{4,6},{6,4},{8,10},{10,8},{12,14},{14,12},{1,3},{3,1},... | collective-permute-start | bytes 98312 | tf_op jit(solution)/shard_map/ppermute | solution.py:804
  16.3 13.4 %collective-permute-start.6 = (bf16[4,2,128,256]{3,2,1,0:T(8,128)(2,1)S(1)}, bf16[4,2,128,256]{3,2,1,0:T(8,128)(2,1)S(1)}, u32[]{:S(2)}, u32[]{:S(2)}) collective-permute-start(bf16[4,2,128,256]{3,2,1,0:T(8,128)(2,1)S(1)} %get-tuple-element.40), channel_id=1, source_target_pairs={{0,2},{2,0},{4,6},{6,4},{8,10},{10,8},{12,14},{14,12},{1,3},{3,1},... | collective-permute-start | bytes 1572872 | tf_op jit(solution)/shard_map/ppermute | solution.py:804
  18.4 8.2 %collective-permute-start.1 = (bf16[32,512]{1,0:T(8,128)(2,1)S(1)}, bf16[32,512]{1,0:T(8,128)(2,1)S(1)}, u32[]{:S(2)}, u32[]{:S(2)}) collective-permute-start(bf16[32,512]{1,0:T(8,128)(2,1)S(1)} %get-tuple-element.65), channel_id=1, source_target_pairs={{0,4},{2,6},{4,0},{6,2},{8,12},{10,14},{12,8},{14,10},{1,5},{3,7},... | collective-permute-start | bytes 98312 | tf_op jit(solution)/shard_map/ppermute | solution.py:800
  20.0 6.6 %collective-permute-start.2 = (bf16[32,512]{1,0:T(8,128)(2,1)S(1)}, bf16[32,512]{1,0:T(8,128)(2,1)S(1)}, u32[]{:S(2)}, u32[]{:S(2)}) collective-permute-start(bf16[32,512]{1,0:T(8,128)(2,1)S(1)} %get-tuple-element.67), channel_id=1, source_target_pairs={{0,8},{2,10},{4,12},{6,14},{8,0},{10,2},{12,4},{14,6},{1,9},{3,11}... | collective-permute-start | bytes 98312 | tf_op jit(solution)/shard_map/ppermute | solution.py:800
  22.6 5.7 %collective-permute-start.3 = (bf16[32,512]{1,0:T(8,128)(2,1)S(1)}, bf16[32,512]{1,0:T(8,128)(2,1)S(1)}, u32[]{:S(2)}, u32[]{:S(2)}) collective-permute-start(bf16[32,512]{1,0:T(8,128)(2,1)S(1)} %get-tuple-element.66), channel_id=1, source_target_pairs={{0,12},{2,14},{4,8},{6,10},{8,4},{10,6},{12,0},{14,2},{1,13},{3,15... | collective-permute-start | bytes 98312 | tf_op jit(solution)/shard_map/ppermute | solution.py:800
  31.3 7.6 %collective-permute-start.7 = (bf16[3,4,64,128]{3,2,1,0:T(8,128)(2,1)S(1)}, bf16[3,4,64,128]{3,2,1,0:T(8,128)(2,1)S(1)}, u32[]{:S(2)}, u32[]{:S(2)}) collective-permute-start(bf16[3,4,64,128]{3,2,1,0:T(8,128)(2,1)S(1)} %get-tuple-element.44), channel_id=1, source_target_pairs={{0,2},{2,0},{4,6},{6,4},{8,10},{10,8},{12,14},{14,12},{1,3},{3,1},... | collective-permute-start | bytes 589832 | tf_op jit(solution)/shard_map/ppermute | solution.py:804
  33.0 13.5 %collective-permute-start.11 = (bf16[4,64,128]{2,1,0:T(8,128)(2,1)S(1)}, bf16[4,64,128]{2,1,0:T(8,128)(2,1)S(1)}, u32[]{:S(2)}, u32[]{:S(2)}) collective-permute-start(bf16[4,64,128]{2,1,0:T(8,128)(2,1)S(1)} %get-tuple-element.45), channel_id=1, source_target_pairs={{0,2},{2,0},{4,6},{6,4},{8,10},{10,8},{12,14},{14,12},{1,3},{3,1},... | collective-permute-start | bytes 196616 | tf_op jit(solution)/shard_map/ppermute | solution.py:804
  39.0 7.6 %collective-permute-start.10 = (bf16[4,64,128]{2,1,0:T(8,128)(2,1)S(1)}, bf16[4,64,128]{2,1,0:T(8,128)(2,1)S(1)}, u32[]{:S(2)}, u32[]{:S(2)}) collective-permute-start(bf16[4,64,128]{2,1,0:T(8,128)(2,1)S(1)} %get-tuple-element.63), channel_id=1, source_target_pairs={{0,12},{2,14},{4,8},{6,10},{8,4},{10,6},{12,0},{14,2},{1,13},{3,15... | collective-permute-start | bytes 196616 | tf_op jit(solution)/shard_map/ppermute | solution.py:800
  41.1 5.6 %collective-permute-start.8 = (bf16[4,64,128]{2,1,0:T(8,128)(2,1)S(1)}, bf16[4,64,128]{2,1,0:T(8,128)(2,1)S(1)}, u32[]{:S(2)}, u32[]{:S(2)}) collective-permute-start(bf16[4,64,128]{2,1,0:T(8,128)(2,1)S(1)} %get-tuple-element.62), channel_id=1, source_target_pairs={{0,4},{2,6},{4,0},{6,2},{8,12},{10,14},{12,8},{14,10},{1,5},{3,7},... | collective-permute-start | bytes 196616 | tf_op jit(solution)/shard_map/ppermute | solution.py:800
  41.1 5.6 %collective-permute-start.9 = (bf16[4,64,128]{2,1,0:T(8,128)(2,1)S(1)}, bf16[4,64,128]{2,1,0:T(8,128)(2,1)S(1)}, u32[]{:S(2)}, u32[]{:S(2)}) collective-permute-start(bf16[4,64,128]{2,1,0:T(8,128)(2,1)S(1)} %get-tuple-element.64), channel_id=1, source_target_pairs={{0,8},{2,10},{4,12},{6,14},{8,0},{10,2},{12,4},{14,6},{1,9},{3,11}... | collective-permute-start | bytes 196616 | tf_op jit(solution)/shard_map/ppermute | solution.py:800
  46.7 4.5 %collective-permute-start.12 = (bf16[4,64,128]{2,1,0:T(8,128)(2,1)S(1)}, bf16[4,64,128]{2,1,0:T(8,128)(2,1)S(1)}, u32[]{:S(2)}, u32[]{:S(2)}) collective-permute-start(bf16[4,64,128]{2,1,0:T(8,128)(2,1)S(1)} %multiply_convert_fusion.rest_0_), channel_id=1, source_target_pairs={{0,4},{2,6},{4,0},{6,2},{8,12},{10,14},{12,8},{14,10},{1,5},{3,7},... | collective-permute-start | bytes 196616 | tf_op jit(solution)/shard_map/ppermute | solution.py:800
  48.4 6.0 %collective-permute-start.13 = (bf16[4,64,128]{2,1,0:T(8,128)(2,1)S(1)}, bf16[4,64,128]{2,1,0:T(8,128)(2,1)S(1)}, u32[]{:S(2)}, u32[]{:S(2)}) collective-permute-start(bf16[4,64,128]{2,1,0:T(8,128)(2,1)S(1)} %multiply_convert_fusion.rest_0_), channel_id=1, source_target_pairs={{0,8},{2,10},{4,12},{6,14},{8,0},{10,2},{12,4},{14,6},{1,9},{3,11}... | collective-permute-start | bytes 196616 | tf_op jit(solution)/shard_map/ppermute | solution.py:800
  49.3 6.2 %collective-permute-start.14 = (bf16[4,64,128]{2,1,0:T(8,128)(2,1)S(1)}, bf16[4,64,128]{2,1,0:T(8,128)(2,1)S(1)}, u32[]{:S(2)}, u32[]{:S(2)}) collective-permute-start(bf16[4,64,128]{2,1,0:T(8,128)(2,1)S(1)} %multiply_convert_fusion.rest_0_), channel_id=1, source_target_pairs={{0,12},{2,14},{4,8},{6,10},{8,4},{10,6},{12,0},{14,2},{1,13},{3,15... | collective-permute-start | bytes 196616 | tf_op jit(solution)/shard_map/ppermute | solution.py:800
  55.5 6.4 %collective-permute-start.15 = (bf16[3,4,64,128]{3,2,1,0:T(8,128)(2,1)S(1)}, bf16[3,4,64,128]{3,2,1,0:T(8,128)(2,1)S(1)}, u32[]{:S(2)}, u32[]{:S(2)}) collective-permute-start(bf16[3,4,64,128]{3,2,1,0:T(8,128)(2,1)S(1)} %pad_maximum_fusion), channel_id=1, source_target_pairs={{0,2},{2,0},{4,6},{6,4},{8,10},{10,8},{12,14},{14,12},{1,3},{3,1},... | collective-permute-start | bytes 589832 | tf_op jit(solution)/shard_map/ppermute | solution.py:804
  57.1 4.8 %collective-permute-start.16 = (bf16[4,64,128]{2,1,0:T(8,128)(2,1)S(1)}, bf16[4,64,128]{2,1,0:T(8,128)(2,1)S(1)}, u32[]{:S(2)}, u32[]{:S(2)}) collective-permute-start(bf16[4,64,128]{2,1,0:T(8,128)(2,1)S(1)} %multiply_convert_fusion.rest_0_), channel_id=1, source_target_pairs={{0,2},{2,0},{4,6},{6,4},{8,10},{10,8},{12,14},{14,12},{1,3},{3,1},... | collective-permute-start | bytes 196616 | tf_op jit(solution)/shard_map/ppermute | solution.py:804
  57.6 25.6 %collective-permute-start.22 = (bf16[4,2,128,256]{3,2,1,0:T(8,128)(2,1)S(1)}, bf16[4,2,128,256]{3,2,1,0:T(8,128)(2,1)S(1)}, u32[]{:S(2)}, u32[]{:S(2)}) collective-permute-start(bf16[4,2,128,256]{3,2,1,0:T(8,128)(2,1)S(1)} %collective-permute-done.6.after_ref.early_ref), channel_id=1, source_target_pairs={{0,16},{16,0},{1,17},{17,1},{2,18},{18,2},{3,19},{19,3},{4,20},{20... | collective-permute-start | bytes 1572872 | tf_op jit(solution)/shard_map/ppermute | solution.py:827
  66.8 7.7 %collective-permute-start.18 = (bf16[4,64,256]{2,1,0:T(8,128)(2,1)S(1)}, bf16[4,64,256]{2,1,0:T(8,128)(2,1)S(1)}, u32[]{:S(2)}, u32[]{:S(2)}) collective-permute-start(bf16[4,64,256]{2,1,0:T(8,128)(2,1)S(1)} %get-tuple-element.51), channel_id=1, source_target_pairs={{0,4},{2,6},{4,0},{6,2},{8,12},{10,14},{12,8},{14,10},{1,5},{3,7},... | collective-permute-start | bytes 393224 | tf_op jit(solution)/shard_map/ppermute | solution.py:800
  67.8 12.9 %collective-permute-start.19 = (bf16[4,64,256]{2,1,0:T(8,128)(2,1)S(1)}, bf16[4,64,256]{2,1,0:T(8,128)(2,1)S(1)}, u32[]{:S(2)}, u32[]{:S(2)}) collective-permute-start(bf16[4,64,256]{2,1,0:T(8,128)(2,1)S(1)} %get-tuple-element.52), channel_id=1, source_target_pairs={{0,8},{2,10},{4,12},{6,14},{8,0},{10,2},{12,4},{14,6},{1,9},{3,11}... | collective-permute-start | bytes 393224 | tf_op jit(solution)/shard_map/ppermute | solution.py:800
  69.3 11.4 %collective-permute-start.20 = (bf16[4,64,256]{2,1,0:T(8,128)(2,1)S(1)}, bf16[4,64,256]{2,1,0:T(8,128)(2,1)S(1)}, u32[]{:S(2)}, u32[]{:S(2)}) collective-permute-start(bf16[4,64,256]{2,1,0:T(8,128)(2,1)S(1)} %get-tuple-element.53), channel_id=1, source_target_pairs={{0,12},{2,14},{4,8},{6,10},{8,4},{10,6},{12,0},{14,2},{1,13},{3,15... | collective-permute-start | bytes 393224 | tf_op jit(solution)/shard_map/ppermute | solution.py:800
  80.8 5.0 %collective-permute-start.21 = (bf16[4,64,256]{2,1,0:T(8,128)(2,1)S(1)}, bf16[4,64,256]{2,1,0:T(8,128)(2,1)S(1)}, u32[]{:S(2)}, u32[]{:S(2)}) collective-permute-start(bf16[4,64,256]{2,1,0:T(8,128)(2,1)S(1)} %get-tuple-element.60), channel_id=1, source_target_pairs={{0,2},{2,0},{4,6},{6,4},{8,10},{10,8},{12,14},{14,12},{1,3},{3,1},... | collective-permute-start | bytes 393224 | tf_op jit(solution)/shard_map/ppermute | solution.py:804
  86.9 6.7 %collective-permute-start.23 = (bf16[272,256]{1,0:T(8,128)(2,1)S(1)}, bf16[272,256]{1,0:T(8,128)(2,1)S(1)}, u32[]{:S(2)}, u32[]{:S(2)}) collective-permute-start(bf16[272,256]{1,0:T(8,128)(2,1)S(1)} %get-tuple-element.57), channel_id=1, source_target_pairs={{0,4},{2,6},{4,0},{6,2},{8,12},{10,14},{12,8},{14,10},{1,5},{3,7},... | collective-permute-start | bytes 417800 | tf_op jit(solution)/shard_map/ppermute | solution.py:800
  89.4 11.6 %collective-permute-start.24 = (bf16[272,256]{1,0:T(8,128)(2,1)S(1)}, bf16[272,256]{1,0:T(8,128)(2,1)S(1)}, u32[]{:S(2)}, u32[]{:S(2)}) collective-permute-start(bf16[272,256]{1,0:T(8,128)(2,1)S(1)} %get-tuple-element.58), channel_id=1, source_target_pairs={{0,8},{2,10},{4,12},{6,14},{8,0},{10,2},{12,4},{14,6},{1,9},{3,11}... | collective-permute-start | bytes 417800 | tf_op jit(solution)/shard_map/ppermute | solution.py:800
  89.7 11.3 %collective-permute-start.25 = (bf16[272,256]{1,0:T(8,128)(2,1)S(1)}, bf16[272,256]{1,0:T(8,128)(2,1)S(1)}, u32[]{:S(2)}, u32[]{:S(2)}) collective-permute-start(bf16[272,256]{1,0:T(8,128)(2,1)S(1)} %get-tuple-element.59), channel_id=1, source_target_pairs={{0,12},{2,14},{4,8},{6,10},{8,4},{10,6},{12,0},{14,2},{1,13},{3,15... | collective-permute-start | bytes 417800 | tf_op jit(solution)/shard_map/ppermute | solution.py:800
  (5 other events, 49.9 us)

commit v5 on v4

--- a/solution.py
+++ b/solution.py
@@ -231,7 +231,6 @@
 
 
 IN_FLIGHT = 6
-IN_FLIGHT_BESIDE = 6
 CHUNKS = 1
 
 
@@ -252,8 +251,8 @@
 
 
 def temporal_kernel(
-    place_ref, hidden_hbm, gain_hbm, lengths_hbm, qkv_hbm, out_hbm, keys_hbm, values_hbm, kept_ref, last_ref, sent_ref,
-    hidden_buf, gain_buf, lengths_buf, qkv_buf, out_buf, keys_buf, values_buf, small_sems, sems,
+    place_ref, hidden_hbm, gain_hbm, lengths_hbm, qkv_hbm, out_hbm, keys_hbm, values_hbm, head_hbm, kept_ref, last_ref, sent_ref, columns_ref,
+    hidden_buf, gain_buf, lengths_buf, qkv_buf, out_buf, keys_buf, values_buf, small_sems, sems, column_sems,
 ):
     streams, depth = hidden_buf.shape
     cols = qkv_buf.shape[2]
@@ -282,6 +281,12 @@
         (out_hbm.at[:, pl.ds(pl.multiple_of((place ^ k) * 2 * width, 2 * width), 2 * width)], out_buf.at[k])
         for k in range(count)
     ]
+    _, half_codes, _, part = columns_ref.shape
+    columns = []
+    for k in range(count):
+        start = pl.multiple_of(((place ^ k) * 2 + 1 - odd) * part, part)
+        source = head_hbm.at[pl.ds(place_ref[2] * half_codes, half_codes), :, pl.ds(start, part)]
+        columns.append(pltpu.make_async_copy(source, columns_ref.at[k], column_sems.at[k]))
     stream = Stream([pltpu.make_async_copy(src, dst, sems.at[i]) for i, (src, dst) in enumerate(pairs)], IN_FLIGHT)
     first_of = (0, steps, 2 * steps + halves)
     keys_end = 2 * steps + halves - 1
@@ -318,6 +323,8 @@
         return jnp.concatenate(pieces, axis=1)
 
     queries = rotated(projected(0))
+    for copy in columns:
+        copy.start()
     keys_new = rotated(projected(1)).astype(jnp.bfloat16)
     head_lane = lax.broadcasted_iota(jnp.int32, (streams, cols), 1) // HEAD_DIM
     spread = jnp.concatenate(
@@ -364,6 +371,8 @@
             mixed_all[h * streams : (h + 1) * streams, lanes] + own_col * values_new[:, lanes]
         )
     mixed = jnp.concatenate(mixed, axis=1).astype(jnp.bfloat16)
+    for copy in columns:
+        copy.wait()
     for k in range(count):
         stream.arrived(values_end + 1 + k)
         block = product(mixed, out_buf[k])
@@ -380,16 +389,22 @@
 CACHE_STEPS = 2
 
 
-def temporal_parts(place, hidden_in, gain, lengths, qkv, out_weight, keys, values, places):
+def temporal_parts(place, hidden_in, gain, lengths, qkv, out_weight, keys, values, head_weight, places):
+    codes, head_depth, vocab = head_weight.shape
     streams, depth = hidden_in.shape
     bf16 = jnp.bfloat16
     count, width = places // 2, out_weight.shape[1] // places
     block = (count, streams, width)
     return pl.pallas_call(
         temporal_kernel,
-        in_specs=[SMEM] + [HBM] * 7,
-        out_specs=[VMEM] * 3,
-        out_shape=[vmem(block, jnp.float32), vmem(block[1:], bf16), vmem((count - 1,) + block[1:], bf16)],
+        in_specs=[SMEM] + [HBM] * 8,
+        out_specs=[VMEM] * 4,
+        out_shape=[
+            vmem(block, jnp.float32),
+            vmem(block[1:], bf16),
+            vmem((count - 1,) + block[1:], bf16),
+            vmem((count, codes // 2, head_depth, vocab // places), bf16),
+        ],
         scratch_shapes=[
             pltpu.VMEM(hidden_in.shape, bf16),
             pltpu.VMEM((1, depth), jnp.float32),
@@ -400,6 +415,7 @@
             pltpu.VMEM(values.shape, bf16),
             pltpu.SemaphoreType.DMA((3,)),
             pltpu.SemaphoreType.DMA((3 * QKV_STEPS + 2 * CACHE_STEPS + count,)),
+            pltpu.SemaphoreType.DMA((count,)),
         ],
         compiler_params=params(30),
         name="temporal",
@@ -412,6 +428,7 @@
         in_hbm(out_weight),
         in_hbm(keys),
         in_hbm(values),
+        in_hbm(head_weight),
     )
 
 
@@ -426,7 +443,7 @@
     resid.start()
     embed = [pltpu.make_async_copy(embed_hbm.at[c], embed_buf.at[c], sems.at[0, c]) for c in range(codes)]
     weight = [pltpu.make_async_copy(weight_hbm.at[c], weight_ref.at[c], sems.at[1, c]) for c in range(codes)]
-    stream = Stream(embed + weight, IN_FLIGHT_BESIDE)
+    stream = Stream(embed + weight, IN_FLIGHT)
     vocab_lane = lax.broadcasted_iota(jnp.int32, (streams, vocab), 1) + place_ref[0] * vocab
     for c in range(codes):
         hit = tokens_ref[:, c : c + 1] == vocab_lane
@@ -460,74 +477,47 @@
     )(place, tokens, in_hbm(hidden_in), in_hbm(embed), in_hbm(weight))
 
 
-def near_kernel(place_ref, token_ref, gain_ref, qkv_hbm, out_hbm, own_ref, qkv_ref, out_ref, sems):
+def near_kernel(place_ref, token_ref, gain_ref, qkv_hbm, out_hbm, head_hbm, own_ref, qkv_ref, out_ref, *rest):
+    column_refs, (sems, column_sems) = rest[:-2], rest[-2:]
     del token_ref
     copies = [
         pltpu.make_async_copy(source.at[c], target.at[c], sems.at[i, c])
         for i, (source, target) in enumerate(((qkv_hbm, qkv_ref), (out_hbm, out_ref)))
         for c in range(source.shape[0])
     ]
-    stream = Stream(copies, IN_FLIGHT_BESIDE)
+    for n, out in enumerate(column_refs):
+        count, codes, _, vocab_part = out.shape
+        for k in range(count):
+            start = pl.multiple_of(((place_ref[0] // 2 ^ k) * 2 + place_ref[0] % 2) * vocab_part, vocab_part)
+            source = head_hbm.at[pl.ds(n * codes, codes), :, pl.ds(start, vocab_part)]
+            copies.append(pltpu.make_async_copy(source, out.at[k], column_sems.at[n, k]))
+    stream = Stream(copies, IN_FLIGHT)
     part = own_ref.shape[1]
     own_ref[...] = gain_ref[:, pl.ds(pl.multiple_of(place_ref[0] * part, part), part)]
     stream.arrived(len(copies) - 1)
 
 
-def brought_near(place, token, gain, qkv, out_weight, places):
+def brought_near(place, token, gain, qkv, out_weight, head_weight, places):
     width = gain.shape[0]
+    codes, depth, vocab = head_weight.shape
+    columns = vmem((places // 2, codes // CHUNKS, depth, vocab // places), jnp.bfloat16)
     return pl.pallas_call(
         near_kernel,
-        in_specs=[SMEM, VMEM, VMEM, HBM, HBM],
-        out_specs=[VMEM] * 3,
+        in_specs=[SMEM, VMEM, VMEM, HBM, HBM, HBM],
+        out_specs=[VMEM] * (3 + CHUNKS),
         out_shape=[
             vmem((1, width // places), jnp.float32),
             vmem(qkv.shape, jnp.bfloat16),
             vmem(out_weight.shape, jnp.bfloat16),
+        ]
+        + [columns] * CHUNKS,
+        scratch_shapes=[
+            pltpu.SemaphoreType.DMA((2, qkv.shape[0])),
+            pltpu.SemaphoreType.DMA((CHUNKS, places // 2)),
         ],
-        scratch_shapes=[pltpu.SemaphoreType.DMA((2, qkv.shape[0]))],
         compiler_params=params(16),
         name="brought_near",
-    )(place, token, gain.reshape(1, width), in_hbm(qkv), in_hbm(out_weight))
-
-
-def split_kernel(place_ref, head_hbm, far_ref, *rest):
-    outs, sems = rest[:-1], rest[-1]
-    count, half, _, part = far_ref.shape
-    each = outs[0].shape[1]
-    odd = place_ref[0] % 2
-    place = place_ref[0] // 2
-    blocks = [(far_ref, place_ref[2] * half, half, 1 - odd)]
-    blocks += [(out, n * each, each, odd) for n, out in enumerate(outs)]
-    copies = []
-    for n, (out, first, size, side) in enumerate(blocks):
-        for k in range(count):
-            start = pl.multiple_of(((place ^ k) * 2 + side) * part, part)
-            copies.append(
-                pltpu.make_async_copy(
-                    head_hbm.at[pl.ds(first, size), :, pl.ds(start, part)], out.at[k], sems.at[n, k]
-                )
-            )
-    for copy in copies:
-        copy.start()
-    for copy in copies:
-        copy.wait()
-
-
-def split_columns(place, weight, places):
-    codes, depth, vocab = weight.shape
-
-    def block(size):
-        return vmem((places // 2, size, depth, vocab // places), jnp.bfloat16)
-
-    return pl.pallas_call(
-        split_kernel,
-        in_specs=[SMEM, HBM],
-        out_specs=[VMEM] * (1 + CHUNKS),
-        out_shape=[block(codes // 2)] + [block(codes // CHUNKS)] * CHUNKS,
-        scratch_shapes=[pltpu.SemaphoreType.DMA((1 + CHUNKS, places // 2))],
-        compiler_params=params(16),
-        name="split_columns",
-    )(place, in_hbm(weight))
+    )(place, token, gain.reshape(1, width), in_hbm(qkv), in_hbm(out_weight), in_hbm(head_weight))
 
 
 def entry_kernel(place_ref, own_ref, other_ref, embedded_ref, weight_ref, after_ref, kept_ref, last_ref, sent_ref, token_ref, total_buf):
@@ -574,15 +564,18 @@
     )(place, own, other, embedded, weight, after)
 
 
+def nearest_last(far):
+    return list(range(1, far)) + [0]
+
+
 def qkv_kernel(count, place_ref, gain_ref, weight_ref, far_ref, *rest):
     near_refs, (last_ref, queries_ref, pair_ref) = rest[:count], rest[count:]
     codes, _, width, cols = weight_ref.shape
     part = last_ref.shape[2]
     odd = place_ref[0] % 2
     place = place_ref[0] // 2
-    starts = [
-        pl.multiple_of(((place ^ k) * 2 + side) * part, part) for side in (odd, 1 - odd) for k in range(count)
-    ]
+    order = [0] + [k + 1 for k in nearest_last(count - 1)]
+    starts = [pl.multiple_of(((place ^ k) * 2 + side) * part, part) for side in (odd, 1 - odd) for k in order]
     inverse_gain = 1.0 / jnp.concatenate([gain_ref[:, pl.ds(start, part)] for start in starts], axis=1)
     for c in range(codes):
         blocks = [ref[c] for ref in near_refs] + [last_ref[c]] + [far_ref[k, c] for k in range(count - 1)]
@@ -800,35 +793,50 @@
             arrived[k] = lax.ppermute(blocks[k], "tp", [(i, i ^ 2 * (k + 1)) for i in range(tp)])
         return arrived
 
+    order = nearest_last(far)
+
+    def in_order(blocks, order):
+        return [blocks[k] for k in order]
+
     def to_neighbour(block):
         return lax.ppermute(block, "tp", [(i, i ^ 1) for i in range(tp)])
 
-    def summed(kept, last, sent):
+    def summed(kept, last, sent, order):
         folded = kept[1:] + to_neighbour(sent).astype(jnp.float32)
         arrived = to_pairs([folded[k].astype(jnp.bfloat16) for k in range(far)])
-        return [kept[0]] + arrived + [to_neighbour(last)]
+        return [kept[0]] + [arrived[k] for k in order] + [to_neighbour(last)]
 
     def added(terms):
         return sum(term.astype(jnp.float32) for term in terms)
 
-    kept, last, sent = temporal_parts(
-        place, hidden_in, temporal_gain, lengths, temporal_qkv, temporal_out_weight, cache_keys, cache_values, tp
-    )
-    sent, depth_in, head_weight = lax.optimization_barrier((sent, depth_in, head_weight))
-    neighbour_columns, *own_columns = split_columns(place, head_weight, tp)
+    kept, last, sent, neighbour_columns = temporal_parts(
+        place,
+        hidden_in,
+        temporal_gain,
+        lengths,
+        temporal_qkv,
+        temporal_out_weight,
+        cache_keys,
+        cache_values,
+        head_weight,
+        tp,
+    )
+    sent, depth_in = lax.optimization_barrier((sent, depth_in))
     early = to_neighbour(neighbour_columns)
     resid_in, embedded, near_in = prepared_entry(place, tokens, hidden_in, depth_embed, depth_in, tp)
-    temporal = (resid_in.astype(jnp.float32) + added(summed(kept, last, sent))).astype(jnp.bfloat16)
+    temporal = (resid_in.astype(jnp.float32) + added(summed(kept, last, sent, order))).astype(jnp.bfloat16)
     other_rows = lax.ppermute(temporal, "section", [(0, 1), (1, 0)])
     codes = depth_in.shape[0]
     width = depth_in.shape[2]
     hidden_rows = head_weight.shape[1]
     kept, last, sent, token = entry_parts(place, temporal, other_rows, embedded, near_in, early, tp)
     late = lax.ppermute(early, "grp", [(i, i ^ 1) for i in range(lax.axis_size("grp"))])
-    own_gain, near_qkv, near_out = brought_near(place, token, depth_gain, depth_qkv, depth_out_weight, tp)
-    entry_terms = summed(kept, last, sent)
+    own_gain, near_qkv, near_out, *own_columns = brought_near(
+        place, token, depth_gain, depth_qkv, depth_out_weight, head_weight, tp
+    )
+    entry_terms = summed(kept, last, sent, order)
     scaled = (added(entry_terms) * own_gain[None]).astype(jnp.bfloat16)
-    near = [scaled] + to_pairs([scaled] * far)
+    near = [scaled] + in_order(to_pairs([scaled] * far), order)
     last = to_neighbour(scaled)
     queries, own_pair = depth_projections(
         place, near, last, to_neighbour(jnp.stack(near[1:])), depth_gain, near_qkv
@@ -837,7 +845,7 @@
     chunks = mixed_parts(place, queries, own_pair, prior_pair, near_out, entry_terms, far)
     pair_gain = lax.dynamic_slice_in_dim(head_gain, tp_place // 2 * 2 * hidden_rows, 2 * hidden_rows, 0)
     each = codes // CHUNKS
-    arrived = [to_pairs(blocks) for _, *blocks in chunks]
+    arrived = [in_order(to_pairs(blocks), order) for _, *blocks in chunks]
     totals = [
         kept + added(blocks) for (kept, *_), blocks in zip(chunks, arrived)
     ]
@@ -846,7 +854,7 @@
         head_parts(n * each, place, pair_gain.reshape(1, 1, -1), total, other, own, early, late)
         for n, (total, other, own) in enumerate(zip(totals, others, own_columns))
     ]
-    finished = [[kept, stat, *to_pairs(blocks)] for kept, stat, *blocks in heads]
+    finished = [[kept, stat, *in_order(to_pairs(blocks), order)] for kept, stat, *blocks in heads]
     logits = finished_logits(finished, sent.shape[2], codes, width)
     return (temporal, logits)
 

time: 102 us -> 100 us (0.980)
  starting transfers between devices: 36.7 us -> 34.2 us
  waiting for transfers between devices: 38 us -> 40 us
  Pallas kernels: 25.2 us -> 23.9 us
    ppermute x8, waiting for transfers between devices: 11.1 us -> 13.2 us  [to_neighbour(): return lax.ppermute(block, 'tp', [(i, i ^ 1) for i in range(tp)])]
    ppermute x15, starting transfers between devices: 22.8 us -> 20.9 us  [to_pairs(): lax.ppermute(blocks[k], 'tp', [(i, i ^ 2 * (k + 1)) for i in range(tp)])]
    pallas_call x3 -> x2, Pallas kernels: 15.6 us -> 14.3 us  [the longest x1 10.6 us: temporal_parts(): pl.pallas_call(temporal_kernel, in_specs=[SMEM] + [HBM] * 8, out_specs=[V...]
  transfers between devices with their start and end apart: 26 -> 26, of which waited for: 14 -> 16; matrix products, arithmetic and copies ran while one was open for 1% -> 1% of each run, Pallas kernels for 11% -> 10%
where the time goes in v5:
time: 100 us
  waiting for transfers between devices  40 us (40%)
  starting transfers between devices  34.2 us (34%)
  Pallas kernels  23.9 us (24%)
    ppermute x15, waiting for transfers between devices, to_pairs(): lax.ppermute(blocks[k], 'tp', [(i, i ^ 2 * (k + 1)) for i in range(tp)])  24.7 us
    ppermute x15, starting transfers between devices, to_pairs(): lax.ppermute(blocks[k], 'tp', [(i, i ^ 2 * (k + 1)) for i in range(tp)])  20.9 us
    ppermute x8, waiting for transfers between devices, to_neighbour(): return lax.ppermute(block, 'tp', [(i, i ^ 1) for i in range(tp)])  13.2 us
    pallas_call x1, Pallas kernels, temporal_parts(): pl.pallas_call(temporal_kernel, in_specs=[SMEM] + [HBM] * 8, out_specs=[V...  10.6 us
    ppermute x8, starting transfers between devices, to_neighbour(): return lax.ppermute(block, 'tp', [(i, i ^ 1) for i in range(tp)])  10.4 us
    pallas_call x1, Pallas kernels, brought_near(): pl.pallas_call(near_kernel, in_specs=[SMEM, VMEM, VMEM, HBM, HBM, HBM], o...  3.67 us
    pallas_call x1, Pallas kernels, prepared_entry(): pl.pallas_call(prepare_kernel, in_specs=[SMEM, VMEM, HBM, HBM, HBM], out_...  3.66 us
  transfers between devices with their start and end apart: 26, of which 16 were waited for; matrix products, arithmetic and copies ran while one was open for 1% of the time, Pallas kernels for 10%

profile of v5, /device:TPU:0, one launch (start us, length us, event | category | flops | bytes accessed | tf_op | source)
XLA Modules:
  0.0 100.1 jit_solution(4593637467459130588)
XLA Ops:
  0.7 10.6 %temporal.1 = (f32[4,32,512]{2,1,0:T(8,128)S(1)}, bf16[32,512]{1,0:T(8,128)(2,1)S(1)}, bf16[3,32,512]{2,1,0:T(8,128)(2,1)S(1)}, bf16[4,2,128,256]{3,2,1,0:T(8,128)(2,1)S(1)}) custom-call(s32[3]{0:T(128)S(1)} %pad_add_fusion.place_ref, bf16[32,4096]{1,0:T(8,128)(2,1)} %hidden_hbm.3, f32[1,4096]{1,0:T(1,128)} %bitcast.46, s32[1,32]{1,0:T(1,128)} %bitcast.47, ...), custom_call_target="tpu_custom_call" | custom-call | tf_op jit(solution)/shard_map/temporal/pallas_call | solution.py:398
  11.3 3.0 %collective-permute-start = (bf16[3,32,512]{2,1,0:T(8,128)(2,1)S(1)}, bf16[3,32,512]{2,1,0:T(8,128)(2,1)S(1)}, u32[]{:S(2)}, u32[]{:S(2)}) collective-permute-start(bf16[3,32,512]{2,1,0:T(8,128)(2,1)S(1)} %get-tuple-element.34), channel_id=1, source_target_pairs={{0,2},{2,0},{4,6},{6,4},{8,10},{10,8},{12,14},{14,12},{1,3},{3,1},... | collective-permute-start | bytes 294920 | tf_op jit(solution)/shard_map/ppermute | solution.py:802
  14.4 1.9 %collective-permute-start.6 = (bf16[4,2,128,256]{3,2,1,0:T(8,128)(2,1)S(1)}, bf16[4,2,128,256]{3,2,1,0:T(8,128)(2,1)S(1)}, u32[]{:S(2)}, u32[]{:S(2)}) collective-permute-start(bf16[4,2,128,256]{3,2,1,0:T(8,128)(2,1)S(1)} %get-tuple-element.38), channel_id=1, source_target_pairs={{0,2},{2,0},{4,6},{6,4},{8,10},{10,8},{12,14},{14,12},{1,3},{3,1},... | collective-permute-start | bytes 1572872 | tf_op jit(solution)/shard_map/ppermute | solution.py:802
  16.4 1.5 %collective-permute-done = bf16[3,32,512]{2,1,0:T(8,128)(2,1)S(1)} collective-permute-done((bf16[3,32,512]{2,1,0:T(8,128)(2,1)S(1)}, bf16[3,32,512]{2,1,0:T(8,128)(2,1)S(1)}, u32[]{:S(2)}, u32[]{:S(2)}) %collective-permute-start) | collective-permute-done | bytes 98336 | tf_op jit(solution)/shard_map/ppermute | solution.py:802
  17.9 3.2 %collective-permute-start.1 = (bf16[32,512]{1,0:T(8,128)(2,1)S(1)}, bf16[32,512]{1,0:T(8,128)(2,1)S(1)}, u32[]{:S(2)}, u32[]{:S(2)}) collective-permute-start(bf16[32,512]{1,0:T(8,128)(2,1)S(1)} %get-tuple-element.63), channel_id=1, source_target_pairs={{0,8},{2,10},{4,12},{6,14},{8,0},{10,2},{12,4},{14,6},{1,9},{3,11}... | collective-permute-start | bytes 98312 | tf_op jit(solution)/shard_map/ppermute | solution.py:793
  22.8 3.7 %entry_prepare.1 = (bf16[32,512]{1,0:T(8,128)(2,1)S(1)}, f32[4,64,1024]{2,1,0:T(8,128)S(1)}, bf16[4,512,1024]{2,1,0:T(8,128)(2,1)S(1)}) custom-call(s32[3]{0:T(128)S(1)} %pad_add_fusion.place_ref, s32[64,4]{1,0:T(8,128)S(1)} %copy.17.tokens_ref, bf16[32,4096]{1,0:T(8,128)(2,1)} %hidden_hbm.3, bf16[4,256,1024]{2,1,0:T(8,128)(2,1)} %embed_hbm.1, ...), custom_call_target="tpu_custom_call" | custom-call | tf_op jit(solution)/shard_map/entry_prepare/pallas_call | solution.py:461
  29.1 1.5 %entry.1 = (f32[4,4,64,128]{3,2,1,0:T(8,128)S(1)}, bf16[4,64,128]{2,1,0:T(8,128)(2,1)S(1)}, bf16[3,4,64,128]{3,2,1,0:T(8,128)(2,1)S(1)}, f32[8,128]{1,0:T(8,128)S(1)}) custom-call(s32[3]{0:T(128)S(1)} %pad_add_fusion.place_ref, bf16[32,512]{1,0:T(8,128)(2,1)S(1)} %fusion.4.own_ref, bf16[32,512]{1,0:T(8,128)(2,1)S(1)} %collective-permute-done.5.other_ref, ...), custom_call_target="tpu_custom_call" | custom-call | tf_op jit(solution)/shard_map/entry/pallas_call | solution.py:551
  30.6 1.8 %collective-permute-start.7 = (bf16[3,4,64,128]{3,2,1,0:T(8,128)(2,1)S(1)}, bf16[3,4,64,128]{3,2,1,0:T(8,128)(2,1)S(1)}, u32[]{:S(2)}, u32[]{:S(2)}) collective-permute-start(bf16[3,4,64,128]{3,2,1,0:T(8,128)(2,1)S(1)} %get-tuple-element.42), channel_id=1, source_target_pairs={{0,2},{2,0},{4,6},{6,4},{8,10},{10,8},{12,14},{14,12},{1,3},{3,1},... | collective-permute-start | bytes 589832 | tf_op jit(solution)/shard_map/ppermute | solution.py:802
  32.6 4.8 %collective-permute-done.7 = bf16[3,4,64,128]{3,2,1,0:T(8,128)(2,1)S(1)} collective-permute-done((bf16[3,4,64,128]{3,2,1,0:T(8,128)(2,1)S(1)}, bf16[3,4,64,128]{3,2,1,0:T(8,128)(2,1)S(1)}, u32[]{:S(2)}, u32[]{:S(2)}) %collective-permute-start.7) | collective-permute-done | bytes 196640 | tf_op jit(solution)/shard_map/ppermute | solution.py:802
  37.5 1.8 %collective-permute-start.10 = (bf16[4,64,128]{2,1,0:T(8,128)(2,1)S(1)}, bf16[4,64,128]{2,1,0:T(8,128)(2,1)S(1)}, u32[]{:S(2)}, u32[]{:S(2)}) collective-permute-start(bf16[4,64,128]{2,1,0:T(8,128)(2,1)S(1)} %get-tuple-element.61), channel_id=1, source_target_pairs={{0,4},{2,6},{4,0},{6,2},{8,12},{10,14},{12,8},{14,10},{1,5},{3,7},... | collective-permute-start | bytes 196616 | tf_op jit(solution)/shard_map/ppermute | solution.py:793
  39.3 2.6 %collective-permute-start.8 = (bf16[4,64,128]{2,1,0:T(8,128)(2,1)S(1)}, bf16[4,64,128]{2,1,0:T(8,128)(2,1)S(1)}, u32[]{:S(2)}, u32[]{:S(2)}) collective-permute-start(bf16[4,64,128]{2,1,0:T(8,128)(2,1)S(1)} %get-tuple-element.60), channel_id=1, source_target_pairs={{0,8},{2,10},{4,12},{6,14},{8,0},{10,2},{12,4},{14,6},{1,9},{3,11}... | collective-permute-start | bytes 196616 | tf_op jit(solution)/shard_map/ppermute | solution.py:793
  42.0 3.7 %brought_near.1 = (f32[1,128]{1,0:T(1,128)S(1)}, bf16[4,3,1024,128]{3,2,1,0:T(8,128)(2,1)S(1)}, bf16[4,128,1024]{2,1,0:T(8,128)(2,1)S(1)}, bf16[4,4,128,256]{3,2,1,0:T(8,128)(2,1)S(1)}) custom-call(s32[3]{0:T(128)S(1)} %pad_add_fusion.place_ref, f32[8,128]{1,0:T(8,128)S(1)} %get-tuple-element.39.token_ref, f32[1,1024]{1,0:T(1,128)S(1)} %bitcast.42, ...), custom_call_target="tpu_custom_call" | custom-call | tf_op jit(solution)/shard_map/brought_near/pallas_call | solution.py:504
  45.7 2.9 %collective-permute-done.9.rest_2_ = bf16[4,64,128]{2,1,0:T(8,128)(2,1)S(1)} collective-permute-done((bf16[4,64,128]{2,1,0:T(8,128)(2,1)S(1)}, bf16[4,64,128]{2,1,0:T(8,128)(2,1)S(1)}, u32[]{:S(2)}, u32[]{:S(2)}) %collective-permute-start.9) | collective-permute-done | bytes 65568 | tf_op jit(solution)/shard_map/ppermute | solution.py:793
  49.7 2.5 %collective-permute-start.14 = (bf16[4,64,128]{2,1,0:T(8,128)(2,1)S(1)}, bf16[4,64,128]{2,1,0:T(8,128)(2,1)S(1)}, u32[]{:S(2)}, u32[]{:S(2)}) collective-permute-start(bf16[4,64,128]{2,1,0:T(8,128)(2,1)S(1)} %multiply_convert_fusion.rest_0_), channel_id=1, source_target_pairs={{0,4},{2,6},{4,0},{6,2},{8,12},{10,14},{12,8},{14,10},{1,5},{3,7},... | collective-permute-start | bytes 196616 | tf_op jit(solution)/shard_map/ppermute | solution.py:793
  52.2 1.7 %collective-permute-done.12.rest_1_ = bf16[4,64,128]{2,1,0:T(8,128)(2,1)S(1)} collective-permute-done((bf16[4,64,128]{2,1,0:T(8,128)(2,1)S(1)}, bf16[4,64,128]{2,1,0:T(8,128)(2,1)S(1)}, u32[]{:S(2)}, u32[]{:S(2)}) %collective-permute-start.12) | collective-permute-done | bytes 65568 | tf_op jit(solution)/shard_map/ppermute | solution.py:793
  57.4 1.5 %collective-permute-start.22 = (bf16[4,2,128,256]{3,2,1,0:T(8,128)(2,1)S(1)}, bf16[4,2,128,256]{3,2,1,0:T(8,128)(2,1)S(1)}, u32[]{:S(2)}, u32[]{:S(2)}) collective-permute-start(bf16[4,2,128,256]{3,2,1,0:T(8,128)(2,1)S(1)} %collective-permute-done.6.after_ref.early_ref), channel_id=1, source_target_pairs={{0,16},{16,0},{1,17},{17,1},{2,18},{18,2},{3,19},{19,3},{4,20},{20... | collective-permute-start | bytes 1572872 | tf_op jit(solution)/shard_map/ppermute | solution.py:833
  58.9 2.8 %collective-permute-done.16.rest_4_ = bf16[4,64,128]{2,1,0:T(8,128)(2,1)S(1)} collective-permute-done((bf16[4,64,128]{2,1,0:T(8,128)(2,1)S(1)}, bf16[4,64,128]{2,1,0:T(8,128)(2,1)S(1)}, u32[]{:S(2)}, u32[]{:S(2)}) %collective-permute-start.16) | collective-permute-done | bytes 65568 | tf_op jit(solution)/shard_map/ppermute | solution.py:802
  65.2 1.4 %depth_mix.1 = (f32[4,64,256]{2,1,0:T(8,128)S(1)}, bf16[4,64,256]{2,1,0:T(8,128)(2,1)S(1)}, bf16[4,64,256]{2,1,0:T(8,128)(2,1)S(1)}, bf16[4,64,256]{2,1,0:T(8,128)(2,1)S(1)}) custom-call(s32[3]{0:T(128)S(1)} %pad_add_fusion.place_ref, bf16[4,64,128]{2,1,0:T(8,128)(2,1)S(1)} %get-tuple-element.45.queries_ref, ...), custom_call_target="tpu_custom_call" | custom-call | tf_op jit(solution)/shard_map/depth_mix/pallas_call | solution.py:661
  67.5 2.7 %collective-permute-start.19 = (bf16[4,64,256]{2,1,0:T(8,128)(2,1)S(1)}, bf16[4,64,256]{2,1,0:T(8,128)(2,1)S(1)}, u32[]{:S(2)}, u32[]{:S(2)}) collective-permute-start(bf16[4,64,256]{2,1,0:T(8,128)(2,1)S(1)} %get-tuple-element.50), channel_id=1, source_target_pairs={{0,12},{2,14},{4,8},{6,10},{8,4},{10,6},{12,0},{14,2},{1,13},{3,15... | collective-permute-start | bytes 393224 | tf_op jit(solution)/shard_map/ppermute | solution.py:793
  70.2 9.3 %collective-permute-done.18 = bf16[4,64,256]{2,1,0:T(8,128)(2,1)S(1)} collective-permute-done((bf16[4,64,256]{2,1,0:T(8,128)(2,1)S(1)}, bf16[4,64,256]{2,1,0:T(8,128)(2,1)S(1)}, u32[]{:S(2)}, u32[]{:S(2)}) %collective-permute-start.18) | collective-permute-done | bytes 131104 | tf_op jit(solution)/shard_map/ppermute | solution.py:793
  82.3 3.1 %collective-permute-done.21.arrived_ref = bf16[4,64,256]{2,1,0:T(8,128)(2,1)S(1)} collective-permute-done((bf16[4,64,256]{2,1,0:T(8,128)(2,1)S(1)}, bf16[4,64,256]{2,1,0:T(8,128)(2,1)S(1)}, u32[]{:S(2)}, u32[]{:S(2)}) %collective-permute-start.21) | collective-permute-done | bytes 131104 | tf_op jit(solution)/shard_map/ppermute | solution.py:802
  86.5 2.6 %collective-permute-start.23 = (bf16[272,256]{1,0:T(8,128)(2,1)S(1)}, bf16[272,256]{1,0:T(8,128)(2,1)S(1)}, u32[]{:S(2)}, u32[]{:S(2)}) collective-permute-start(bf16[272,256]{1,0:T(8,128)(2,1)S(1)} %get-tuple-element.55), channel_id=1, source_target_pairs={{0,8},{2,10},{4,12},{6,14},{8,0},{10,2},{12,4},{14,6},{1,9},{3,11}... | collective-permute-start | bytes 417800 | tf_op jit(solution)/shard_map/ppermute | solution.py:793
  89.1 1.9 %collective-permute-start.24 = (bf16[272,256]{1,0:T(8,128)(2,1)S(1)}, bf16[272,256]{1,0:T(8,128)(2,1)S(1)}, u32[]{:S(2)}, u32[]{:S(2)}) collective-permute-start(bf16[272,256]{1,0:T(8,128)(2,1)S(1)} %get-tuple-element.56), channel_id=1, source_target_pairs={{0,12},{2,14},{4,8},{6,10},{8,4},{10,6},{12,0},{14,2},{1,13},{3,15... | collective-permute-start | bytes 417800 | tf_op jit(solution)/shard_map/ppermute | solution.py:793
  91.0 8.1 %collective-permute-done.23.refs_2_ = bf16[272,256]{1,0:T(8,128)(2,1)S(1)} collective-permute-done((bf16[272,256]{1,0:T(8,128)(2,1)S(1)}, bf16[272,256]{1,0:T(8,128)(2,1)S(1)}, u32[]{:S(2)}, u32[]{:S(2)}) %collective-permute-start.23) | collective-permute-done | bytes 139296 | tf_op jit(solution)/shard_map/ppermute | solution.py:793
  (54 shorter events, 18.7 us)
Async XLA Ops:
  11.3 6.5 %collective-permute-start = (bf16[3,32,512]{2,1,0:T(8,128)(2,1)S(1)}, bf16[3,32,512]{2,1,0:T(8,128)(2,1)S(1)}, u32[]{:S(2)}, u32[]{:S(2)}) collective-permute-start(bf16[3,32,512]{2,1,0:T(8,128)(2,1)S(1)} %get-tuple-element.34), channel_id=1, source_target_pairs={{0,2},{2,0},{4,6},{6,4},{8,10},{10,8},{12,14},{14,12},{1,3},{3,1},... | collective-permute-start | bytes 294920 | tf_op jit(solution)/shard_map/ppermute | solution.py:802
  14.3 12.1 %collective-permute-start.4 = (bf16[32,512]{1,0:T(8,128)(2,1)S(1)}, bf16[32,512]{1,0:T(8,128)(2,1)S(1)}, u32[]{:S(2)}, u32[]{:S(2)}) collective-permute-start(bf16[32,512]{1,0:T(8,128)(2,1)S(1)} %get-tuple-element.35), channel_id=1, source_target_pairs={{0,2},{2,0},{4,6},{6,4},{8,10},{10,8},{12,14},{14,12},{1,3},{3,1},... | collective-permute-start | bytes 98312 | tf_op jit(solution)/shard_map/ppermute | solution.py:802
  14.4 14.6 %collective-permute-start.6 = (bf16[4,2,128,256]{3,2,1,0:T(8,128)(2,1)S(1)}, bf16[4,2,128,256]{3,2,1,0:T(8,128)(2,1)S(1)}, u32[]{:S(2)}, u32[]{:S(2)}) collective-permute-start(bf16[4,2,128,256]{3,2,1,0:T(8,128)(2,1)S(1)} %get-tuple-element.38), channel_id=1, source_target_pairs={{0,2},{2,0},{4,6},{6,4},{8,10},{10,8},{12,14},{14,12},{1,3},{3,1},... | collective-permute-start | bytes 1572872 | tf_op jit(solution)/shard_map/ppermute | solution.py:802
  17.9 8.6 %collective-permute-start.1 = (bf16[32,512]{1,0:T(8,128)(2,1)S(1)}, bf16[32,512]{1,0:T(8,128)(2,1)S(1)}, u32[]{:S(2)}, u32[]{:S(2)}) collective-permute-start(bf16[32,512]{1,0:T(8,128)(2,1)S(1)} %get-tuple-element.63), channel_id=1, source_target_pairs={{0,8},{2,10},{4,12},{6,14},{8,0},{10,2},{12,4},{14,6},{1,9},{3,11}... | collective-permute-start | bytes 98312 | tf_op jit(solution)/shard_map/ppermute | solution.py:793
  21.1 5.7 %collective-permute-start.2 = (bf16[32,512]{1,0:T(8,128)(2,1)S(1)}, bf16[32,512]{1,0:T(8,128)(2,1)S(1)}, u32[]{:S(2)}, u32[]{:S(2)}) collective-permute-start(bf16[32,512]{1,0:T(8,128)(2,1)S(1)} %get-tuple-element.65), channel_id=1, source_target_pairs={{0,12},{2,14},{4,8},{6,10},{8,4},{10,6},{12,0},{14,2},{1,13},{3,15... | collective-permute-start | bytes 98312 | tf_op jit(solution)/shard_map/ppermute | solution.py:793
  22.4 4.4 %collective-permute-start.3 = (bf16[32,512]{1,0:T(8,128)(2,1)S(1)}, bf16[32,512]{1,0:T(8,128)(2,1)S(1)}, u32[]{:S(2)}, u32[]{:S(2)}) collective-permute-start(bf16[32,512]{1,0:T(8,128)(2,1)S(1)} %get-tuple-element.64), channel_id=1, source_target_pairs={{0,4},{2,6},{4,0},{6,2},{8,12},{10,14},{12,8},{14,10},{1,5},{3,7},... | collective-permute-start | bytes 98312 | tf_op jit(solution)/shard_map/ppermute | solution.py:793
  30.6 6.9 %collective-permute-start.7 = (bf16[3,4,64,128]{3,2,1,0:T(8,128)(2,1)S(1)}, bf16[3,4,64,128]{3,2,1,0:T(8,128)(2,1)S(1)}, u32[]{:S(2)}, u32[]{:S(2)}) collective-permute-start(bf16[3,4,64,128]{3,2,1,0:T(8,128)(2,1)S(1)} %get-tuple-element.42), channel_id=1, source_target_pairs={{0,2},{2,0},{4,6},{6,4},{8,10},{10,8},{12,14},{14,12},{1,3},{3,1},... | collective-permute-start | bytes 589832 | tf_op jit(solution)/shard_map/ppermute | solution.py:802
  32.4 13.3 %collective-permute-start.11 = (bf16[4,64,128]{2,1,0:T(8,128)(2,1)S(1)}, bf16[4,64,128]{2,1,0:T(8,128)(2,1)S(1)}, u32[]{:S(2)}, u32[]{:S(2)}) collective-permute-start(bf16[4,64,128]{2,1,0:T(8,128)(2,1)S(1)} %get-tuple-element.43), channel_id=1, source_target_pairs={{0,2},{2,0},{4,6},{6,4},{8,10},{10,8},{12,14},{14,12},{1,3},{3,1},... | collective-permute-start | bytes 196616 | tf_op jit(solution)/shard_map/ppermute | solution.py:802
  37.5 8.2 %collective-permute-start.10 = (bf16[4,64,128]{2,1,0:T(8,128)(2,1)S(1)}, bf16[4,64,128]{2,1,0:T(8,128)(2,1)S(1)}, u32[]{:S(2)}, u32[]{:S(2)}) collective-permute-start(bf16[4,64,128]{2,1,0:T(8,128)(2,1)S(1)} %get-tuple-element.61), channel_id=1, source_target_pairs={{0,4},{2,6},{4,0},{6,2},{8,12},{10,14},{12,8},{14,10},{1,5},{3,7},... | collective-permute-start | bytes 196616 | tf_op jit(solution)/shard_map/ppermute | solution.py:793
  39.3 6.3 %collective-permute-start.8 = (bf16[4,64,128]{2,1,0:T(8,128)(2,1)S(1)}, bf16[4,64,128]{2,1,0:T(8,128)(2,1)S(1)}, u32[]{:S(2)}, u32[]{:S(2)}) collective-permute-start(bf16[4,64,128]{2,1,0:T(8,128)(2,1)S(1)} %get-tuple-element.60), channel_id=1, source_target_pairs={{0,8},{2,10},{4,12},{6,14},{8,0},{10,2},{12,4},{14,6},{1,9},{3,11}... | collective-permute-start | bytes 196616 | tf_op jit(solution)/shard_map/ppermute | solution.py:793
  41.9 6.7 %collective-permute-start.9 = (bf16[4,64,128]{2,1,0:T(8,128)(2,1)S(1)}, bf16[4,64,128]{2,1,0:T(8,128)(2,1)S(1)}, u32[]{:S(2)}, u32[]{:S(2)}) collective-permute-start(bf16[4,64,128]{2,1,0:T(8,128)(2,1)S(1)} %get-tuple-element.62), channel_id=1, source_target_pairs={{0,12},{2,14},{4,8},{6,10},{8,4},{10,6},{12,0},{14,2},{1,13},{3,15... | collective-permute-start | bytes 196616 | tf_op jit(solution)/shard_map/ppermute | solution.py:793
  48.7 5.2 %collective-permute-start.12 = (bf16[4,64,128]{2,1,0:T(8,128)(2,1)S(1)}, bf16[4,64,128]{2,1,0:T(8,128)(2,1)S(1)}, u32[]{:S(2)}, u32[]{:S(2)}) collective-permute-start(bf16[4,64,128]{2,1,0:T(8,128)(2,1)S(1)} %multiply_convert_fusion.rest_0_), channel_id=1, source_target_pairs={{0,8},{2,10},{4,12},{6,14},{8,0},{10,2},{12,4},{14,6},{1,9},{3,11}... | collective-permute-start | bytes 196616 | tf_op jit(solution)/shard_map/ppermute | solution.py:793
  48.7 6.3 %collective-permute-start.13 = (bf16[4,64,128]{2,1,0:T(8,128)(2,1)S(1)}, bf16[4,64,128]{2,1,0:T(8,128)(2,1)S(1)}, u32[]{:S(2)}, u32[]{:S(2)}) collective-permute-start(bf16[4,64,128]{2,1,0:T(8,128)(2,1)S(1)} %multiply_convert_fusion.rest_0_), channel_id=1, source_target_pairs={{0,12},{2,14},{4,8},{6,10},{8,4},{10,6},{12,0},{14,2},{1,13},{3,15... | collective-permute-start | bytes 196616 | tf_op jit(solution)/shard_map/ppermute | solution.py:793
  49.7 5.6 %collective-permute-start.14 = (bf16[4,64,128]{2,1,0:T(8,128)(2,1)S(1)}, bf16[4,64,128]{2,1,0:T(8,128)(2,1)S(1)}, u32[]{:S(2)}, u32[]{:S(2)}) collective-permute-start(bf16[4,64,128]{2,1,0:T(8,128)(2,1)S(1)} %multiply_convert_fusion.rest_0_), channel_id=1, source_target_pairs={{0,4},{2,6},{4,0},{6,2},{8,12},{10,14},{12,8},{14,10},{1,5},{3,7},... | collective-permute-start | bytes 196616 | tf_op jit(solution)/shard_map/ppermute | solution.py:793
  55.3 6.4 %collective-permute-start.15 = (bf16[3,4,64,128]{3,2,1,0:T(8,128)(2,1)S(1)}, bf16[3,4,64,128]{3,2,1,0:T(8,128)(2,1)S(1)}, u32[]{:S(2)}, u32[]{:S(2)}) collective-permute-start(bf16[3,4,64,128]{3,2,1,0:T(8,128)(2,1)S(1)} %pad_maximum_fusion), channel_id=1, source_target_pairs={{0,2},{2,0},{4,6},{6,4},{8,10},{10,8},{12,14},{14,12},{1,3},{3,1},... | collective-permute-start | bytes 589832 | tf_op jit(solution)/shard_map/ppermute | solution.py:802
  56.5 5.3 %collective-permute-start.16 = (bf16[4,64,128]{2,1,0:T(8,128)(2,1)S(1)}, bf16[4,64,128]{2,1,0:T(8,128)(2,1)S(1)}, u32[]{:S(2)}, u32[]{:S(2)}) collective-permute-start(bf16[4,64,128]{2,1,0:T(8,128)(2,1)S(1)} %multiply_convert_fusion.rest_0_), channel_id=1, source_target_pairs={{0,2},{2,0},{4,6},{6,4},{8,10},{10,8},{12,14},{14,12},{1,3},{3,1},... | collective-permute-start | bytes 196616 | tf_op jit(solution)/shard_map/ppermute | solution.py:802
  57.4 24.9 %collective-permute-start.22 = (bf16[4,2,128,256]{3,2,1,0:T(8,128)(2,1)S(1)}, bf16[4,2,128,256]{3,2,1,0:T(8,128)(2,1)S(1)}, u32[]{:S(2)}, u32[]{:S(2)}) collective-permute-start(bf16[4,2,128,256]{3,2,1,0:T(8,128)(2,1)S(1)} %collective-permute-done.6.after_ref.early_ref), channel_id=1, source_target_pairs={{0,16},{16,0},{1,17},{17,1},{2,18},{18,2},{3,19},{19,3},{4,20},{20... | collective-permute-start | bytes 1572872 | tf_op jit(solution)/shard_map/ppermute | solution.py:833
  66.6 13.0 %collective-permute-start.18 = (bf16[4,64,256]{2,1,0:T(8,128)(2,1)S(1)}, bf16[4,64,256]{2,1,0:T(8,128)(2,1)S(1)}, u32[]{:S(2)}, u32[]{:S(2)}) collective-permute-start(bf16[4,64,256]{2,1,0:T(8,128)(2,1)S(1)} %get-tuple-element.49), channel_id=1, source_target_pairs={{0,8},{2,10},{4,12},{6,14},{8,0},{10,2},{12,4},{14,6},{1,9},{3,11}... | collective-permute-start | bytes 393224 | tf_op jit(solution)/shard_map/ppermute | solution.py:793
  67.5 12.0 %collective-permute-start.19 = (bf16[4,64,256]{2,1,0:T(8,128)(2,1)S(1)}, bf16[4,64,256]{2,1,0:T(8,128)(2,1)S(1)}, u32[]{:S(2)}, u32[]{:S(2)}) collective-permute-start(bf16[4,64,256]{2,1,0:T(8,128)(2,1)S(1)} %get-tuple-element.50), channel_id=1, source_target_pairs={{0,12},{2,14},{4,8},{6,10},{8,4},{10,6},{12,0},{14,2},{1,13},{3,15... | collective-permute-start | bytes 393224 | tf_op jit(solution)/shard_map/ppermute | solution.py:793
  70.2 10.1 %collective-permute-start.20 = (bf16[4,64,256]{2,1,0:T(8,128)(2,1)S(1)}, bf16[4,64,256]{2,1,0:T(8,128)(2,1)S(1)}, u32[]{:S(2)}, u32[]{:S(2)}) collective-permute-start(bf16[4,64,256]{2,1,0:T(8,128)(2,1)S(1)} %get-tuple-element.51), channel_id=1, source_target_pairs={{0,4},{2,6},{4,0},{6,2},{8,12},{10,14},{12,8},{14,10},{1,5},{3,7},... | collective-permute-start | bytes 393224 | tf_op jit(solution)/shard_map/ppermute | solution.py:793
  80.4 5.0 %collective-permute-start.21 = (bf16[4,64,256]{2,1,0:T(8,128)(2,1)S(1)}, bf16[4,64,256]{2,1,0:T(8,128)(2,1)S(1)}, u32[]{:S(2)}, u32[]{:S(2)}) collective-permute-start(bf16[4,64,256]{2,1,0:T(8,128)(2,1)S(1)} %get-tuple-element.58), channel_id=1, source_target_pairs={{0,2},{2,0},{4,6},{6,4},{8,10},{10,8},{12,14},{14,12},{1,3},{3,1},... | collective-permute-start | bytes 393224 | tf_op jit(solution)/shard_map/ppermute | solution.py:802
  86.5 12.6 %collective-permute-start.23 = (bf16[272,256]{1,0:T(8,128)(2,1)S(1)}, bf16[272,256]{1,0:T(8,128)(2,1)S(1)}, u32[]{:S(2)}, u32[]{:S(2)}) collective-permute-start(bf16[272,256]{1,0:T(8,128)(2,1)S(1)} %get-tuple-element.55), channel_id=1, source_target_pairs={{0,8},{2,10},{4,12},{6,14},{8,0},{10,2},{12,4},{14,6},{1,9},{3,11}... | collective-permute-start | bytes 417800 | tf_op jit(solution)/shard_map/ppermute | solution.py:793
  89.1 10.0 %collective-permute-start.24 = (bf16[272,256]{1,0:T(8,128)(2,1)S(1)}, bf16[272,256]{1,0:T(8,128)(2,1)S(1)}, u32[]{:S(2)}, u32[]{:S(2)}) collective-permute-start(bf16[272,256]{1,0:T(8,128)(2,1)S(1)} %get-tuple-element.56), channel_id=1, source_target_pairs={{0,12},{2,14},{4,8},{6,10},{8,4},{10,6},{12,0},{14,2},{1,13},{3,15... | collective-permute-start | bytes 417800 | tf_op jit(solution)/shard_map/ppermute | solution.py:793
  91.0 8.3 %collective-permute-start.25 = (bf16[272,256]{1,0:T(8,128)(2,1)S(1)}, bf16[272,256]{1,0:T(8,128)(2,1)S(1)}, u32[]{:S(2)}, u32[]{:S(2)}) collective-permute-start(bf16[272,256]{1,0:T(8,128)(2,1)S(1)} %get-tuple-element.57), channel_id=1, source_target_pairs={{0,4},{2,6},{4,0},{6,2},{8,12},{10,14},{12,8},{14,10},{1,5},{3,7},... | collective-permute-start | bytes 417800 | tf_op jit(solution)/shard_map/ppermute | solution.py:793
  (5 other events, 49.0 us)

commit v6 on v5

--- a/solution.py
+++ b/solution.py
@@ -520,8 +520,9 @@
     )(place, token, gain.reshape(1, width), in_hbm(qkv), in_hbm(out_weight), in_hbm(head_weight))
 
 
-def entry_kernel(place_ref, own_ref, other_ref, embedded_ref, weight_ref, after_ref, kept_ref, last_ref, sent_ref, token_ref, total_buf):
-    del after_ref
+def entry_kernel(
+    place_ref, own_ref, other_ref, embedded_ref, weight_ref, kept_ref, last_ref, sent_ref, token_ref, total_buf
+):
     token_ref[...] = jnp.zeros_like(token_ref)
     codes = weight_ref.shape[0]
     count, _, _, part = kept_ref.shape
@@ -544,13 +545,13 @@
                 sent_ref[k - 1, c] = sent
 
 
-def entry_parts(place, own, other, embedded, weight, after, places):
+def entry_parts(place, own, other, embedded, weight, places):
     codes, _, width = weight.shape
     streams = 2 * own.shape[0]
     block = (places // 2, codes, streams, width // places)
     return pl.pallas_call(
         entry_kernel,
-        in_specs=[SMEM] + [VMEM] * 5,
+        in_specs=[SMEM] + [VMEM] * 4,
         out_specs=[VMEM] * 4,
         out_shape=[
             vmem(block, jnp.float32),
@@ -561,7 +562,7 @@
         scratch_shapes=[pltpu.VMEM((streams, width), jnp.float32)],
         compiler_params=params(16),
         name="entry",
-    )(place, own, other, embedded, weight, after)
+    )(place, own, other, embedded, weight)
 
 
 def nearest_last(far):
@@ -829,7 +830,8 @@
     codes = depth_in.shape[0]
     width = depth_in.shape[2]
     hidden_rows = head_weight.shape[1]
-    kept, last, sent, token = entry_parts(place, temporal, other_rows, embedded, near_in, early, tp)
+    kept, last, sent, token = entry_parts(place, temporal, other_rows, embedded, near_in, tp)
+    sent, early = lax.optimization_barrier((sent, early))
     late = lax.ppermute(early, "grp", [(i, i ^ 1) for i in range(lax.axis_size("grp"))])
     own_gain, near_qkv, near_out, *own_columns = brought_near(
         place, token, depth_gain, depth_qkv, depth_out_weight, head_weight, tp

time: 100 us -> 99.8 us (level)
  waiting for transfers between devices: 40 us -> 38.5 us
  transfers between devices with their start and end apart: 26 -> 26, of which waited for: 16 -> 14; matrix products, arithmetic and copies ran while one was open for 1% -> 1% of each run, Pallas kernels for 10% -> 11%
where the time goes in v6:
time: 99.8 us; the launch traced here: 99.6 us
  waiting for transfers between devices  38.5 us (39%)
  starting transfers between devices  35.1 us (35%)
  Pallas kernels  23.9 us (24%)
    ppermute x15, waiting for transfers between devices, to_pairs(): lax.ppermute(blocks[k], 'tp', [(i, i ^ 2 * (k + 1)) for i in range(tp)])  23.9 us
    ppermute x15, starting transfers between devices, to_pairs(): lax.ppermute(blocks[k], 'tp', [(i, i ^ 2 * (k + 1)) for i in range(tp)])  21.3 us
    ppermute x8, waiting for transfers between devices, to_neighbour(): return lax.ppermute(block, 'tp', [(i, i ^ 1) for i in range(tp)])  12.5 us
    ppermute x8, starting transfers between devices, to_neighbour(): return lax.ppermute(block, 'tp', [(i, i ^ 1) for i in range(tp)])  10.9 us
    pallas_call x1, Pallas kernels, temporal_parts(): pl.pallas_call(temporal_kernel, in_specs=[SMEM] + [HBM] * 8, out_specs=[V...  10.6 us
    pallas_call x1, Pallas kernels, brought_near(): pl.pallas_call(near_kernel, in_specs=[SMEM, VMEM, VMEM, HBM, HBM, HBM], o...  3.67 us
    pallas_call x1, Pallas kernels, prepared_entry(): pl.pallas_call(prepare_kernel, in_specs=[SMEM, VMEM, HBM, HBM, HBM], out_...  3.66 us
  transfers between devices with their start and end apart: 26, of which 14 were waited for; matrix products, arithmetic and copies ran while one was open for 1% of the time, Pallas kernels for 11%

profile of v6, /device:TPU:0, one launch (start us, length us, event | category | flops | bytes accessed | tf_op | source)
XLA Modules:
  0.0 99.6 jit_solution(9567496094026814891)
XLA Ops:
  0.7 10.6 %temporal.1 = (f32[4,32,512]{2,1,0:T(8,128)S(1)}, bf16[32,512]{1,0:T(8,128)(2,1)S(1)}, bf16[3,32,512]{2,1,0:T(8,128)(2,1)S(1)}, bf16[4,2,128,256]{3,2,1,0:T(8,128)(2,1)S(1)}) custom-call(s32[3]{0:T(128)S(1)} %pad_add_fusion.place_ref, bf16[32,4096]{1,0:T(8,128)(2,1)} %hidden_hbm.3, f32[1,4096]{1,0:T(1,128)} %bitcast.46, s32[1,32]{1,0:T(1,128)} %bitcast.47, ...), custom_call_target="tpu_custom_call" | custom-call | tf_op jit(solution)/shard_map/temporal/pallas_call | solution.py:398
  11.3 3.0 %collective-permute-start = (bf16[3,32,512]{2,1,0:T(8,128)(2,1)S(1)}, bf16[3,32,512]{2,1,0:T(8,128)(2,1)S(1)}, u32[]{:S(2)}, u32[]{:S(2)}) collective-permute-start(bf16[3,32,512]{2,1,0:T(8,128)(2,1)S(1)} %get-tuple-element.36), channel_id=1, source_target_pairs={{0,2},{2,0},{4,6},{6,4},{8,10},{10,8},{12,14},{14,12},{1,3},{3,1},... | collective-permute-start | bytes 294920 | tf_op jit(solution)/shard_map/ppermute | solution.py:803
  14.4 1.9 %collective-permute-start.6 = (bf16[4,2,128,256]{3,2,1,0:T(8,128)(2,1)S(1)}, bf16[4,2,128,256]{3,2,1,0:T(8,128)(2,1)S(1)}, u32[]{:S(2)}, u32[]{:S(2)}) collective-permute-start(bf16[4,2,128,256]{3,2,1,0:T(8,128)(2,1)S(1)} %get-tuple-element.44), channel_id=1, source_target_pairs={{0,2},{2,0},{4,6},{6,4},{8,10},{10,8},{12,14},{14,12},{1,3},{3,1},... | collective-permute-start | bytes 1572872 | tf_op jit(solution)/shard_map/ppermute | solution.py:803
  16.4 1.5 %collective-permute-done = bf16[3,32,512]{2,1,0:T(8,128)(2,1)S(1)} collective-permute-done((bf16[3,32,512]{2,1,0:T(8,128)(2,1)S(1)}, bf16[3,32,512]{2,1,0:T(8,128)(2,1)S(1)}, u32[]{:S(2)}, u32[]{:S(2)}) %collective-permute-start) | collective-permute-done | bytes 98336 | tf_op jit(solution)/shard_map/ppermute | solution.py:803
  17.9 3.2 %collective-permute-start.1 = (bf16[32,512]{1,0:T(8,128)(2,1)S(1)}, bf16[32,512]{1,0:T(8,128)(2,1)S(1)}, u32[]{:S(2)}, u32[]{:S(2)}) collective-permute-start(bf16[32,512]{1,0:T(8,128)(2,1)S(1)} %get-tuple-element.67), channel_id=1, source_target_pairs={{0,8},{2,10},{4,12},{6,14},{8,0},{10,2},{12,4},{14,6},{1,9},{3,11}... | collective-permute-start | bytes 98312 | tf_op jit(solution)/shard_map/ppermute | solution.py:794
  22.8 3.7 %entry_prepare.1 = (bf16[32,512]{1,0:T(8,128)(2,1)S(1)}, f32[4,64,1024]{2,1,0:T(8,128)S(1)}, bf16[4,512,1024]{2,1,0:T(8,128)(2,1)S(1)}) custom-call(s32[3]{0:T(128)S(1)} %pad_add_fusion.place_ref, s32[64,4]{1,0:T(8,128)S(1)} %copy.17.tokens_ref, bf16[32,4096]{1,0:T(8,128)(2,1)} %hidden_hbm.3, bf16[4,256,1024]{2,1,0:T(8,128)(2,1)} %embed_hbm.1, ...), custom_call_target="tpu_custom_call" | custom-call | tf_op jit(solution)/shard_map/entry_prepare/pallas_call | solution.py:461
  28.1 1.5 %entry.1 = (f32[4,4,64,128]{3,2,1,0:T(8,128)S(1)}, bf16[4,64,128]{2,1,0:T(8,128)(2,1)S(1)}, bf16[3,4,64,128]{3,2,1,0:T(8,128)(2,1)S(1)}, f32[8,128]{1,0:T(8,128)S(1)}) custom-call(s32[3]{0:T(128)S(1)} %pad_add_fusion.place_ref, bf16[32,512]{1,0:T(8,128)(2,1)S(1)} %fusion.4.own_ref, bf16[32,512]{1,0:T(8,128)(2,1)S(1)} %collective-permute-done.5.other_ref, ...), custom_call_target="tpu_custom_call" | custom-call | tf_op jit(solution)/shard_map/entry/pallas_call | solution.py:552
  29.6 1.7 %collective-permute-start.7 = (bf16[3,4,64,128]{3,2,1,0:T(8,128)(2,1)S(1)}, bf16[3,4,64,128]{3,2,1,0:T(8,128)(2,1)S(1)}, u32[]{:S(2)}, u32[]{:S(2)}) collective-permute-start(bf16[3,4,64,128]{3,2,1,0:T(8,128)(2,1)S(1)} %get-tuple-element.45), channel_id=1, source_target_pairs={{0,2},{2,0},{4,6},{6,4},{8,10},{10,8},{12,14},{14,12},{1,3},{3,1},... | collective-permute-start | bytes 589832 | tf_op jit(solution)/shard_map/ppermute | solution.py:803
  31.7 5.6 %collective-permute-done.7 = bf16[3,4,64,128]{3,2,1,0:T(8,128)(2,1)S(1)} collective-permute-done((bf16[3,4,64,128]{3,2,1,0:T(8,128)(2,1)S(1)}, bf16[3,4,64,128]{3,2,1,0:T(8,128)(2,1)S(1)}, u32[]{:S(2)}, u32[]{:S(2)}) %collective-permute-start.7) | collective-permute-done | bytes 196640 | tf_op jit(solution)/shard_map/ppermute | solution.py:803
  37.4 1.5 %collective-permute-start.10 = (bf16[4,64,128]{2,1,0:T(8,128)(2,1)S(1)}, bf16[4,64,128]{2,1,0:T(8,128)(2,1)S(1)}, u32[]{:S(2)}, u32[]{:S(2)}) collective-permute-start(bf16[4,64,128]{2,1,0:T(8,128)(2,1)S(1)} %get-tuple-element.65), channel_id=1, source_target_pairs={{0,4},{2,6},{4,0},{6,2},{8,12},{10,14},{12,8},{14,10},{1,5},{3,7},... | collective-permute-start | bytes 196616 | tf_op jit(solution)/shard_map/ppermute | solution.py:794
  39.0 1.7 %collective-permute-start.8 = (bf16[4,64,128]{2,1,0:T(8,128)(2,1)S(1)}, bf16[4,64,128]{2,1,0:T(8,128)(2,1)S(1)}, u32[]{:S(2)}, u32[]{:S(2)}) collective-permute-start(bf16[4,64,128]{2,1,0:T(8,128)(2,1)S(1)} %get-tuple-element.64), channel_id=1, source_target_pairs={{0,8},{2,10},{4,12},{6,14},{8,0},{10,2},{12,4},{14,6},{1,9},{3,11}... | collective-permute-start | bytes 196616 | tf_op jit(solution)/shard_map/ppermute | solution.py:794
  41.9 3.7 %brought_near.1 = (f32[1,128]{1,0:T(1,128)S(1)}, bf16[4,3,1024,128]{3,2,1,0:T(8,128)(2,1)S(1)}, bf16[4,128,1024]{2,1,0:T(8,128)(2,1)S(1)}, bf16[4,4,128,256]{3,2,1,0:T(8,128)(2,1)S(1)}) custom-call(s32[3]{0:T(128)S(1)} %pad_add_fusion.place_ref, f32[8,128]{1,0:T(8,128)S(1)} %get-tuple-element.40.token_ref, f32[1,1024]{1,0:T(1,128)S(1)} %bitcast.42, ...), custom_call_target="tpu_custom_call" | custom-call | tf_op jit(solution)/shard_map/brought_near/pallas_call | solution.py:504
  50.3 1.7 %collective-permute-done.12.rest_1_ = bf16[4,64,128]{2,1,0:T(8,128)(2,1)S(1)} collective-permute-done((bf16[4,64,128]{2,1,0:T(8,128)(2,1)S(1)}, bf16[4,64,128]{2,1,0:T(8,128)(2,1)S(1)}, u32[]{:S(2)}, u32[]{:S(2)}) %collective-permute-start.12) | collective-permute-done | bytes 65568 | tf_op jit(solution)/shard_map/ppermute | solution.py:794
  52.0 2.0 %collective-permute-done.13.rest_2_ = bf16[4,64,128]{2,1,0:T(8,128)(2,1)S(1)} collective-permute-done((bf16[4,64,128]{2,1,0:T(8,128)(2,1)S(1)}, bf16[4,64,128]{2,1,0:T(8,128)(2,1)S(1)}, u32[]{:S(2)}, u32[]{:S(2)}) %collective-permute-start.13) | collective-permute-done | bytes 65568 | tf_op jit(solution)/shard_map/ppermute | solution.py:794
  54.0 1.7 %collective-permute-start.15 = (bf16[3,4,64,128]{3,2,1,0:T(8,128)(2,1)S(1)}, bf16[3,4,64,128]{3,2,1,0:T(8,128)(2,1)S(1)}, u32[]{:S(2)}, u32[]{:S(2)}) collective-permute-start(bf16[3,4,64,128]{3,2,1,0:T(8,128)(2,1)S(1)} %pad_maximum_fusion), channel_id=1, source_target_pairs={{0,2},{2,0},{4,6},{6,4},{8,10},{10,8},{12,14},{14,12},{1,3},{3,1},... | collective-permute-start | bytes 589832 | tf_op jit(solution)/shard_map/ppermute | solution.py:803
  56.1 1.5 %collective-permute-start.22 = (bf16[4,2,128,256]{3,2,1,0:T(8,128)(2,1)S(1)}, bf16[4,2,128,256]{3,2,1,0:T(8,128)(2,1)S(1)}, u32[]{:S(2)}, u32[]{:S(2)}) collective-permute-start(bf16[4,2,128,256]{3,2,1,0:T(8,128)(2,1)S(1)} %collective-permute-done.6.early_ref), channel_id=1, source_target_pairs={{0,16},{16,0},{1,17},{17,1},{2,18},{18,2},{3,19},{19,3},{4,20},{20... | collective-permute-start | bytes 1572872 | tf_op jit(solution)/shard_map/ppermute | solution.py:835
  57.6 2.8 %collective-permute-done.16.rest_4_ = bf16[4,64,128]{2,1,0:T(8,128)(2,1)S(1)} collective-permute-done((bf16[4,64,128]{2,1,0:T(8,128)(2,1)S(1)}, bf16[4,64,128]{2,1,0:T(8,128)(2,1)S(1)}, u32[]{:S(2)}, u32[]{:S(2)}) %collective-permute-start.16) | collective-permute-done | bytes 65568 | tf_op jit(solution)/shard_map/ppermute | solution.py:803
  66.7 1.7 %collective-permute-start.19 = (bf16[4,64,256]{2,1,0:T(8,128)(2,1)S(1)}, bf16[4,64,256]{2,1,0:T(8,128)(2,1)S(1)}, u32[]{:S(2)}, u32[]{:S(2)}) collective-permute-start(bf16[4,64,256]{2,1,0:T(8,128)(2,1)S(1)} %get-tuple-element.53), channel_id=1, source_target_pairs={{0,12},{2,14},{4,8},{6,10},{8,4},{10,6},{12,0},{14,2},{1,13},{3,15... | collective-permute-start | bytes 393224 | tf_op jit(solution)/shard_map/ppermute | solution.py:794
  68.9 9.0 %collective-permute-done.18 = bf16[4,64,256]{2,1,0:T(8,128)(2,1)S(1)} collective-permute-done((bf16[4,64,256]{2,1,0:T(8,128)(2,1)S(1)}, bf16[4,64,256]{2,1,0:T(8,128)(2,1)S(1)}, u32[]{:S(2)}, u32[]{:S(2)}) %collective-permute-start.18) | collective-permute-done | bytes 131104 | tf_op jit(solution)/shard_map/ppermute | solution.py:794
  79.1 1.7 %collective-permute-start.21 = (bf16[4,64,256]{2,1,0:T(8,128)(2,1)S(1)}, bf16[4,64,256]{2,1,0:T(8,128)(2,1)S(1)}, u32[]{:S(2)}, u32[]{:S(2)}) collective-permute-start(bf16[4,64,256]{2,1,0:T(8,128)(2,1)S(1)} %get-tuple-element.62), channel_id=1, source_target_pairs={{0,2},{2,0},{4,6},{6,4},{8,10},{10,8},{12,14},{14,12},{1,3},{3,1},... | collective-permute-start | bytes 393224 | tf_op jit(solution)/shard_map/ppermute | solution.py:803
  81.6 2.6 %collective-permute-done.21.arrived_ref = bf16[4,64,256]{2,1,0:T(8,128)(2,1)S(1)} collective-permute-done((bf16[4,64,256]{2,1,0:T(8,128)(2,1)S(1)}, bf16[4,64,256]{2,1,0:T(8,128)(2,1)S(1)}, u32[]{:S(2)}, u32[]{:S(2)}) %collective-permute-start.21) | collective-permute-done | bytes 131104 | tf_op jit(solution)/shard_map/ppermute | solution.py:803
  85.2 3.0 %collective-permute-start.23 = (bf16[272,256]{1,0:T(8,128)(2,1)S(1)}, bf16[272,256]{1,0:T(8,128)(2,1)S(1)}, u32[]{:S(2)}, u32[]{:S(2)}) collective-permute-start(bf16[272,256]{1,0:T(8,128)(2,1)S(1)} %get-tuple-element.59), channel_id=1, source_target_pairs={{0,8},{2,10},{4,12},{6,14},{8,0},{10,2},{12,4},{14,6},{1,9},{3,11}... | collective-permute-start | bytes 417800 | tf_op jit(solution)/shard_map/ppermute | solution.py:794
  88.2 1.9 %collective-permute-start.24 = (bf16[272,256]{1,0:T(8,128)(2,1)S(1)}, bf16[272,256]{1,0:T(8,128)(2,1)S(1)}, u32[]{:S(2)}, u32[]{:S(2)}) collective-permute-start(bf16[272,256]{1,0:T(8,128)(2,1)S(1)} %get-tuple-element.60), channel_id=1, source_target_pairs={{0,12},{2,14},{4,8},{6,10},{8,4},{10,6},{12,0},{14,2},{1,13},{3,15... | collective-permute-start | bytes 417800 | tf_op jit(solution)/shard_map/ppermute | solution.py:794
  90.1 8.4 %collective-permute-done.23.refs_2_ = bf16[272,256]{1,0:T(8,128)(2,1)S(1)} collective-permute-done((bf16[272,256]{1,0:T(8,128)(2,1)S(1)}, bf16[272,256]{1,0:T(8,128)(2,1)S(1)}, u32[]{:S(2)}, u32[]{:S(2)}) %collective-permute-start.23) | collective-permute-done | bytes 139296 | tf_op jit(solution)/shard_map/ppermute | solution.py:794
  (54 shorter events, 21.2 us)
Async XLA Ops:
  11.3 6.5 %collective-permute-start = (bf16[3,32,512]{2,1,0:T(8,128)(2,1)S(1)}, bf16[3,32,512]{2,1,0:T(8,128)(2,1)S(1)}, u32[]{:S(2)}, u32[]{:S(2)}) collective-permute-start(bf16[3,32,512]{2,1,0:T(8,128)(2,1)S(1)} %get-tuple-element.36), channel_id=1, source_target_pairs={{0,2},{2,0},{4,6},{6,4},{8,10},{10,8},{12,14},{14,12},{1,3},{3,1},... | collective-permute-start | bytes 294920 | tf_op jit(solution)/shard_map/ppermute | solution.py:803
  14.3 12.1 %collective-permute-start.4 = (bf16[32,512]{1,0:T(8,128)(2,1)S(1)}, bf16[32,512]{1,0:T(8,128)(2,1)S(1)}, u32[]{:S(2)}, u32[]{:S(2)}) collective-permute-start(bf16[32,512]{1,0:T(8,128)(2,1)S(1)} %get-tuple-element.37), channel_id=1, source_target_pairs={{0,2},{2,0},{4,6},{6,4},{8,10},{10,8},{12,14},{14,12},{1,3},{3,1},... | collective-permute-start | bytes 98312 | tf_op jit(solution)/shard_map/ppermute | solution.py:803
  14.4 15.2 %collective-permute-start.6 = (bf16[4,2,128,256]{3,2,1,0:T(8,128)(2,1)S(1)}, bf16[4,2,128,256]{3,2,1,0:T(8,128)(2,1)S(1)}, u32[]{:S(2)}, u32[]{:S(2)}) collective-permute-start(bf16[4,2,128,256]{3,2,1,0:T(8,128)(2,1)S(1)} %get-tuple-element.44), channel_id=1, source_target_pairs={{0,2},{2,0},{4,6},{6,4},{8,10},{10,8},{12,14},{14,12},{1,3},{3,1},... | collective-permute-start | bytes 1572872 | tf_op jit(solution)/shard_map/ppermute | solution.py:803
  17.9 8.6 %collective-permute-start.1 = (bf16[32,512]{1,0:T(8,128)(2,1)S(1)}, bf16[32,512]{1,0:T(8,128)(2,1)S(1)}, u32[]{:S(2)}, u32[]{:S(2)}) collective-permute-start(bf16[32,512]{1,0:T(8,128)(2,1)S(1)} %get-tuple-element.67), channel_id=1, source_target_pairs={{0,8},{2,10},{4,12},{6,14},{8,0},{10,2},{12,4},{14,6},{1,9},{3,11}... | collective-permute-start | bytes 98312 | tf_op jit(solution)/shard_map/ppermute | solution.py:794
  21.1 5.7 %collective-permute-start.2 = (bf16[32,512]{1,0:T(8,128)(2,1)S(1)}, bf16[32,512]{1,0:T(8,128)(2,1)S(1)}, u32[]{:S(2)}, u32[]{:S(2)}) collective-permute-start(bf16[32,512]{1,0:T(8,128)(2,1)S(1)} %get-tuple-element.69), channel_id=1, source_target_pairs={{0,12},{2,14},{4,8},{6,10},{8,4},{10,6},{12,0},{14,2},{1,13},{3,15... | collective-permute-start | bytes 98312 | tf_op jit(solution)/shard_map/ppermute | solution.py:794
  22.4 4.4 %collective-permute-start.3 = (bf16[32,512]{1,0:T(8,128)(2,1)S(1)}, bf16[32,512]{1,0:T(8,128)(2,1)S(1)}, u32[]{:S(2)}, u32[]{:S(2)}) collective-permute-start(bf16[32,512]{1,0:T(8,128)(2,1)S(1)} %get-tuple-element.68), channel_id=1, source_target_pairs={{0,4},{2,6},{4,0},{6,2},{8,12},{10,14},{12,8},{14,10},{1,5},{3,7},... | collective-permute-start | bytes 98312 | tf_op jit(solution)/shard_map/ppermute | solution.py:794
  29.6 7.7 %collective-permute-start.7 = (bf16[3,4,64,128]{3,2,1,0:T(8,128)(2,1)S(1)}, bf16[3,4,64,128]{3,2,1,0:T(8,128)(2,1)S(1)}, u32[]{:S(2)}, u32[]{:S(2)}) collective-permute-start(bf16[3,4,64,128]{3,2,1,0:T(8,128)(2,1)S(1)} %get-tuple-element.45), channel_id=1, source_target_pairs={{0,2},{2,0},{4,6},{6,4},{8,10},{10,8},{12,14},{14,12},{1,3},{3,1},... | collective-permute-start | bytes 589832 | tf_op jit(solution)/shard_map/ppermute | solution.py:803
  31.3 14.3 %collective-permute-start.11 = (bf16[4,64,128]{2,1,0:T(8,128)(2,1)S(1)}, bf16[4,64,128]{2,1,0:T(8,128)(2,1)S(1)}, u32[]{:S(2)}, u32[]{:S(2)}) collective-permute-start(bf16[4,64,128]{2,1,0:T(8,128)(2,1)S(1)} %get-tuple-element.46), channel_id=1, source_target_pairs={{0,2},{2,0},{4,6},{6,4},{8,10},{10,8},{12,14},{14,12},{1,3},{3,1},... | collective-permute-start | bytes 196616 | tf_op jit(solution)/shard_map/ppermute | solution.py:803
  37.4 8.2 %collective-permute-start.10 = (bf16[4,64,128]{2,1,0:T(8,128)(2,1)S(1)}, bf16[4,64,128]{2,1,0:T(8,128)(2,1)S(1)}, u32[]{:S(2)}, u32[]{:S(2)}) collective-permute-start(bf16[4,64,128]{2,1,0:T(8,128)(2,1)S(1)} %get-tuple-element.65), channel_id=1, source_target_pairs={{0,4},{2,6},{4,0},{6,2},{8,12},{10,14},{12,8},{14,10},{1,5},{3,7},... | collective-permute-start | bytes 196616 | tf_op jit(solution)/shard_map/ppermute | solution.py:794
  39.0 6.6 %collective-permute-start.8 = (bf16[4,64,128]{2,1,0:T(8,128)(2,1)S(1)}, bf16[4,64,128]{2,1,0:T(8,128)(2,1)S(1)}, u32[]{:S(2)}, u32[]{:S(2)}) collective-permute-start(bf16[4,64,128]{2,1,0:T(8,128)(2,1)S(1)} %get-tuple-element.64), channel_id=1, source_target_pairs={{0,8},{2,10},{4,12},{6,14},{8,0},{10,2},{12,4},{14,6},{1,9},{3,11}... | collective-permute-start | bytes 196616 | tf_op jit(solution)/shard_map/ppermute | solution.py:794
  40.7 6.1 %collective-permute-start.9 = (bf16[4,64,128]{2,1,0:T(8,128)(2,1)S(1)}, bf16[4,64,128]{2,1,0:T(8,128)(2,1)S(1)}, u32[]{:S(2)}, u32[]{:S(2)}) collective-permute-start(bf16[4,64,128]{2,1,0:T(8,128)(2,1)S(1)} %get-tuple-element.66), channel_id=1, source_target_pairs={{0,12},{2,14},{4,8},{6,10},{8,4},{10,6},{12,0},{14,2},{1,13},{3,15... | collective-permute-start | bytes 196616 | tf_op jit(solution)/shard_map/ppermute | solution.py:794
  46.8 5.2 %collective-permute-start.12 = (bf16[4,64,128]{2,1,0:T(8,128)(2,1)S(1)}, bf16[4,64,128]{2,1,0:T(8,128)(2,1)S(1)}, u32[]{:S(2)}, u32[]{:S(2)}) collective-permute-start(bf16[4,64,128]{2,1,0:T(8,128)(2,1)S(1)} %multiply_convert_fusion.rest_0_), channel_id=1, source_target_pairs={{0,8},{2,10},{4,12},{6,14},{8,0},{10,2},{12,4},{14,6},{1,9},{3,11}... | collective-permute-start | bytes 196616 | tf_op jit(solution)/shard_map/ppermute | solution.py:794
  47.9 6.1 %collective-permute-start.13 = (bf16[4,64,128]{2,1,0:T(8,128)(2,1)S(1)}, bf16[4,64,128]{2,1,0:T(8,128)(2,1)S(1)}, u32[]{:S(2)}, u32[]{:S(2)}) collective-permute-start(bf16[4,64,128]{2,1,0:T(8,128)(2,1)S(1)} %multiply_convert_fusion.rest_0_), channel_id=1, source_target_pairs={{0,12},{2,14},{4,8},{6,10},{8,4},{10,6},{12,0},{14,2},{1,13},{3,15... | collective-permute-start | bytes 196616 | tf_op jit(solution)/shard_map/ppermute | solution.py:794
  48.9 5.1 %collective-permute-start.14 = (bf16[4,64,128]{2,1,0:T(8,128)(2,1)S(1)}, bf16[4,64,128]{2,1,0:T(8,128)(2,1)S(1)}, u32[]{:S(2)}, u32[]{:S(2)}) collective-permute-start(bf16[4,64,128]{2,1,0:T(8,128)(2,1)S(1)} %multiply_convert_fusion.rest_0_), channel_id=1, source_target_pairs={{0,4},{2,6},{4,0},{6,2},{8,12},{10,14},{12,8},{14,10},{1,5},{3,7},... | collective-permute-start | bytes 196616 | tf_op jit(solution)/shard_map/ppermute | solution.py:794
  54.0 6.4 %collective-permute-start.15 = (bf16[3,4,64,128]{3,2,1,0:T(8,128)(2,1)S(1)}, bf16[3,4,64,128]{3,2,1,0:T(8,128)(2,1)S(1)}, u32[]{:S(2)}, u32[]{:S(2)}) collective-permute-start(bf16[3,4,64,128]{3,2,1,0:T(8,128)(2,1)S(1)} %pad_maximum_fusion), channel_id=1, source_target_pairs={{0,2},{2,0},{4,6},{6,4},{8,10},{10,8},{12,14},{14,12},{1,3},{3,1},... | collective-permute-start | bytes 589832 | tf_op jit(solution)/shard_map/ppermute | solution.py:803
  55.7 4.7 %collective-permute-start.16 = (bf16[4,64,128]{2,1,0:T(8,128)(2,1)S(1)}, bf16[4,64,128]{2,1,0:T(8,128)(2,1)S(1)}, u32[]{:S(2)}, u32[]{:S(2)}) collective-permute-start(bf16[4,64,128]{2,1,0:T(8,128)(2,1)S(1)} %multiply_convert_fusion.rest_0_), channel_id=1, source_target_pairs={{0,2},{2,0},{4,6},{6,4},{8,10},{10,8},{12,14},{14,12},{1,3},{3,1},... | collective-permute-start | bytes 196616 | tf_op jit(solution)/shard_map/ppermute | solution.py:803
  56.1 25.5 %collective-permute-start.22 = (bf16[4,2,128,256]{3,2,1,0:T(8,128)(2,1)S(1)}, bf16[4,2,128,256]{3,2,1,0:T(8,128)(2,1)S(1)}, u32[]{:S(2)}, u32[]{:S(2)}) collective-permute-start(bf16[4,2,128,256]{3,2,1,0:T(8,128)(2,1)S(1)} %collective-permute-done.6.early_ref), channel_id=1, source_target_pairs={{0,16},{16,0},{1,17},{17,1},{2,18},{18,2},{3,19},{19,3},{4,20},{20... | collective-permute-start | bytes 1572872 | tf_op jit(solution)/shard_map/ppermute | solution.py:835
  65.3 12.5 %collective-permute-start.18 = (bf16[4,64,256]{2,1,0:T(8,128)(2,1)S(1)}, bf16[4,64,256]{2,1,0:T(8,128)(2,1)S(1)}, u32[]{:S(2)}, u32[]{:S(2)}) collective-permute-start(bf16[4,64,256]{2,1,0:T(8,128)(2,1)S(1)} %get-tuple-element.52), channel_id=1, source_target_pairs={{0,8},{2,10},{4,12},{6,14},{8,0},{10,2},{12,4},{14,6},{1,9},{3,11}... | collective-permute-start | bytes 393224 | tf_op jit(solution)/shard_map/ppermute | solution.py:794
  66.7 11.2 %collective-permute-start.19 = (bf16[4,64,256]{2,1,0:T(8,128)(2,1)S(1)}, bf16[4,64,256]{2,1,0:T(8,128)(2,1)S(1)}, u32[]{:S(2)}, u32[]{:S(2)}) collective-permute-start(bf16[4,64,256]{2,1,0:T(8,128)(2,1)S(1)} %get-tuple-element.53), channel_id=1, source_target_pairs={{0,12},{2,14},{4,8},{6,10},{8,4},{10,6},{12,0},{14,2},{1,13},{3,15... | collective-permute-start | bytes 393224 | tf_op jit(solution)/shard_map/ppermute | solution.py:794
  68.4 10.7 %collective-permute-start.20 = (bf16[4,64,256]{2,1,0:T(8,128)(2,1)S(1)}, bf16[4,64,256]{2,1,0:T(8,128)(2,1)S(1)}, u32[]{:S(2)}, u32[]{:S(2)}) collective-permute-start(bf16[4,64,256]{2,1,0:T(8,128)(2,1)S(1)} %get-tuple-element.54), channel_id=1, source_target_pairs={{0,4},{2,6},{4,0},{6,2},{8,12},{10,14},{12,8},{14,10},{1,5},{3,7},... | collective-permute-start | bytes 393224 | tf_op jit(solution)/shard_map/ppermute | solution.py:794
  79.1 5.0 %collective-permute-start.21 = (bf16[4,64,256]{2,1,0:T(8,128)(2,1)S(1)}, bf16[4,64,256]{2,1,0:T(8,128)(2,1)S(1)}, u32[]{:S(2)}, u32[]{:S(2)}) collective-permute-start(bf16[4,64,256]{2,1,0:T(8,128)(2,1)S(1)} %get-tuple-element.62), channel_id=1, source_target_pairs={{0,2},{2,0},{4,6},{6,4},{8,10},{10,8},{12,14},{14,12},{1,3},{3,1},... | collective-permute-start | bytes 393224 | tf_op jit(solution)/shard_map/ppermute | solution.py:803
  85.2 13.3 %collective-permute-start.23 = (bf16[272,256]{1,0:T(8,128)(2,1)S(1)}, bf16[272,256]{1,0:T(8,128)(2,1)S(1)}, u32[]{:S(2)}, u32[]{:S(2)}) collective-permute-start(bf16[272,256]{1,0:T(8,128)(2,1)S(1)} %get-tuple-element.59), channel_id=1, source_target_pairs={{0,8},{2,10},{4,12},{6,14},{8,0},{10,2},{12,4},{14,6},{1,9},{3,11}... | collective-permute-start | bytes 417800 | tf_op jit(solution)/shard_map/ppermute | solution.py:794
  88.2 10.3 %collective-permute-start.24 = (bf16[272,256]{1,0:T(8,128)(2,1)S(1)}, bf16[272,256]{1,0:T(8,128)(2,1)S(1)}, u32[]{:S(2)}, u32[]{:S(2)}) collective-permute-start(bf16[272,256]{1,0:T(8,128)(2,1)S(1)} %get-tuple-element.60), channel_id=1, source_target_pairs={{0,12},{2,14},{4,8},{6,10},{8,4},{10,6},{12,0},{14,2},{1,13},{3,15... | collective-permute-start | bytes 417800 | tf_op jit(solution)/shard_map/ppermute | solution.py:794
  90.1 8.6 %collective-permute-start.25 = (bf16[272,256]{1,0:T(8,128)(2,1)S(1)}, bf16[272,256]{1,0:T(8,128)(2,1)S(1)}, u32[]{:S(2)}, u32[]{:S(2)}) collective-permute-start(bf16[272,256]{1,0:T(8,128)(2,1)S(1)} %get-tuple-element.61), channel_id=1, source_target_pairs={{0,4},{2,6},{4,0},{6,2},{8,12},{10,14},{12,8},{14,10},{1,5},{3,7},... | collective-permute-start | bytes 417800 | tf_op jit(solution)/shard_map/ppermute | solution.py:794
  (5 other events, 49.9 us)

commit v7 on v6

--- a/solution.py
+++ b/solution.py
@@ -836,7 +836,7 @@
     own_gain, near_qkv, near_out, *own_columns = brought_near(
         place, token, depth_gain, depth_qkv, depth_out_weight, head_weight, tp
     )
-    entry_terms = summed(kept, last, sent, order)
+    entry_terms = summed(kept, last, sent, list(range(far)))
     scaled = (added(entry_terms) * own_gain[None]).astype(jnp.bfloat16)
     near = [scaled] + in_order(to_pairs([scaled] * far), order)
     last = to_neighbour(scaled)

time: 99.8 us -> 99.9 us (level)
  transfers between devices with their start and end apart: 26 -> 26, of which waited for: 14 -> 15; matrix products, arithmetic and copies ran while one was open for 1% -> 1% of each run, Pallas kernels for 11% -> 11%
where the time goes in v7:
time: 99.9 us; the launch traced here: 99.7 us
  waiting for transfers between devices  38.3 us (38%)
  starting transfers between devices  35.4 us (35%)
  Pallas kernels  23.9 us (24%)
    ppermute x15, waiting for transfers between devices, to_pairs(): lax.ppermute(blocks[k], 'tp', [(i, i ^ 2 * (k + 1)) for i in range(tp)])  23.6 us
    ppermute x15, starting transfers between devices, to_pairs(): lax.ppermute(blocks[k], 'tp', [(i, i ^ 2 * (k + 1)) for i in range(tp)])  21.6 us
    ppermute x8, waiting for transfers between devices, to_neighbour(): return lax.ppermute(block, 'tp', [(i, i ^ 1) for i in range(tp)])  12.6 us
    ppermute x8, starting transfers between devices, to_neighbour(): return lax.ppermute(block, 'tp', [(i, i ^ 1) for i in range(tp)])  10.9 us
    pallas_call x1, Pallas kernels, temporal_parts(): pl.pallas_call(temporal_kernel, in_specs=[SMEM] + [HBM] * 8, out_specs=[V...  10.6 us
    pallas_call x1, Pallas kernels, brought_near(): pl.pallas_call(near_kernel, in_specs=[SMEM, VMEM, VMEM, HBM, HBM, HBM], o...  3.67 us
    pallas_call x1, Pallas kernels, prepared_entry(): pl.pallas_call(prepare_kernel, in_specs=[SMEM, VMEM, HBM, HBM, HBM], out_...  3.66 us
  transfers between devices with their start and end apart: 26, of which 15 were waited for; matrix products, arithmetic and copies ran while one was open for 1% of the time, Pallas kernels for 11%

profile of v7, /device:TPU:0, one launch (start us, length us, event | category | flops | bytes accessed | tf_op | source)
XLA Modules:
  0.0 99.7 jit_solution(9100852128989010561)
XLA Ops:
  0.7 10.6 %temporal.1 = (f32[4,32,512]{2,1,0:T(8,128)S(1)}, bf16[32,512]{1,0:T(8,128)(2,1)S(1)}, bf16[3,32,512]{2,1,0:T(8,128)(2,1)S(1)}, bf16[4,2,128,256]{3,2,1,0:T(8,128)(2,1)S(1)}) custom-call(s32[3]{0:T(128)S(1)} %pad_add_fusion.place_ref, bf16[32,4096]{1,0:T(8,128)(2,1)} %hidden_hbm.3, f32[1,4096]{1,0:T(1,128)} %bitcast.46, s32[1,32]{1,0:T(1,128)} %bitcast.47, ...), custom_call_target="tpu_custom_call" | custom-call | tf_op jit(solution)/shard_map/temporal/pallas_call | solution.py:398
  11.3 3.0 %collective-permute-start = (bf16[3,32,512]{2,1,0:T(8,128)(2,1)S(1)}, bf16[3,32,512]{2,1,0:T(8,128)(2,1)S(1)}, u32[]{:S(2)}, u32[]{:S(2)}) collective-permute-start(bf16[3,32,512]{2,1,0:T(8,128)(2,1)S(1)} %get-tuple-element.36), channel_id=1, source_target_pairs={{0,2},{2,0},{4,6},{6,4},{8,10},{10,8},{12,14},{14,12},{1,3},{3,1},... | collective-permute-start | bytes 294920 | tf_op jit(solution)/shard_map/ppermute | solution.py:803
  14.4 1.9 %collective-permute-start.6 = (bf16[4,2,128,256]{3,2,1,0:T(8,128)(2,1)S(1)}, bf16[4,2,128,256]{3,2,1,0:T(8,128)(2,1)S(1)}, u32[]{:S(2)}, u32[]{:S(2)}) collective-permute-start(bf16[4,2,128,256]{3,2,1,0:T(8,128)(2,1)S(1)} %get-tuple-element.44), channel_id=1, source_target_pairs={{0,2},{2,0},{4,6},{6,4},{8,10},{10,8},{12,14},{14,12},{1,3},{3,1},... | collective-permute-start | bytes 1572872 | tf_op jit(solution)/shard_map/ppermute | solution.py:803
  16.4 1.5 %collective-permute-done = bf16[3,32,512]{2,1,0:T(8,128)(2,1)S(1)} collective-permute-done((bf16[3,32,512]{2,1,0:T(8,128)(2,1)S(1)}, bf16[3,32,512]{2,1,0:T(8,128)(2,1)S(1)}, u32[]{:S(2)}, u32[]{:S(2)}) %collective-permute-start) | collective-permute-done | bytes 98336 | tf_op jit(solution)/shard_map/ppermute | solution.py:803
  17.9 3.2 %collective-permute-start.1 = (bf16[32,512]{1,0:T(8,128)(2,1)S(1)}, bf16[32,512]{1,0:T(8,128)(2,1)S(1)}, u32[]{:S(2)}, u32[]{:S(2)}) collective-permute-start(bf16[32,512]{1,0:T(8,128)(2,1)S(1)} %get-tuple-element.67), channel_id=1, source_target_pairs={{0,8},{2,10},{4,12},{6,14},{8,0},{10,2},{12,4},{14,6},{1,9},{3,11}... | collective-permute-start | bytes 98312 | tf_op jit(solution)/shard_map/ppermute | solution.py:794
  22.8 3.7 %entry_prepare.1 = (bf16[32,512]{1,0:T(8,128)(2,1)S(1)}, f32[4,64,1024]{2,1,0:T(8,128)S(1)}, bf16[4,512,1024]{2,1,0:T(8,128)(2,1)S(1)}) custom-call(s32[3]{0:T(128)S(1)} %pad_add_fusion.place_ref, s32[64,4]{1,0:T(8,128)S(1)} %copy.17.tokens_ref, bf16[32,4096]{1,0:T(8,128)(2,1)} %hidden_hbm.3, bf16[4,256,1024]{2,1,0:T(8,128)(2,1)} %embed_hbm.1, ...), custom_call_target="tpu_custom_call" | custom-call | tf_op jit(solution)/shard_map/entry_prepare/pallas_call | solution.py:461
  28.1 1.5 %entry.1 = (f32[4,4,64,128]{3,2,1,0:T(8,128)S(1)}, bf16[4,64,128]{2,1,0:T(8,128)(2,1)S(1)}, bf16[3,4,64,128]{3,2,1,0:T(8,128)(2,1)S(1)}, f32[8,128]{1,0:T(8,128)S(1)}) custom-call(s32[3]{0:T(128)S(1)} %pad_add_fusion.place_ref, bf16[32,512]{1,0:T(8,128)(2,1)S(1)} %fusion.4.own_ref, bf16[32,512]{1,0:T(8,128)(2,1)S(1)} %collective-permute-done.5.other_ref, ...), custom_call_target="tpu_custom_call" | custom-call | tf_op jit(solution)/shard_map/entry/pallas_call | solution.py:552
  29.6 1.7 %collective-permute-start.7 = (bf16[3,4,64,128]{3,2,1,0:T(8,128)(2,1)S(1)}, bf16[3,4,64,128]{3,2,1,0:T(8,128)(2,1)S(1)}, u32[]{:S(2)}, u32[]{:S(2)}) collective-permute-start(bf16[3,4,64,128]{3,2,1,0:T(8,128)(2,1)S(1)} %get-tuple-element.45), channel_id=1, source_target_pairs={{0,2},{2,0},{4,6},{6,4},{8,10},{10,8},{12,14},{14,12},{1,3},{3,1},... | collective-permute-start | bytes 589832 | tf_op jit(solution)/shard_map/ppermute | solution.py:803
  31.7 5.6 %collective-permute-done.7 = bf16[3,4,64,128]{3,2,1,0:T(8,128)(2,1)S(1)} collective-permute-done((bf16[3,4,64,128]{3,2,1,0:T(8,128)(2,1)S(1)}, bf16[3,4,64,128]{3,2,1,0:T(8,128)(2,1)S(1)}, u32[]{:S(2)}, u32[]{:S(2)}) %collective-permute-start.7) | collective-permute-done | bytes 196640 | tf_op jit(solution)/shard_map/ppermute | solution.py:803
  37.4 2.7 %collective-permute-start.10 = (bf16[4,64,128]{2,1,0:T(8,128)(2,1)S(1)}, bf16[4,64,128]{2,1,0:T(8,128)(2,1)S(1)}, u32[]{:S(2)}, u32[]{:S(2)}) collective-permute-start(bf16[4,64,128]{2,1,0:T(8,128)(2,1)S(1)} %get-tuple-element.65), channel_id=1, source_target_pairs={{0,12},{2,14},{4,8},{6,10},{8,4},{10,6},{12,0},{14,2},{1,13},{3,15... | collective-permute-start | bytes 196616 | tf_op jit(solution)/shard_map/ppermute | solution.py:794
  41.9 3.7 %brought_near.1 = (f32[1,128]{1,0:T(1,128)S(1)}, bf16[4,3,1024,128]{3,2,1,0:T(8,128)(2,1)S(1)}, bf16[4,128,1024]{2,1,0:T(8,128)(2,1)S(1)}, bf16[4,4,128,256]{3,2,1,0:T(8,128)(2,1)S(1)}) custom-call(s32[3]{0:T(128)S(1)} %pad_add_fusion.place_ref, f32[8,128]{1,0:T(8,128)S(1)} %get-tuple-element.40.token_ref, f32[1,1024]{1,0:T(1,128)S(1)} %bitcast.42, ...), custom_call_target="tpu_custom_call" | custom-call | tf_op jit(solution)/shard_map/brought_near/pallas_call | solution.py:504
  45.8 1.5 %collective-permute-start.12 = (bf16[4,64,128]{2,1,0:T(8,128)(2,1)S(1)}, bf16[4,64,128]{2,1,0:T(8,128)(2,1)S(1)}, u32[]{:S(2)}, u32[]{:S(2)}) collective-permute-start(bf16[4,64,128]{2,1,0:T(8,128)(2,1)S(1)} %multiply_convert_fusion.rest_0_), channel_id=1, source_target_pairs={{0,8},{2,10},{4,12},{6,14},{8,0},{10,2},{12,4},{14,6},{1,9},{3,11}... | collective-permute-start | bytes 196616 | tf_op jit(solution)/shard_map/ppermute | solution.py:794
  47.3 2.5 %collective-permute-start.13 = (bf16[4,64,128]{2,1,0:T(8,128)(2,1)S(1)}, bf16[4,64,128]{2,1,0:T(8,128)(2,1)S(1)}, u32[]{:S(2)}, u32[]{:S(2)}) collective-permute-start(bf16[4,64,128]{2,1,0:T(8,128)(2,1)S(1)} %multiply_convert_fusion.rest_0_), channel_id=1, source_target_pairs={{0,12},{2,14},{4,8},{6,10},{8,4},{10,6},{12,0},{14,2},{1,13},{3,15... | collective-permute-start | bytes 196616 | tf_op jit(solution)/shard_map/ppermute | solution.py:794
  51.1 2.4 %collective-permute-done.13.rest_2_ = bf16[4,64,128]{2,1,0:T(8,128)(2,1)S(1)} collective-permute-done((bf16[4,64,128]{2,1,0:T(8,128)(2,1)S(1)}, bf16[4,64,128]{2,1,0:T(8,128)(2,1)S(1)}, u32[]{:S(2)}, u32[]{:S(2)}) %collective-permute-start.13) | collective-permute-done | bytes 65568 | tf_op jit(solution)/shard_map/ppermute | solution.py:794
  54.1 1.7 %collective-permute-start.15 = (bf16[3,4,64,128]{3,2,1,0:T(8,128)(2,1)S(1)}, bf16[3,4,64,128]{3,2,1,0:T(8,128)(2,1)S(1)}, u32[]{:S(2)}, u32[]{:S(2)}) collective-permute-start(bf16[3,4,64,128]{3,2,1,0:T(8,128)(2,1)S(1)} %pad_maximum_fusion), channel_id=1, source_target_pairs={{0,2},{2,0},{4,6},{6,4},{8,10},{10,8},{12,14},{14,12},{1,3},{3,1},... | collective-permute-start | bytes 589832 | tf_op jit(solution)/shard_map/ppermute | solution.py:803
  56.2 1.5 %collective-permute-start.22 = (bf16[4,2,128,256]{3,2,1,0:T(8,128)(2,1)S(1)}, bf16[4,2,128,256]{3,2,1,0:T(8,128)(2,1)S(1)}, u32[]{:S(2)}, u32[]{:S(2)}) collective-permute-start(bf16[4,2,128,256]{3,2,1,0:T(8,128)(2,1)S(1)} %collective-permute-done.6.early_ref), channel_id=1, source_target_pairs={{0,16},{16,0},{1,17},{17,1},{2,18},{18,2},{3,19},{19,3},{4,20},{20... | collective-permute-start | bytes 1572872 | tf_op jit(solution)/shard_map/ppermute | solution.py:835
  57.7 2.9 %collective-permute-done.16.rest_4_ = bf16[4,64,128]{2,1,0:T(8,128)(2,1)S(1)} collective-permute-done((bf16[4,64,128]{2,1,0:T(8,128)(2,1)S(1)}, bf16[4,64,128]{2,1,0:T(8,128)(2,1)S(1)}, u32[]{:S(2)}, u32[]{:S(2)}) %collective-permute-start.16) | collective-permute-done | bytes 65568 | tf_op jit(solution)/shard_map/ppermute | solution.py:803
  66.1 2.4 %collective-permute-start.19 = (bf16[4,64,256]{2,1,0:T(8,128)(2,1)S(1)}, bf16[4,64,256]{2,1,0:T(8,128)(2,1)S(1)}, u32[]{:S(2)}, u32[]{:S(2)}) collective-permute-start(bf16[4,64,256]{2,1,0:T(8,128)(2,1)S(1)} %get-tuple-element.53), channel_id=1, source_target_pairs={{0,12},{2,14},{4,8},{6,10},{8,4},{10,6},{12,0},{14,2},{1,13},{3,15... | collective-permute-start | bytes 393224 | tf_op jit(solution)/shard_map/ppermute | solution.py:794
  69.0 9.0 %collective-permute-done.18 = bf16[4,64,256]{2,1,0:T(8,128)(2,1)S(1)} collective-permute-done((bf16[4,64,256]{2,1,0:T(8,128)(2,1)S(1)}, bf16[4,64,256]{2,1,0:T(8,128)(2,1)S(1)}, u32[]{:S(2)}, u32[]{:S(2)}) %collective-permute-start.18) | collective-permute-done | bytes 131104 | tf_op jit(solution)/shard_map/ppermute | solution.py:794
  79.2 1.7 %collective-permute-start.21 = (bf16[4,64,256]{2,1,0:T(8,128)(2,1)S(1)}, bf16[4,64,256]{2,1,0:T(8,128)(2,1)S(1)}, u32[]{:S(2)}, u32[]{:S(2)}) collective-permute-start(bf16[4,64,256]{2,1,0:T(8,128)(2,1)S(1)} %get-tuple-element.62), channel_id=1, source_target_pairs={{0,2},{2,0},{4,6},{6,4},{8,10},{10,8},{12,14},{14,12},{1,3},{3,1},... | collective-permute-start | bytes 393224 | tf_op jit(solution)/shard_map/ppermute | solution.py:803
  81.7 2.6 %collective-permute-done.21.arrived_ref = bf16[4,64,256]{2,1,0:T(8,128)(2,1)S(1)} collective-permute-done((bf16[4,64,256]{2,1,0:T(8,128)(2,1)S(1)}, bf16[4,64,256]{2,1,0:T(8,128)(2,1)S(1)}, u32[]{:S(2)}, u32[]{:S(2)}) %collective-permute-start.21) | collective-permute-done | bytes 131104 | tf_op jit(solution)/shard_map/ppermute | solution.py:803
  85.3 2.6 %collective-permute-start.23 = (bf16[272,256]{1,0:T(8,128)(2,1)S(1)}, bf16[272,256]{1,0:T(8,128)(2,1)S(1)}, u32[]{:S(2)}, u32[]{:S(2)}) collective-permute-start(bf16[272,256]{1,0:T(8,128)(2,1)S(1)} %get-tuple-element.59), channel_id=1, source_target_pairs={{0,8},{2,10},{4,12},{6,14},{8,0},{10,2},{12,4},{14,6},{1,9},{3,11}... | collective-permute-start | bytes 417800 | tf_op jit(solution)/shard_map/ppermute | solution.py:794
  87.9 2.3 %collective-permute-start.24 = (bf16[272,256]{1,0:T(8,128)(2,1)S(1)}, bf16[272,256]{1,0:T(8,128)(2,1)S(1)}, u32[]{:S(2)}, u32[]{:S(2)}) collective-permute-start(bf16[272,256]{1,0:T(8,128)(2,1)S(1)} %get-tuple-element.60), channel_id=1, source_target_pairs={{0,12},{2,14},{4,8},{6,10},{8,4},{10,6},{12,0},{14,2},{1,13},{3,15... | collective-permute-start | bytes 417800 | tf_op jit(solution)/shard_map/ppermute | solution.py:794
  90.2 8.3 %collective-permute-done.23.refs_2_ = bf16[272,256]{1,0:T(8,128)(2,1)S(1)} collective-permute-done((bf16[272,256]{1,0:T(8,128)(2,1)S(1)}, bf16[272,256]{1,0:T(8,128)(2,1)S(1)}, u32[]{:S(2)}, u32[]{:S(2)}) %collective-permute-start.23) | collective-permute-done | bytes 139296 | tf_op jit(solution)/shard_map/ppermute | solution.py:794
  (54 shorter events, 18.6 us)
Async XLA Ops:
  11.3 6.5 %collective-permute-start = (bf16[3,32,512]{2,1,0:T(8,128)(2,1)S(1)}, bf16[3,32,512]{2,1,0:T(8,128)(2,1)S(1)}, u32[]{:S(2)}, u32[]{:S(2)}) collective-permute-start(bf16[3,32,512]{2,1,0:T(8,128)(2,1)S(1)} %get-tuple-element.36), channel_id=1, source_target_pairs={{0,2},{2,0},{4,6},{6,4},{8,10},{10,8},{12,14},{14,12},{1,3},{3,1},... | collective-permute-start | bytes 294920 | tf_op jit(solution)/shard_map/ppermute | solution.py:803
  14.3 12.1 %collective-permute-start.4 = (bf16[32,512]{1,0:T(8,128)(2,1)S(1)}, bf16[32,512]{1,0:T(8,128)(2,1)S(1)}, u32[]{:S(2)}, u32[]{:S(2)}) collective-permute-start(bf16[32,512]{1,0:T(8,128)(2,1)S(1)} %get-tuple-element.37), channel_id=1, source_target_pairs={{0,2},{2,0},{4,6},{6,4},{8,10},{10,8},{12,14},{14,12},{1,3},{3,1},... | collective-permute-start | bytes 98312 | tf_op jit(solution)/shard_map/ppermute | solution.py:803
  14.4 15.2 %collective-permute-start.6 = (bf16[4,2,128,256]{3,2,1,0:T(8,128)(2,1)S(1)}, bf16[4,2,128,256]{3,2,1,0:T(8,128)(2,1)S(1)}, u32[]{:S(2)}, u32[]{:S(2)}) collective-permute-start(bf16[4,2,128,256]{3,2,1,0:T(8,128)(2,1)S(1)} %get-tuple-element.44), channel_id=1, source_target_pairs={{0,2},{2,0},{4,6},{6,4},{8,10},{10,8},{12,14},{14,12},{1,3},{3,1},... | collective-permute-start | bytes 1572872 | tf_op jit(solution)/shard_map/ppermute | solution.py:803
  17.9 8.6 %collective-permute-start.1 = (bf16[32,512]{1,0:T(8,128)(2,1)S(1)}, bf16[32,512]{1,0:T(8,128)(2,1)S(1)}, u32[]{:S(2)}, u32[]{:S(2)}) collective-permute-start(bf16[32,512]{1,0:T(8,128)(2,1)S(1)} %get-tuple-element.67), channel_id=1, source_target_pairs={{0,8},{2,10},{4,12},{6,14},{8,0},{10,2},{12,4},{14,6},{1,9},{3,11}... | collective-permute-start | bytes 98312 | tf_op jit(solution)/shard_map/ppermute | solution.py:794
  21.1 5.7 %collective-permute-start.2 = (bf16[32,512]{1,0:T(8,128)(2,1)S(1)}, bf16[32,512]{1,0:T(8,128)(2,1)S(1)}, u32[]{:S(2)}, u32[]{:S(2)}) collective-permute-start(bf16[32,512]{1,0:T(8,128)(2,1)S(1)} %get-tuple-element.69), channel_id=1, source_target_pairs={{0,12},{2,14},{4,8},{6,10},{8,4},{10,6},{12,0},{14,2},{1,13},{3,15... | collective-permute-start | bytes 98312 | tf_op jit(solution)/shard_map/ppermute | solution.py:794
  22.4 4.4 %collective-permute-start.3 = (bf16[32,512]{1,0:T(8,128)(2,1)S(1)}, bf16[32,512]{1,0:T(8,128)(2,1)S(1)}, u32[]{:S(2)}, u32[]{:S(2)}) collective-permute-start(bf16[32,512]{1,0:T(8,128)(2,1)S(1)} %get-tuple-element.68), channel_id=1, source_target_pairs={{0,4},{2,6},{4,0},{6,2},{8,12},{10,14},{12,8},{14,10},{1,5},{3,7},... | collective-permute-start | bytes 98312 | tf_op jit(solution)/shard_map/ppermute | solution.py:794
  29.6 7.7 %collective-permute-start.7 = (bf16[3,4,64,128]{3,2,1,0:T(8,128)(2,1)S(1)}, bf16[3,4,64,128]{3,2,1,0:T(8,128)(2,1)S(1)}, u32[]{:S(2)}, u32[]{:S(2)}) collective-permute-start(bf16[3,4,64,128]{3,2,1,0:T(8,128)(2,1)S(1)} %get-tuple-element.45), channel_id=1, source_target_pairs={{0,2},{2,0},{4,6},{6,4},{8,10},{10,8},{12,14},{14,12},{1,3},{3,1},... | collective-permute-start | bytes 589832 | tf_op jit(solution)/shard_map/ppermute | solution.py:803
  31.3 14.3 %collective-permute-start.11 = (bf16[4,64,128]{2,1,0:T(8,128)(2,1)S(1)}, bf16[4,64,128]{2,1,0:T(8,128)(2,1)S(1)}, u32[]{:S(2)}, u32[]{:S(2)}) collective-permute-start(bf16[4,64,128]{2,1,0:T(8,128)(2,1)S(1)} %get-tuple-element.46), channel_id=1, source_target_pairs={{0,2},{2,0},{4,6},{6,4},{8,10},{10,8},{12,14},{14,12},{1,3},{3,1},... | collective-permute-start | bytes 196616 | tf_op jit(solution)/shard_map/ppermute | solution.py:803
  37.4 8.2 %collective-permute-start.10 = (bf16[4,64,128]{2,1,0:T(8,128)(2,1)S(1)}, bf16[4,64,128]{2,1,0:T(8,128)(2,1)S(1)}, u32[]{:S(2)}, u32[]{:S(2)}) collective-permute-start(bf16[4,64,128]{2,1,0:T(8,128)(2,1)S(1)} %get-tuple-element.65), channel_id=1, source_target_pairs={{0,12},{2,14},{4,8},{6,10},{8,4},{10,6},{12,0},{14,2},{1,13},{3,15... | collective-permute-start | bytes 196616 | tf_op jit(solution)/shard_map/ppermute | solution.py:794
  40.1 5.7 %collective-permute-start.8 = (bf16[4,64,128]{2,1,0:T(8,128)(2,1)S(1)}, bf16[4,64,128]{2,1,0:T(8,128)(2,1)S(1)}, u32[]{:S(2)}, u32[]{:S(2)}) collective-permute-start(bf16[4,64,128]{2,1,0:T(8,128)(2,1)S(1)} %get-tuple-element.64), channel_id=1, source_target_pairs={{0,4},{2,6},{4,0},{6,2},{8,12},{10,14},{12,8},{14,10},{1,5},{3,7},... | collective-permute-start | bytes 196616 | tf_op jit(solution)/shard_map/ppermute | solution.py:794
  40.5 5.2 %collective-permute-start.9 = (bf16[4,64,128]{2,1,0:T(8,128)(2,1)S(1)}, bf16[4,64,128]{2,1,0:T(8,128)(2,1)S(1)}, u32[]{:S(2)}, u32[]{:S(2)}) collective-permute-start(bf16[4,64,128]{2,1,0:T(8,128)(2,1)S(1)} %get-tuple-element.66), channel_id=1, source_target_pairs={{0,8},{2,10},{4,12},{6,14},{8,0},{10,2},{12,4},{14,6},{1,9},{3,11}... | collective-permute-start | bytes 196616 | tf_op jit(solution)/shard_map/ppermute | solution.py:794
  45.8 5.2 %collective-permute-start.12 = (bf16[4,64,128]{2,1,0:T(8,128)(2,1)S(1)}, bf16[4,64,128]{2,1,0:T(8,128)(2,1)S(1)}, u32[]{:S(2)}, u32[]{:S(2)}) collective-permute-start(bf16[4,64,128]{2,1,0:T(8,128)(2,1)S(1)} %multiply_convert_fusion.rest_0_), channel_id=1, source_target_pairs={{0,8},{2,10},{4,12},{6,14},{8,0},{10,2},{12,4},{14,6},{1,9},{3,11}... | collective-permute-start | bytes 196616 | tf_op jit(solution)/shard_map/ppermute | solution.py:794
  47.3 6.1 %collective-permute-start.13 = (bf16[4,64,128]{2,1,0:T(8,128)(2,1)S(1)}, bf16[4,64,128]{2,1,0:T(8,128)(2,1)S(1)}, u32[]{:S(2)}, u32[]{:S(2)}) collective-permute-start(bf16[4,64,128]{2,1,0:T(8,128)(2,1)S(1)} %multiply_convert_fusion.rest_0_), channel_id=1, source_target_pairs={{0,12},{2,14},{4,8},{6,10},{8,4},{10,6},{12,0},{14,2},{1,13},{3,15... | collective-permute-start | bytes 196616 | tf_op jit(solution)/shard_map/ppermute | solution.py:794
  49.8 4.3 %collective-permute-start.14 = (bf16[4,64,128]{2,1,0:T(8,128)(2,1)S(1)}, bf16[4,64,128]{2,1,0:T(8,128)(2,1)S(1)}, u32[]{:S(2)}, u32[]{:S(2)}) collective-permute-start(bf16[4,64,128]{2,1,0:T(8,128)(2,1)S(1)} %multiply_convert_fusion.rest_0_), channel_id=1, source_target_pairs={{0,4},{2,6},{4,0},{6,2},{8,12},{10,14},{12,8},{14,10},{1,5},{3,7},... | collective-permute-start | bytes 196616 | tf_op jit(solution)/shard_map/ppermute | solution.py:794
  54.1 6.4 %collective-permute-start.15 = (bf16[3,4,64,128]{3,2,1,0:T(8,128)(2,1)S(1)}, bf16[3,4,64,128]{3,2,1,0:T(8,128)(2,1)S(1)}, u32[]{:S(2)}, u32[]{:S(2)}) collective-permute-start(bf16[3,4,64,128]{3,2,1,0:T(8,128)(2,1)S(1)} %pad_maximum_fusion), channel_id=1, source_target_pairs={{0,2},{2,0},{4,6},{6,4},{8,10},{10,8},{12,14},{14,12},{1,3},{3,1},... | collective-permute-start | bytes 589832 | tf_op jit(solution)/shard_map/ppermute | solution.py:803
  55.8 4.7 %collective-permute-start.16 = (bf16[4,64,128]{2,1,0:T(8,128)(2,1)S(1)}, bf16[4,64,128]{2,1,0:T(8,128)(2,1)S(1)}, u32[]{:S(2)}, u32[]{:S(2)}) collective-permute-start(bf16[4,64,128]{2,1,0:T(8,128)(2,1)S(1)} %multiply_convert_fusion.rest_0_), channel_id=1, source_target_pairs={{0,2},{2,0},{4,6},{6,4},{8,10},{10,8},{12,14},{14,12},{1,3},{3,1},... | collective-permute-start | bytes 196616 | tf_op jit(solution)/shard_map/ppermute | solution.py:803
  56.2 25.4 %collective-permute-start.22 = (bf16[4,2,128,256]{3,2,1,0:T(8,128)(2,1)S(1)}, bf16[4,2,128,256]{3,2,1,0:T(8,128)(2,1)S(1)}, u32[]{:S(2)}, u32[]{:S(2)}) collective-permute-start(bf16[4,2,128,256]{3,2,1,0:T(8,128)(2,1)S(1)} %collective-permute-done.6.early_ref), channel_id=1, source_target_pairs={{0,16},{16,0},{1,17},{17,1},{2,18},{18,2},{3,19},{19,3},{4,20},{20... | collective-permute-start | bytes 1572872 | tf_op jit(solution)/shard_map/ppermute | solution.py:835
  65.4 12.6 %collective-permute-start.18 = (bf16[4,64,256]{2,1,0:T(8,128)(2,1)S(1)}, bf16[4,64,256]{2,1,0:T(8,128)(2,1)S(1)}, u32[]{:S(2)}, u32[]{:S(2)}) collective-permute-start(bf16[4,64,256]{2,1,0:T(8,128)(2,1)S(1)} %get-tuple-element.52), channel_id=1, source_target_pairs={{0,8},{2,10},{4,12},{6,14},{8,0},{10,2},{12,4},{14,6},{1,9},{3,11}... | collective-permute-start | bytes 393224 | tf_op jit(solution)/shard_map/ppermute | solution.py:794
  66.1 11.9 %collective-permute-start.19 = (bf16[4,64,256]{2,1,0:T(8,128)(2,1)S(1)}, bf16[4,64,256]{2,1,0:T(8,128)(2,1)S(1)}, u32[]{:S(2)}, u32[]{:S(2)}) collective-permute-start(bf16[4,64,256]{2,1,0:T(8,128)(2,1)S(1)} %get-tuple-element.53), channel_id=1, source_target_pairs={{0,12},{2,14},{4,8},{6,10},{8,4},{10,6},{12,0},{14,2},{1,13},{3,15... | collective-permute-start | bytes 393224 | tf_op jit(solution)/shard_map/ppermute | solution.py:794
  68.5 10.7 %collective-permute-start.20 = (bf16[4,64,256]{2,1,0:T(8,128)(2,1)S(1)}, bf16[4,64,256]{2,1,0:T(8,128)(2,1)S(1)}, u32[]{:S(2)}, u32[]{:S(2)}) collective-permute-start(bf16[4,64,256]{2,1,0:T(8,128)(2,1)S(1)} %get-tuple-element.54), channel_id=1, source_target_pairs={{0,4},{2,6},{4,0},{6,2},{8,12},{10,14},{12,8},{14,10},{1,5},{3,7},... | collective-permute-start | bytes 393224 | tf_op jit(solution)/shard_map/ppermute | solution.py:794
  79.2 5.0 %collective-permute-start.21 = (bf16[4,64,256]{2,1,0:T(8,128)(2,1)S(1)}, bf16[4,64,256]{2,1,0:T(8,128)(2,1)S(1)}, u32[]{:S(2)}, u32[]{:S(2)}) collective-permute-start(bf16[4,64,256]{2,1,0:T(8,128)(2,1)S(1)} %get-tuple-element.62), channel_id=1, source_target_pairs={{0,2},{2,0},{4,6},{6,4},{8,10},{10,8},{12,14},{14,12},{1,3},{3,1},... | collective-permute-start | bytes 393224 | tf_op jit(solution)/shard_map/ppermute | solution.py:803
  85.3 13.1 %collective-permute-start.23 = (bf16[272,256]{1,0:T(8,128)(2,1)S(1)}, bf16[272,256]{1,0:T(8,128)(2,1)S(1)}, u32[]{:S(2)}, u32[]{:S(2)}) collective-permute-start(bf16[272,256]{1,0:T(8,128)(2,1)S(1)} %get-tuple-element.59), channel_id=1, source_target_pairs={{0,8},{2,10},{4,12},{6,14},{8,0},{10,2},{12,4},{14,6},{1,9},{3,11}... | collective-permute-start | bytes 417800 | tf_op jit(solution)/shard_map/ppermute | solution.py:794
  87.9 10.6 %collective-permute-start.24 = (bf16[272,256]{1,0:T(8,128)(2,1)S(1)}, bf16[272,256]{1,0:T(8,128)(2,1)S(1)}, u32[]{:S(2)}, u32[]{:S(2)}) collective-permute-start(bf16[272,256]{1,0:T(8,128)(2,1)S(1)} %get-tuple-element.60), channel_id=1, source_target_pairs={{0,12},{2,14},{4,8},{6,10},{8,4},{10,6},{12,0},{14,2},{1,13},{3,15... | collective-permute-start | bytes 417800 | tf_op jit(solution)/shard_map/ppermute | solution.py:794
  90.2 8.6 %collective-permute-start.25 = (bf16[272,256]{1,0:T(8,128)(2,1)S(1)}, bf16[272,256]{1,0:T(8,128)(2,1)S(1)}, u32[]{:S(2)}, u32[]{:S(2)}) collective-permute-start(bf16[272,256]{1,0:T(8,128)(2,1)S(1)} %get-tuple-element.61), channel_id=1, source_target_pairs={{0,4},{2,6},{4,0},{6,2},{8,12},{10,14},{12,8},{14,10},{1,5},{3,7},... | collective-permute-start | bytes 417800 | tf_op jit(solution)/shard_map/ppermute | solution.py:794
  (5 other events, 49.9 us)
